TPU v7x, 32 devices: a whole 2x2x4 slice. The times are simulated.
32 devices in a mesh: frame: 8 (over z, y), band: 4 (over x, core).
Axes of the slice: x: 2, y: 2, z: 4, core: 2. Of those that a mesh axis runs over, the one named last changes fastest.
Arguments:
- latents: bfloat16 [8, 64, 32, 640], P('frame', 'band'), may hold values from -90 to 90, as said below
- conv_weight: bfloat16 [3, 3, 640, 640], replicated, may hold values from -0.078125 to 0.078125
- conv_bias: bfloat16 [640], replicated, may hold values from -3 to 3
- w_query: bfloat16 [640, 640], replicated, may hold values from -0.25 to 0.25
- w_keyval: bfloat16 [640, 1280], replicated, may hold values from -0.25 to 0.25
- w_out: bfloat16 [640, 640], replicated, may hold values from -0.25 to 0.25
Outputs:
- result: bfloat16 [8, 64, 32, 640], P('frame', 'band')
Inputs may be any that keep to these rules, and one draw needn't show every extreme that they name: `latents`: latent features; some frames may be far larger in magnitude than others.
All inputs are finite; a program needn't handle non-finite values.
Results may differ from a plain program's by a relative error of at most 0.023.
Values may be sent and summed in bfloat16 or wider, within the bound.
No kernel may reach another device: no remote copies, remote signals or barrier semaphores. Data moves between devices by JAX's collectives and lax.ppermute only.
A program may use at most 128 MiB of HBM per device.

v0:
```python
import jax
import jax.numpy as jnp
from jax import lax
from jax.sharding import PartitionSpec as P

HEAD_DIM = 64


key_block = 512


def with_halo(block, sides, width):
    for axis, dim in sides:
        count = lax.axis_size(axis)
        forward = [(i, i + 1) for i in range(count - 1)]
        backward = [(target, source) for source, target in forward]
        low = lax.ppermute(
            lax.slice_in_dim(block, block.shape[dim] - width, None, axis=dim), axis, forward
        )
        high = lax.ppermute(lax.slice_in_dim(block, 0, width, axis=dim), axis, backward)
        block = jnp.concatenate([low, block, high], axis=dim)
    return block


def spread(value, axis, source):
    kept = jnp.where(lax.axis_index(axis) == source, value, 0).astype(value.dtype)
    return lax.psum(kept, axis)


def absorb_block(running, queries, keyval, channels):
    row_best, weight_sum, weighted = running
    head_count = channels // HEAD_DIM
    query_count = queries.shape[0]
    key_count = keyval.shape[0]
    query_heads = queries.reshape(query_count, head_count, HEAD_DIM)
    key_heads = keyval[:, :channels].reshape(key_count, head_count, HEAD_DIM)
    value_heads = keyval[:, channels:].reshape(key_count, head_count, HEAD_DIM)
    scores = jnp.einsum(
        "qhd,khd->hqk", query_heads, key_heads, preferred_element_type=jnp.float32
    ) * HEAD_DIM ** (-0.5)
    new_best = jnp.maximum(row_best, jnp.max(scores, axis=2))
    fading = jnp.exp(row_best - new_best)
    probability = jnp.exp(scores - new_best[:, :, None])
    weight_sum = weight_sum * fading + jnp.sum(probability, axis=2)
    update = jnp.einsum(
        "hqk,khd->qhd",
        probability.astype(jnp.bfloat16),
        value_heads,
        preferred_element_type=jnp.float32,
    )
    weighted = weighted * jnp.transpose(fading)[:, :, None] + update
    return (new_best, weight_sum, weighted)


def fold_keys(running, queries, keyval, channels):
    key_count = keyval.shape[0]
    block_rows = min(key_count, key_block)

    def advance(position, partial_value):
        rows_now = lax.dynamic_slice_in_dim(keyval, position * block_rows, block_rows, 0)
        return absorb_block(partial_value, queries, rows_now, channels)

    return lax.fori_loop(0, key_count // block_rows, advance, running)


def per_device(latents, conv_weight, conv_bias, w_query, w_keyval, w_out):
    frames, row_count, col_count, channels = latents.shape
    tokens = frames * row_count * col_count
    activated = jax.nn.silu(latents.astype(jnp.float32)).astype(jnp.bfloat16)
    rimmed = with_halo(activated, (("band", 1),), 1)
    padded = jnp.pad(rimmed, ((0, 0), (0, 0), (1, 1), (0, 0)))
    summed = jnp.zeros((tokens, channels), jnp.float32)
    for row_shift in range(3):
        for col_shift in range(3):
            window = padded[
                :, row_shift : row_shift + row_count, col_shift : col_shift + col_count
            ].reshape(tokens, channels)
            summed = summed + jnp.dot(
                window, conv_weight[row_shift, col_shift], preferred_element_type=jnp.float32
            )
    hidden = (
        latents.reshape(tokens, channels).astype(jnp.float32)
        + summed
        + conv_bias.astype(jnp.float32)
    ).astype(jnp.bfloat16)
    queries = jnp.dot(hidden, w_query, preferred_element_type=jnp.float32).astype(jnp.bfloat16)
    payload = jnp.dot(hidden, w_keyval, preferred_element_type=jnp.float32).astype(jnp.bfloat16)
    head_count = channels // HEAD_DIM
    start_state = (
        jnp.full((head_count, tokens), -jnp.inf, jnp.float32),
        jnp.zeros((head_count, tokens), jnp.float32),
        jnp.zeros((tokens, head_count, HEAD_DIM), jnp.float32),
    )
    band_payload = spread(payload, "frame", 0)
    row_best, weight_sum, weighted = fold_keys(
        start_state, queries, lax.all_gather(band_payload, "band", axis=0, tiled=True), channels
    )
    mixed = (
        (weighted / jnp.transpose(weight_sum)[:, :, None])
        .reshape(tokens, channels)
        .astype(jnp.bfloat16)
    )
    output = hidden.astype(jnp.float32) + jnp.dot(mixed, w_out, preferred_element_type=jnp.float32)
    return output.astype(jnp.bfloat16).reshape(frames, row_count, col_count, channels)


def solution(mesh):
    return jax.shard_map(
        per_device,
        mesh=mesh,
        in_specs=(P("frame", "band", None, None), P(), P(), P(), P(), P()),
        out_specs=P("frame", "band", None, None),
        check_vma=False,
    )
```

profile of v0, /device:TPU:0, one launch (start us, length us, event | category | flops | bytes accessed | tf_op | source)
XLA Modules:
  0.0 245.5 jit_solution(11402060859385472288)
XLA Ops:
  6.5 1.6 multiply_convert_fusion
  8.2 2.4 collective-permute-start
  10.5 1.3 collective-permute-start.1
  11.9 3.9 %collective-permute-done.1 = bf16[1,1,32,640]{3,2,1,0:T(8,128)(2,1)S(1)} collective-permute-done((bf16[1,1,32,640]{3,2,1,0:T(8,128)(2,1)S(1)}, bf16[1,1,32,640]{3,2,1,0:T(8,128)(2,1)S(1)}, u32[]{:S(2)}, u32[]{:S(2)}) %collective-permute-start.1) | collective-permute-done | bytes 40992 | tf_op jit(solution)/shard_map/ppermute | solution.py:20
  15.7 0.3 fusion.27
  16.1 0.4 fusion.49
  16.5 2.6 %copy-done.2 = bf16[3,3,640,640]{3,2,1,0:T(8,128)(2,1)S(1)} copy-done((bf16[3,3,640,640]{3,2,1,0:T(8,128)(2,1)S(1)}, bf16[3,3,640,640]{3,2,1,0:T(8,128)(2,1)}, u32[]{:S(2)}) %copy-start.2) | copy-done | bytes 7372824
  19.2 0.7 fusion.37
  19.9 0.7 fusion.28
  20.8 0.8 convolution_add_fusion.7
  21.5 0.8 convolution_add_fusion.6
  22.3 0.8 convolution_add_fusion.5
  23.1 0.8 convolution_add_fusion.4
  23.8 0.8 convolution_add_fusion.3
  24.6 0.8 convolution_add_fusion.2
  25.4 0.3 copy-done.3
  25.7 0.8 fusion.21
  26.5 2.2 fusion.16
  29.0 85.9 %all-reduce.3.cloned.1.call-done = bf16[512,1280]{1,0:T(8,128)(2,1)} async-done(((bf16[512,1280]{1,0:T(8,128)(2,1)}), bf16[512,1280]{1,0:T(8,128)(2,1)}) %all-reduce.3.cloned.1.call-update) | async-done | bytes 1310736 | tf_op jit(solution)/shard_map/psum | solution.py:27
  115.0 1.9 convolution_convert_fusion.1
  116.9 1.1 copy.9
  118.0 38.2 %all-gather.2.cloned.1.call-done = bf16[2048,1280]{1,0:T(8,128)(2,1)} async-done(((bf16[512,1280]{1,0:T(8,128)(2,1)}), bf16[2048,1280]{1,0:T(8,128)(2,1)}) %all-gather.2.cloned.1.call-update) | async-done | bytes 5242896 | tf_op jit(solution)/shard_map/all_gather | solution.py:96
  156.2 79.0 %while.18 = (s32[]{:T(128)}, f32[10,512]{1,0:T(8,128)S(1)}, f32[10,512]{1,0:T(8,128)S(1)}, f32[512,10,64]{0,2,1:T(8,128)}, bf16[2048,1280]{1,0:T(8,128)(2,1)}, /...) while((s32[]{:T(128)}, f32[10,512]{1,0:T(8,128)S(1)}, ...), condition=%wide.region_4.5_spmd.clone, body=%wide.region_1.4_spmd.clone.sunk | while | flops 693073920 | bytes 83558608 | solution.py:63
  156.2 2.2 fusion.82
  158.5 1.3 copy.16
  159.8 6.6 %bitcast_reduce_fusion.2 = (f32[10,512]{1,0:T(8,128)S(1)}, f32[10,512,512]{2,1,0:T(8,128)}) fusion(bf16[512,10,64]{0,2,1:T(8,128)(2,1)S(1)} %bitcast.104, bf16[512,10,64]{0,2,1:T(8,128)(2,1)} %bitcast.106), kind=kOutput, calls=%fused_computation.1.clone.1 | convolution fusion | flops 340782080 | bytes 11816960 | tf_op jit(solution)/shard_map/while/body/eval_jaxpr/qhd,khd->hqk/dot_general | solution.py:38
  166.5 0.3 copy.17
  166.7 7.2 %fusion.86 = f32[512,10,64]{0,2,1:T(8,128)} fusion(bf16[512,10,64]{0,2,1:T(8,128)(2,1)S(1)} %bitcast.105, f32[10,512,512]{2,1,0:T(8,128)} %get-tuple-element.218, f32[10,512]{1,0:T(8,128)S(1)} %get-tuple-element.244, f32[512,10,64]{0,2,1:T(8,128)} %get-tuple-element.235, f32[512,10]{0,1:T(8,128)S(1)} %get-tuple-element.220, pred[]{:T(512)S(6)} %compare.44), kind=kOutput, calls=%fused_computation.9.clone.1 | convolution fusion | flops 344391680 | bytes 13803521 | tf_op jit(solution)/shard_map/while/body/eval_jaxpr/hqk,khd->qhd/dot_general | solution.py:45
  173.9 1.7 fusion.84
  175.7 2.3 fusion.82
  178.0 1.3 copy.16
  179.3 6.6 %bitcast_reduce_fusion.2 = (f32[10,512]{1,0:T(8,128)S(1)}, f32[10,512,512]{2,1,0:T(8,128)}) fusion(bf16[512,10,64]{0,2,1:T(8,128)(2,1)S(1)} %bitcast.104, bf16[512,10,64]{0,2,1:T(8,128)(2,1)} %bitcast.106), kind=kOutput, calls=%fused_computation.1.clone.1 | convolution fusion | flops 340782080 | bytes 11816960 | tf_op jit(solution)/shard_map/while/body/eval_jaxpr/qhd,khd->hqk/dot_general | solution.py:38
  186.0 0.3 copy.17
  186.3 7.5 %fusion.86 = f32[512,10,64]{0,2,1:T(8,128)} fusion(bf16[512,10,64]{0,2,1:T(8,128)(2,1)S(1)} %bitcast.105, f32[10,512,512]{2,1,0:T(8,128)} %get-tuple-element.218, f32[10,512]{1,0:T(8,128)S(1)} %get-tuple-element.244, f32[512,10,64]{0,2,1:T(8,128)} %get-tuple-element.235, f32[512,10]{0,1:T(8,128)S(1)} %get-tuple-element.220, pred[]{:T(512)S(6)} %compare.44), kind=kOutput, calls=%fused_computation.9.clone.1 | convolution fusion | flops 344391680 | bytes 13803521 | tf_op jit(solution)/shard_map/while/body/eval_jaxpr/hqk,khd->qhd/dot_general | solution.py:45
  193.8 1.7 fusion.84
  195.6 2.3 fusion.82
  197.8 1.3 copy.16
  199.2 6.6 %bitcast_reduce_fusion.2 = (f32[10,512]{1,0:T(8,128)S(1)}, f32[10,512,512]{2,1,0:T(8,128)}) fusion(bf16[512,10,64]{0,2,1:T(8,128)(2,1)S(1)} %bitcast.104, bf16[512,10,64]{0,2,1:T(8,128)(2,1)} %bitcast.106), kind=kOutput, calls=%fused_computation.1.clone.1 | convolution fusion | flops 340782080 | bytes 11816960 | tf_op jit(solution)/shard_map/while/body/eval_jaxpr/qhd,khd->hqk/dot_general | solution.py:38
  206.1 7.5 %fusion.86 = f32[512,10,64]{0,2,1:T(8,128)} fusion(bf16[512,10,64]{0,2,1:T(8,128)(2,1)S(1)} %bitcast.105, f32[10,512,512]{2,1,0:T(8,128)} %get-tuple-element.218, f32[10,512]{1,0:T(8,128)S(1)} %get-tuple-element.244, f32[512,10,64]{0,2,1:T(8,128)} %get-tuple-element.235, f32[512,10]{0,1:T(8,128)S(1)} %get-tuple-element.220, pred[]{:T(512)S(6)} %compare.44), kind=kOutput, calls=%fused_computation.9.clone.1 | convolution fusion | flops 344391680 | bytes 13803521 | tf_op jit(solution)/shard_map/while/body/eval_jaxpr/hqk,khd->qhd/dot_general | solution.py:45
  213.6 1.7 fusion.84
  215.4 2.3 fusion.82
  217.7 1.3 copy.16
  219.0 6.6 %bitcast_reduce_fusion.2 = (f32[10,512]{1,0:T(8,128)S(1)}, f32[10,512,512]{2,1,0:T(8,128)}) fusion(bf16[512,10,64]{0,2,1:T(8,128)(2,1)S(1)} %bitcast.104, bf16[512,10,64]{0,2,1:T(8,128)(2,1)} %bitcast.106), kind=kOutput, calls=%fused_computation.1.clone.1 | convolution fusion | flops 340782080 | bytes 11816960 | tf_op jit(solution)/shard_map/while/body/eval_jaxpr/qhd,khd->hqk/dot_general | solution.py:38
  225.7 0.3 copy.17
  225.9 7.5 %fusion.86 = f32[512,10,64]{0,2,1:T(8,128)} fusion(bf16[512,10,64]{0,2,1:T(8,128)(2,1)S(1)} %bitcast.105, f32[10,512,512]{2,1,0:T(8,128)} %get-tuple-element.218, f32[10,512]{1,0:T(8,128)S(1)} %get-tuple-element.244, f32[512,10,64]{0,2,1:T(8,128)} %get-tuple-element.235, f32[512,10]{0,1:T(8,128)S(1)} %get-tuple-element.220, pred[]{:T(512)S(6)} %compare.44), kind=kOutput, calls=%fused_computation.9.clone.1 | convolution fusion | flops 344391680 | bytes 13803521 | tf_op jit(solution)/shard_map/while/body/eval_jaxpr/hqk,khd->qhd/dot_general | solution.py:45
  233.5 1.7 fusion.84
  235.3 1.6 divide_convert_fusion
  237.0 1.6 fusion.22
  (44 shorter events, 1.0 us)
Async XLA Ops:
  6.5 20.0 %copy-start = (bf16[640,1280]{1,0:T(8,128)(2,1)S(1)}, bf16[640,1280]{1,0:T(8,128)(2,1)}, u32[]{:S(2)}) copy-start(bf16[640,1280]{1,0:T(8,128)(2,1)} %param.12) | copy-start | bytes 4915204
  6.5 5.3 %copy-start.6 = (bf16[640]{0:T(1024)(128)(2,1)S(1)}, bf16[640]{0:T(1024)(128)(2,1)}, u32[]{:S(2)}) copy-start(bf16[640]{0:T(1024)(128)(2,1)} %param.10) | copy-start | bytes 3844
  6.5 108.4 %all-reduce.3.cloned.1.call-start = ((), (), s32[]{:S(2)}) async-start(), calls=%async_computation | async-start | bytes 2621440 | tf_op jit(solution)/shard_map/psum | solution.py:27
  8.2 3.7 %collective-permute-start = (bf16[1,1,32,640]{3,2,1,0:T(8,128)(2,1)S(1)}, bf16[1,1,32,640]{3,2,1,0:T(8,128)(2,1)S(1)}, u32[]{:S(2)}, u32[]{:S(2)}) collective-permute-start(bf16[1,1,32,640]{3,2,1,0:T(8,128)(2,1)S(1)} %get-tuple-element.170), channel_id=1, source_target_pairs={{0,1},{1,2},{2,3},{4,5},{5,6},{6,7},{8,9},{9,10},{10,11},{12,13},{... | collective-permute-start | bytes 122888 | tf_op jit(solution)/shard_map/ppermute | solution.py:17
  10.5 5.2 %collective-permute-start.1 = (bf16[1,1,32,640]{3,2,1,0:T(8,128)(2,1)S(1)}, bf16[1,1,32,640]{3,2,1,0:T(8,128)(2,1)S(1)}, u32[]{:S(2)}, u32[]{:S(2)}) collective-permute-start(bf16[1,1,32,640]{3,2,1,0:T(8,128)(2,1)S(1)} %get-tuple-element.171), channel_id=1, source_target_pairs={{1,0},{2,1},{3,2},{5,4},{6,5},{7,6},{9,8},{10,9},{11,10},{13,12},{... | collective-permute-start | bytes 122888 | tf_op jit(solution)/shard_map/ppermute | solution.py:20
  16.1 3.1 %copy-start.2 = (bf16[3,3,640,640]{3,2,1,0:T(8,128)(2,1)S(1)}, bf16[3,3,640,640]{3,2,1,0:T(8,128)(2,1)}, u32[]{:S(2)}) copy-start(bf16[3,3,640,640]{3,2,1,0:T(8,128)(2,1)} %param.9) | copy-start | bytes 22118404
  24.6 1.1 copy-start.3
  26.5 88.5 %copy-start.4 = (bf16[512,640]{1,0:T(8,128)(2,1)}, bf16[512,640]{1,0:T(8,128)(2,1)S(1)}, u32[]{:S(2)}) copy-start(bf16[512,640]{1,0:T(8,128)(2,1)S(1)} %fusion.21) | copy-start | bytes 1966084
  28.8 127.4 %all-gather.2.cloned.1.call-start = ((), (), s32[]{:S(2)}) async-start(), calls=%async_computation.1 | async-start | bytes 6553600 | tf_op jit(solution)/shard_map/all_gather | solution.py:96
  166.7 7.2 %copy-start.1 = (f32[10,512,512]{2,1,0:T(8,128)S(1)}, f32[10,512,512]{2,1,0:T(8,128)}, u32[]{:S(2)}) copy-start(f32[10,512,512]{2,1,0:T(8,128)} %get-tuple-element.218) | copy-start | bytes 31457284 | tf_op jit(solution)/shard_map/while
  186.2 7.5 %copy-start.1 = (f32[10,512,512]{2,1,0:T(8,128)S(1)}, f32[10,512,512]{2,1,0:T(8,128)}, u32[]{:S(2)}) copy-start(f32[10,512,512]{2,1,0:T(8,128)} %get-tuple-element.218) | copy-start | bytes 31457284 | tf_op jit(solution)/shard_map/while
  206.1 7.5 %copy-start.1 = (f32[10,512,512]{2,1,0:T(8,128)S(1)}, f32[10,512,512]{2,1,0:T(8,128)}, u32[]{:S(2)}) copy-start(f32[10,512,512]{2,1,0:T(8,128)} %get-tuple-element.218) | copy-start | bytes 31457284 | tf_op jit(solution)/shard_map/while
  225.9 7.5 %copy-start.1 = (f32[10,512,512]{2,1,0:T(8,128)S(1)}, f32[10,512,512]{2,1,0:T(8,128)}, u32[]{:S(2)}) copy-start(f32[10,512,512]{2,1,0:T(8,128)} %get-tuple-element.218) | copy-start | bytes 31457284 | tf_op jit(solution)/shard_map/while
  235.3 1.6 copy-start.5
  235.3 1.7 copy-start.7
Sparse Core Ops, SparseCore 0:
  28.9 85.9 all-reduce.2
  116.6 39.6 all-gather.1
where the time goes:
time: 246 us; the launch traced here: 245 us
  waiting for transfers between devices  128 us (52%)
  matrix products  69 us (28%)
  local copies, waits for them, and re-layouts  20 us (8%)
  between operations  13.7 us (6%)
  other arithmetic  10.7 us (4%)
  starting transfers between devices  3.88 us (2%)
    psum x1, waiting for transfers between devices, spread(): return lax.psum(kept, axis)  85.9 us
    all_gather x1, waiting for transfers between devices, per_device(): lax.all_gather(band_payload, 'band', axis=0, tiled=True)  38.2 us
    dot_general x4, matrix products, absorb_block(): jnp.einsum('hqk,khd->qhd', probability.astype(jnp.bfloat16), value_heads,...  29.8 us
    dot_general x4, matrix products, absorb_block(): jnp.einsum('qhd,khd->hqk', query_heads, key_heads, preferred_element_type...  26.6 us
    slice x4, local copies, waits for them, and re-layouts, absorb_block(): value_heads = keyval[:, channels:].reshape(key_count, head_count, HEAD_DIM)  9 us
    reduce_sum x4, other arithmetic, absorb_block(): weight_sum = weight_sum * fading + jnp.sum(probability, axis=2)  6.94 us
    dot_general x9, matrix products, per_device(): jnp.dot(window, conv_weight[row_shift, col_shift], preferred_element_type...  6.83 us
    while x20, local copies, waits for them, and re-layouts  6.36 us
  transfers between devices with their start and end apart: 4, of which 3 were waited for; matrix products, arithmetic and copies ran while one was open for 1% of the time, Pallas kernels for 0%

commit v1 on v0

v1 whole, which is shorter than its diff:
```python
import functools

import jax
import jax.numpy as jnp
from jax import lax
from jax.experimental import pallas as pl
from jax.experimental.pallas import tpu as pltpu
from jax.sharding import PartitionSpec as P

HEAD_DIM = 64
PAIR = 2 * HEAD_DIM
VMEM_BYTES = 56 * 2**20


def conv_kernel(
    width, x_ref, low_ref, high_ref, weight_hbm, bias_ref, query_hbm, hidden_ref, queries_ref,
    weight, w_query, taps, sems,
):
    tokens, channels = x_ref.shape
    order = (1, 0, 2)
    copies = [
        pltpu.make_async_copy(weight_hbm.at[shift], weight.at[shift], sems.at[shift])
        for shift in range(3)
    ]
    for shift in order:
        copies[shift].start()
    query_copy = pltpu.make_async_copy(query_hbm, w_query, sems.at[3])
    query_copy.start()

    padded = tokens + 2 * width
    raw = jnp.concatenate([low_ref[...], x_ref[...], high_ref[...]], axis=0).astype(jnp.float32)
    active = raw * jax.nn.sigmoid(raw)
    column = lax.rem(lax.broadcasted_iota(jnp.int32, (padded, 1), 0), width)
    before = jnp.where(column == 0, 0.0, pltpu.roll(active, 1, 0))
    after = jnp.where(column == width - 1, 0.0, pltpu.roll(active, padded - 1, 0))
    taps[:, :channels] = before.astype(jnp.bfloat16)
    taps[:, channels : 2 * channels] = active.astype(jnp.bfloat16)
    taps[:, 2 * channels :] = after.astype(jnp.bfloat16)

    total = x_ref[...].astype(jnp.float32) + bias_ref[...].astype(jnp.float32)
    for shift in order:
        copies[shift].wait()
        total = total + jnp.dot(
            taps[shift * width : shift * width + tokens, :],
            weight[shift],
            preferred_element_type=jnp.float32,
        )
    hidden = total.astype(jnp.bfloat16)
    hidden_ref[...] = hidden
    query_copy.wait()
    queries = jnp.dot(hidden, w_query[...], preferred_element_type=jnp.float32)
    queries_ref[...] = queries.astype(jnp.bfloat16)


def convolve(x, low, high, conv_weight, conv_bias, w_query, width):
    tokens, channels = x.shape
    in_vmem = pl.BlockSpec(memory_space=pltpu.VMEM)
    in_place = pl.BlockSpec(memory_space=pl.ANY)
    token_array = jax.ShapeDtypeStruct((tokens, channels), jnp.bfloat16)
    return pl.pallas_call(
        functools.partial(conv_kernel, width),
        out_shape=(token_array, token_array),
        in_specs=[in_vmem, in_vmem, in_vmem, in_place, in_vmem, in_place],
        out_specs=(in_vmem, in_vmem),
        scratch_shapes=[
            pltpu.VMEM((3, 3 * channels, channels), jnp.bfloat16),
            pltpu.VMEM((channels, channels), jnp.bfloat16),
            pltpu.VMEM((tokens + 2 * width, 3 * channels), jnp.bfloat16),
            pltpu.SemaphoreType.DMA((4,)),
        ],
        compiler_params=pltpu.CompilerParams(vmem_limit_bytes=VMEM_BYTES),
        cost_estimate=pl.CostEstimate(
            flops=20 * tokens * channels * channels,
            bytes_accessed=20 * channels * channels + 6 * tokens * channels,
            transcendentals=0,
        ),
        name="convolve",
    )(
        x, low, high,
        conv_weight.reshape(3, 3 * channels, channels), conv_bias.reshape(1, channels), w_query,
    )


def attend_kernel(piece_count, *refs):
    queries_ref, hidden_ref, keyval_hbm, out_hbm = refs[:4]
    pieces = refs[4 : 4 + piece_count]
    result_ref, w_keyval, w_out, keys, values, mixed, sems = refs[4 + piece_count :]
    tokens, channels = queries_ref.shape
    keyval_copy = pltpu.make_async_copy(keyval_hbm, w_keyval, sems.at[0])
    out_copy = pltpu.make_async_copy(out_hbm, w_out, sems.at[1])
    keyval_copy.start()
    out_copy.start()
    keyval_copy.wait()
    start = 0
    for piece in pieces:
        count = piece.shape[0]
        keyval = jnp.dot(piece[...], w_keyval[...], preferred_element_type=jnp.float32)
        keyval = keyval.astype(jnp.bfloat16)
        keys[start : start + count, :] = keyval[:, :channels]
        values[start : start + count, :] = keyval[:, channels:]
        start += count
    lane = lax.broadcasted_iota(jnp.int32, (tokens, PAIR), 1)
    ones = jnp.ones((start, PAIR), jnp.bfloat16)
    for first in range(0, channels, PAIR):
        lanes = slice(first, first + PAIR)
        both = queries_ref[:, lanes] * HEAD_DIM ** (-0.5)
        nothing = jnp.zeros_like(both)
        split = jnp.concatenate(
            [jnp.where(lane < HEAD_DIM, both, nothing), jnp.where(lane < HEAD_DIM, nothing, both)], axis=0
        )
        scores = lax.dot_general(
            split, keys[:, lanes], (((1,), (1,)), ((), ())), preferred_element_type=jnp.float32
        )
        probability = jnp.exp(scores - jnp.max(scores, axis=1, keepdims=True)).astype(jnp.bfloat16)
        weighted = jnp.dot(
            probability,
            jnp.concatenate([values[:, lanes], ones], axis=1),
            preferred_element_type=jnp.float32,
        )
        heads = weighted[:, :PAIR] / weighted[:, PAIR:]
        mixed[:, lanes] = jnp.where(lane < HEAD_DIM, heads[:tokens], heads[tokens:]).astype(jnp.bfloat16)
    out_copy.wait()
    result = hidden_ref[...].astype(jnp.float32) + jnp.dot(
        mixed[...], w_out[...], preferred_element_type=jnp.float32
    )
    result_ref[...] = result.astype(jnp.bfloat16)


def attend(queries, hidden, w_keyval, w_out, pieces):
    tokens, channels = queries.shape
    key_count = sum(piece.shape[0] for piece in pieces)
    in_vmem = pl.BlockSpec(memory_space=pltpu.VMEM)
    in_place = pl.BlockSpec(memory_space=pl.ANY)
    return pl.pallas_call(
        functools.partial(attend_kernel, len(pieces)),
        out_shape=jax.ShapeDtypeStruct((tokens, channels), jnp.bfloat16),
        in_specs=[in_vmem, in_vmem, in_place, in_place] + [in_vmem] * len(pieces),
        out_specs=in_vmem,
        scratch_shapes=[
            pltpu.VMEM(w_keyval.shape, jnp.bfloat16),
            pltpu.VMEM(w_out.shape, jnp.bfloat16),
            pltpu.VMEM((key_count, channels), jnp.bfloat16),
            pltpu.VMEM((key_count, channels), jnp.bfloat16),
            pltpu.VMEM((tokens, channels), jnp.bfloat16),
            pltpu.SemaphoreType.DMA((2,)),
        ],
        compiler_params=pltpu.CompilerParams(vmem_limit_bytes=VMEM_BYTES),
        cost_estimate=pl.CostEstimate(
            flops=4 * tokens * key_count * channels,
            bytes_accessed=2 * channels * (key_count + 3 * tokens),
            transcendentals=tokens * key_count * channels // HEAD_DIM,
        ),
        name="attend",
    )(queries, hidden, w_keyval, w_out, *pieces)


def from_edges(block, axis):
    count = lax.axis_size(axis)
    forward = [(i, i + 1) for i in range(count - 1)]
    backward = [(target, source) for source, target in forward]
    low = lax.ppermute(block[:, -1], axis, forward)
    high = lax.ppermute(block[:, 0], axis, backward)
    return low, high


def swap(value, axis, distance):
    pairs = [(i, i ^ distance) for i in range(lax.axis_size(axis))]
    return lax.ppermute(value, axis, pairs)


def spread(hidden):
    frame_count, band_count = lax.axis_size("frame"), lax.axis_size("band")
    frame = lax.axis_index("frame")
    half = hidden.shape[0] // 2
    other = lax.ppermute(hidden[half:], "frame", [(0, 1)])
    mine = jnp.where(frame == 0, hidden[:half], other)
    reach = frame_count // 2
    while reach > 1:
        reach //= 2
        starts = range(0, frame_count, 4 * reach)
        pairs = [(i + y, i + 2 * reach + y) for i in starts for y in range(2)]
        arrived = lax.ppermute(mine, "frame", pairs)
        mine = jnp.where(lax.rem(frame // 2, 2 * reach) == reach, arrived, mine)
    beside = swap(mine, "frame", 1)
    pieces = [mine, beside]
    across = band_count
    while across > 2:
        across //= 2
        pieces = pieces + [swap(piece, "band", across) for piece in pieces]
    return pieces + [swap(piece, "band", 1) for piece in pieces]


def per_device(latents, conv_weight, conv_bias, w_query, w_keyval, w_out):
    frames, row_count, col_count, channels = latents.shape
    low, high = from_edges(latents, "band")
    hidden, queries = [], []
    for frame in range(frames):
        block = latents[frame].reshape(row_count * col_count, channels)
        parts = convolve(block, low[frame], high[frame], conv_weight, conv_bias, w_query, col_count)
        hidden.append(parts[0])
        queries.append(parts[1])
    pieces = spread(hidden[0])
    results = [
        attend(queries[frame], hidden[frame], w_keyval, w_out, pieces) for frame in range(frames)
    ]
    return jnp.stack(results).reshape(latents.shape)


def solution(mesh):
    return jax.shard_map(
        per_device,
        mesh=mesh,
        in_specs=(P("frame", "band", None, None), P(), P(), P(), P(), P()),
        out_specs=P("frame", "band", None, None),
        check_vma=False,
    )
```

time: 246 us -> 95 us (0.39)
  waiting for transfers between devices: 128 us -> 39 us
  matrix products: 69 us -> 0 us
  Pallas kernels: 0 us -> 34.5 us
  local copies, waits for them, and re-layouts: 20 us -> 4.39 us
  between operations: 13.7 us -> 0.4 us
  starting transfers between devices: 3.88 us -> 14.7 us
  other arithmetic: 10.7 us -> 1.09 us
    psum x1 -> x0, waiting for transfers between devices: 85.9 us -> none  [spread(): return lax.psum(kept, axis)]
    dot_general x20 -> x0, matrix products: 69 us -> none  [the longest x4 29.8 us: absorb_block(): jnp.einsum('hqk,khd->qhd', probability.astype(jnp.bfloat16), value_heads,...]
    all_gather x1 -> x0, waiting for transfers between devices: 38.2 us -> none  [per_device(): lax.all_gather(band_payload, 'band', axis=0, tiled=True)]
    ppermute x2 -> x12, waiting for transfers between devices: 3.88 us -> 39 us  [the longest x7 16.4 us: swap(): return lax.ppermute(value, axis, pairs)]
    pallas_call x0 -> x2, Pallas kernels: none -> 34.5 us  [the longest x1 22.9 us: attend(): pl.pallas_call(functools.partial(attend_kernel, len(pieces)), out_shape=j...]
    ppermute x2 -> x12, starting transfers between devices: 3.65 us -> 14.7 us  [the longest x1 4.89 us: spread(): other = lax.ppermute(hidden[half:], 'frame', [(0, 1)])]
    slice x6 -> x1, local copies, waits for them, and re-layouts: 9.44 us -> 1 us  [spread(): other = lax.ppermute(hidden[half:], 'frame', [(0, 1)])]
    reduce_sum x4 -> x0, other arithmetic: 6.94 us -> none  [absorb_block(): weight_sum = weight_sum * fading + jnp.sum(probability, axis=2)]
  transfers between devices with their start and end apart: 4 -> 12, of which waited for: 3 -> 7; matrix products, arithmetic and copies ran while one was open for 1% -> 1% of each run, Pallas kernels for 0% -> 0%
where the time goes in v1:
time: 95 us; the launch traced here: 94 us
  waiting for transfers between devices  39 us (41%)
  Pallas kernels  34.5 us (36%)
  starting transfers between devices  14.7 us (15%)
  local copies, waits for them, and re-layouts  4.39 us (5%)
  other arithmetic  1.09 us (1%)
    pallas_call x1, Pallas kernels, attend(): pl.pallas_call(functools.partial(attend_kernel, len(pieces)), out_shape=j...  22.9 us
    ppermute x7, waiting for transfers between devices, swap(): return lax.ppermute(value, axis, pairs)  16.4 us
    ppermute x2, waiting for transfers between devices, spread(): arrived = lax.ppermute(mine, 'frame', pairs)  14.6 us
    pallas_call x1, Pallas kernels, convolve(): pl.pallas_call(functools.partial(conv_kernel, width), out_shape=(token_ar...  11.6 us
    ppermute x1, waiting for transfers between devices, spread(): other = lax.ppermute(hidden[half:], 'frame', [(0, 1)])  7.92 us
    ppermute x1, starting transfers between devices, spread(): other = lax.ppermute(hidden[half:], 'frame', [(0, 1)])  4.89 us
    ppermute x1, starting transfers between devices, from_edges(): low = lax.ppermute(block[:, -1], axis, forward)  3.03 us
    ppermute x2, starting transfers between devices, spread(): arrived = lax.ppermute(mine, 'frame', pairs)  2.8 us
  transfers between devices with their start and end apart: 12, of which 7 were waited for; matrix products, arithmetic and copies ran while one was open for 1% of the time, Pallas kernels for 0%

profile of v1, /device:TPU:0, one launch (start us, length us, event | category | flops | bytes accessed | tf_op | source)
XLA Modules:
  0.0 94.0 jit_solution(2275848462303778859)
XLA Ops:
  0.0 0.8 slice_bitcast_fusion
  0.8 1.3 %collective-permute-start.1 = (bf16[1,32,640]{2,1,0:T(8,128)(2,1)S(1)}, bf16[1,32,640]{2,1,0:T(8,128)(2,1)S(1)}, u32[]{:S(2)}, u32[]{:S(2)}) collective-permute-start(bf16[1,32,640]{2,1,0:T(8,128)(2,1)S(1)} %get-tuple-element.9), channel_id=1, source_target_pairs={{1,0},{2,1},{3,2},{5,4},{6,5},{7,6},{9,8},{10,9},{11,10},{13,12},{... | collective-permute-start | bytes 122888 | tf_op jit(solution)/shard_map/ppermute | solution.py:162
  2.1 3.0 %collective-permute-start = (bf16[1,32,640]{2,1,0:T(8,128)(2,1)S(1)}, bf16[1,32,640]{2,1,0:T(8,128)(2,1)S(1)}, u32[]{:S(2)}, u32[]{:S(2)}) collective-permute-start(bf16[1,32,640]{2,1,0:T(8,128)(2,1)S(1)} %get-tuple-element.10), channel_id=1, source_target_pairs={{0,1},{1,2},{2,3},{4,5},{5,6},{6,7},{8,9},{9,10},{10,11},{12,13},{... | collective-permute-start | bytes 122888 | tf_op jit(solution)/shard_map/ppermute | solution.py:161
  5.1 1.3 %reshape.7.bias_ref = bf16[1,640]{1,0:T(2,128)(2,1)} reshape(bf16[640]{0:T(1024)(128)(2,1)} %param.8) | data formatting | bytes 2560 | tf_op jit(solution)/shard_map/reshape | solution.py:80
  6.4 0.0 collective-permute-done.1
  6.4 0.0 copy-start.8
  6.4 0.0 collective-permute-done
  6.4 0.0 copy-start.9
  6.4 0.6 copy-done.8
  7.0 0.0 copy-done.9
  7.0 11.6 %convolve.1 = (bf16[512,640]{1,0:T(8,128)(2,1)}, bf16[512,640]{1,0:T(8,128)(2,1)}) custom-call(bf16[512,640]{1,0:T(8,128)(2,1)} %bitcast.9, bf16[32,640]{1,0:T(8,128)(2,1)} %bitcast.12, bf16[32,640]{1,0:T(8,128)(2,1)} %bitcast.11, bf16[3,1920,640]{2,1,0:T(8,128)(2,1)} %bitcast.10, bf16[1,640]{1,0:T(2,128)(2,1)} %reshape.7.bias_ref, bf16[640,640]{1,0:T(8,128)(2,1)} %query_hbm.1), custom_call_target="tpu_custom_call" | custom-call | flops 4194304000 | bytes 10158080 | tf_op jit(solution)/shard_map/convolve/pallas_call | solution.py:60
  18.6 1.0 %slice.15 = bf16[256,640]{1,0:T(8,128)(2,1)S(1)} slice(bf16[512,640]{1,0:T(8,128)(2,1)} %get-tuple-element.8.refs_1_), slice={[256:512], [0:640]} | slice | bytes 655360 | tf_op jit(solution)/shard_map/slice | solution.py:175
  19.6 4.9 %collective-permute-start.2 = (bf16[256,640]{1,0:T(8,128)(2,1)S(1)}, bf16[256,640]{1,0:T(8,128)(2,1)S(1)}, u32[]{:S(2)}, u32[]{:S(2)}) collective-permute-start(bf16[256,640]{1,0:T(8,128)(2,1)S(1)} %slice.15), channel_id=1, source_target_pairs={{0,4},{1,5},{2,6},{3,7}} | collective-permute-start | bytes 983048 | tf_op jit(solution)/shard_map/ppermute | solution.py:175
  24.5 7.9 %collective-permute-done.2 = bf16[256,640]{1,0:T(8,128)(2,1)S(1)} collective-permute-done((bf16[256,640]{1,0:T(8,128)(2,1)S(1)}, bf16[256,640]{1,0:T(8,128)(2,1)S(1)}, u32[]{:S(2)}, u32[]{:S(2)}) %collective-permute-start.2) | collective-permute-done | bytes 327712 | tf_op jit(solution)/shard_map/ppermute | solution.py:175
  32.4 1.0 %slice_select_fusion = bf16[256,640]{1,0:T(8,128)(2,1)S(1)} fusion(bf16[256,640]{1,0:T(8,128)(2,1)S(1)} %collective-permute-done.2, bf16[512,640]{1,0:T(8,128)(2,1)} %get-tuple-element.8.refs_1_, pred[]{:T(512)S(6)} %eq.11), kind=kLoop, calls=%fused_computation | loop fusion | flops 163840 | bytes 983041 | tf_op jit(solution)/shard_map/jit(_where)/select_n | solution.py:176
  33.5 1.3 %collective-permute-start.3 = (bf16[256,640]{1,0:T(8,128)(2,1)S(1)}, bf16[256,640]{1,0:T(8,128)(2,1)S(1)}, u32[]{:S(2)}, u32[]{:S(2)}) collective-permute-start(bf16[256,640]{1,0:T(8,128)(2,1)S(1)} %slice_select_fusion), channel_id=1, source_target_pairs={{0,16},{4,20},{1,17},{5,21},{2,18},{6,22},{3,19},{7,23}} | collective-permute-start | bytes 983048 | tf_op jit(solution)/shard_map/ppermute | solution.py:182
  34.8 7.6 %collective-permute-done.3 = bf16[256,640]{1,0:T(8,128)(2,1)S(1)} collective-permute-done((bf16[256,640]{1,0:T(8,128)(2,1)S(1)}, bf16[256,640]{1,0:T(8,128)(2,1)S(1)}, u32[]{:S(2)}, u32[]{:S(2)}) %collective-permute-start.3) | collective-permute-done | bytes 327712 | tf_op jit(solution)/shard_map/ppermute | solution.py:182
  42.5 1.5 %collective-permute-start.4 = (bf16[256,640]{1,0:T(8,128)(2,1)S(1)}, bf16[256,640]{1,0:T(8,128)(2,1)S(1)}, u32[]{:S(2)}, u32[]{:S(2)}) collective-permute-start(bf16[256,640]{1,0:T(8,128)(2,1)S(1)} %broadcast_select_fusion), channel_id=1, source_target_pairs={{0,8},{4,12},{16,24},{20,28},{1,9},{5,13},{17,25},{21,29},{2,10},{... | collective-permute-start | bytes 983048 | tf_op jit(solution)/shard_map/ppermute | solution.py:182
  44.0 7.0 %collective-permute-done.4 = bf16[256,640]{1,0:T(8,128)(2,1)S(1)} collective-permute-done((bf16[256,640]{1,0:T(8,128)(2,1)S(1)}, bf16[256,640]{1,0:T(8,128)(2,1)S(1)}, u32[]{:S(2)}, u32[]{:S(2)}) %collective-permute-start.4) | collective-permute-done | bytes 327712 | tf_op jit(solution)/shard_map/ppermute | solution.py:182
  51.0 0.0 copy-start
  51.0 2.2 %collective-permute-start.5 = (bf16[256,640]{1,0:T(8,128)(2,1)S(1)}, bf16[256,640]{1,0:T(8,128)(2,1)S(1)}, u32[]{:S(2)}, u32[]{:S(2)}) collective-permute-start(bf16[256,640]{1,0:T(8,128)(2,1)S(1)} %broadcast_select_fusion.1.refs_4_), channel_id=1, source_target_pairs={{0,4},{4,0},{8,12},{12,8},{16,20},{20,16},{24,28},{28,24},{1,5},{5... | collective-permute-start | bytes 983048 | tf_op jit(solution)/shard_map/ppermute | solution.py:168
  53.2 0.0 collective-permute-start.6
  53.2 6.9 %collective-permute-done.5.refs_5_ = bf16[256,640]{1,0:T(8,128)(2,1)S(1)} collective-permute-done((bf16[256,640]{1,0:T(8,128)(2,1)S(1)}, bf16[256,640]{1,0:T(8,128)(2,1)S(1)}, u32[]{:S(2)}, u32[]{:S(2)}) %collective-permute-start.5) | collective-permute-done | bytes 327712 | tf_op jit(solution)/shard_map/ppermute | solution.py:168
  60.1 0.0 copy-start.1
  60.1 0.0 collective-permute-start.7
  60.1 0.0 collective-permute-start.8
  60.1 0.5 collective-permute-start.9
  60.6 1.4 %collective-permute-done.6.refs_6_ = bf16[256,640]{1,0:T(8,128)(2,1)S(1)} collective-permute-done((bf16[256,640]{1,0:T(8,128)(2,1)S(1)}, bf16[256,640]{1,0:T(8,128)(2,1)S(1)}, u32[]{:S(2)}, u32[]{:S(2)}) %collective-permute-start.6) | collective-permute-done | bytes 327712 | tf_op jit(solution)/shard_map/ppermute | solution.py:168
  62.0 0.0 copy-start.2
  62.0 0.0 collective-permute-start.10
  62.0 6.6 %collective-permute-done.7.refs_7_ = bf16[256,640]{1,0:T(8,128)(2,1)S(1)} collective-permute-done((bf16[256,640]{1,0:T(8,128)(2,1)S(1)}, bf16[256,640]{1,0:T(8,128)(2,1)S(1)}, u32[]{:S(2)}, u32[]{:S(2)}) %collective-permute-start.7) | collective-permute-done | bytes 327712 | tf_op jit(solution)/shard_map/ppermute | solution.py:168
  68.6 0.0 collective-permute-start.11
  68.6 0.0 collective-permute-done.8.refs_8_
  68.6 0.0 copy-start.4
  68.6 0.0 collective-permute-done.10.refs_10_
  68.6 0.0 copy-start.6
  68.6 0.0 collective-permute-done.9.refs_9_
  68.6 0.0 copy-start.5
  68.6 1.6 %collective-permute-done.11.refs_11_ = bf16[256,640]{1,0:T(8,128)(2,1)S(1)} collective-permute-done((bf16[256,640]{1,0:T(8,128)(2,1)S(1)}, bf16[256,640]{1,0:T(8,128)(2,1)S(1)}, u32[]{:S(2)}, u32[]{:S(2)}) %collective-permute-start.11) | collective-permute-done | bytes 327712 | tf_op jit(solution)/shard_map/ppermute | solution.py:168
  70.2 0.0 copy-done
  70.2 0.0 copy-done.1
  70.2 0.0 copy-done.2
  70.2 0.0 copy-done.3
  70.2 0.0 copy-done.4
  70.2 0.0 copy-done.6
  70.2 0.0 copy-done.5
  70.3 0.7 copy-done.7
  70.9 22.9 %attend.1 = bf16[512,640]{1,0:T(8,128)(2,1)} custom-call(bf16[512,640]{1,0:T(8,128)(2,1)} %get-tuple-element.7.refs_0_, bf16[512,640]{1,0:T(8,128)(2,1)} %get-tuple-element.8.refs_1_, bf16[640,1280]{1,0:T(8,128)(2,1)} %refs_2_.1, bf16[640,640]{1,0:T(8,128)(2,1)} %refs_3_.1, bf16[256,640]{1,0:T(8,128)(2,1)} %copy-done, bf16[256,640]{1,0:T(8,128)(2,1)} %copy-done.1, ...), custom_call_target="tpu_custom_call" | custom-call | flops 2684354560 | bytes 4587520 | tf_op jit(solution)/shard_map/attend/pallas_call | solution.py:134
  (4 shorter events, 0.1 us)
Async XLA Ops:
  0.8 5.6 %collective-permute-start.1 = (bf16[1,32,640]{2,1,0:T(8,128)(2,1)S(1)}, bf16[1,32,640]{2,1,0:T(8,128)(2,1)S(1)}, u32[]{:S(2)}, u32[]{:S(2)}) collective-permute-start(bf16[1,32,640]{2,1,0:T(8,128)(2,1)S(1)} %get-tuple-element.9), channel_id=1, source_target_pairs={{1,0},{2,1},{3,2},{5,4},{6,5},{7,6},{9,8},{10,9},{11,10},{13,12},{... | collective-permute-start | bytes 122888 | tf_op jit(solution)/shard_map/ppermute | solution.py:162
  2.1 4.3 %collective-permute-start = (bf16[1,32,640]{2,1,0:T(8,128)(2,1)S(1)}, bf16[1,32,640]{2,1,0:T(8,128)(2,1)S(1)}, u32[]{:S(2)}, u32[]{:S(2)}) collective-permute-start(bf16[1,32,640]{2,1,0:T(8,128)(2,1)S(1)} %get-tuple-element.10), channel_id=1, source_target_pairs={{0,1},{1,2},{2,3},{4,5},{5,6},{6,7},{8,9},{9,10},{10,11},{12,13},{... | collective-permute-start | bytes 122888 | tf_op jit(solution)/shard_map/ppermute | solution.py:161
  6.4 0.6 copy-start.8
  6.4 0.6 copy-start.9
  19.6 12.8 %collective-permute-start.2 = (bf16[256,640]{1,0:T(8,128)(2,1)S(1)}, bf16[256,640]{1,0:T(8,128)(2,1)S(1)}, u32[]{:S(2)}, u32[]{:S(2)}) collective-permute-start(bf16[256,640]{1,0:T(8,128)(2,1)S(1)} %slice.15), channel_id=1, source_target_pairs={{0,4},{1,5},{2,6},{3,7}} | collective-permute-start | bytes 983048 | tf_op jit(solution)/shard_map/ppermute | solution.py:175
  33.5 9.0 %collective-permute-start.3 = (bf16[256,640]{1,0:T(8,128)(2,1)S(1)}, bf16[256,640]{1,0:T(8,128)(2,1)S(1)}, u32[]{:S(2)}, u32[]{:S(2)}) collective-permute-start(bf16[256,640]{1,0:T(8,128)(2,1)S(1)} %slice_select_fusion), channel_id=1, source_target_pairs={{0,16},{4,20},{1,17},{5,21},{2,18},{6,22},{3,19},{7,23}} | collective-permute-start | bytes 983048 | tf_op jit(solution)/shard_map/ppermute | solution.py:182
  42.5 8.5 %collective-permute-start.4 = (bf16[256,640]{1,0:T(8,128)(2,1)S(1)}, bf16[256,640]{1,0:T(8,128)(2,1)S(1)}, u32[]{:S(2)}, u32[]{:S(2)}) collective-permute-start(bf16[256,640]{1,0:T(8,128)(2,1)S(1)} %broadcast_select_fusion), channel_id=1, source_target_pairs={{0,8},{4,12},{16,24},{20,28},{1,9},{5,13},{17,25},{21,29},{2,10},{... | collective-permute-start | bytes 983048 | tf_op jit(solution)/shard_map/ppermute | solution.py:182
  51.0 19.2 %copy-start = (bf16[256,640]{1,0:T(8,128)(2,1)}, bf16[256,640]{1,0:T(8,128)(2,1)S(1)}, u32[]{:S(2)}) copy-start(bf16[256,640]{1,0:T(8,128)(2,1)S(1)} %broadcast_select_fusion.1.refs_4_) | copy-start | bytes 983044
  51.0 9.1 %collective-permute-start.5 = (bf16[256,640]{1,0:T(8,128)(2,1)S(1)}, bf16[256,640]{1,0:T(8,128)(2,1)S(1)}, u32[]{:S(2)}, u32[]{:S(2)}) collective-permute-start(bf16[256,640]{1,0:T(8,128)(2,1)S(1)} %broadcast_select_fusion.1.refs_4_), channel_id=1, source_target_pairs={{0,4},{4,0},{8,12},{12,8},{16,20},{20,16},{24,28},{28,24},{1,5},{5... | collective-permute-start | bytes 983048 | tf_op jit(solution)/shard_map/ppermute | solution.py:168
  53.2 8.8 %collective-permute-start.6 = (bf16[256,640]{1,0:T(8,128)(2,1)S(1)}, bf16[256,640]{1,0:T(8,128)(2,1)S(1)}, u32[]{:S(2)}, u32[]{:S(2)}) collective-permute-start(bf16[256,640]{1,0:T(8,128)(2,1)S(1)} %broadcast_select_fusion.1.refs_4_), channel_id=1, source_target_pairs={{0,2},{1,3},{2,0},{3,1},{4,6},{5,7},{6,4},{7,5},{8,10},{9,11},{10,... | collective-permute-start | bytes 983048 | tf_op jit(solution)/shard_map/ppermute | solution.py:168
  60.1 10.1 %copy-start.1 = (bf16[256,640]{1,0:T(8,128)(2,1)}, bf16[256,640]{1,0:T(8,128)(2,1)S(1)}, u32[]{:S(2)}) copy-start(bf16[256,640]{1,0:T(8,128)(2,1)S(1)} %collective-permute-done.5.refs_5_) | copy-start | bytes 983044
  60.1 8.5 %collective-permute-start.7 = (bf16[256,640]{1,0:T(8,128)(2,1)S(1)}, bf16[256,640]{1,0:T(8,128)(2,1)S(1)}, u32[]{:S(2)}, u32[]{:S(2)}) collective-permute-start(bf16[256,640]{1,0:T(8,128)(2,1)S(1)} %collective-permute-done.5.refs_5_), channel_id=1, source_target_pairs={{0,2},{1,3},{2,0},{3,1},{4,6},{5,7},{6,4},{7,5},{8,10},{9,11},{10,... | collective-permute-start | bytes 983048 | tf_op jit(solution)/shard_map/ppermute | solution.py:168
  60.1 8.5 %collective-permute-start.8 = (bf16[256,640]{1,0:T(8,128)(2,1)S(1)}, bf16[256,640]{1,0:T(8,128)(2,1)S(1)}, u32[]{:S(2)}, u32[]{:S(2)}) collective-permute-start(bf16[256,640]{1,0:T(8,128)(2,1)S(1)} %broadcast_select_fusion.1.refs_4_), channel_id=1, source_target_pairs={{0,1},{1,0},{2,3},{3,2},{4,5},{5,4},{6,7},{7,6},{8,9},{9,8},{10,11... | collective-permute-start | bytes 983048 | tf_op jit(solution)/shard_map/ppermute | solution.py:168
  60.1 8.5 %collective-permute-start.9 = (bf16[256,640]{1,0:T(8,128)(2,1)S(1)}, bf16[256,640]{1,0:T(8,128)(2,1)S(1)}, u32[]{:S(2)}, u32[]{:S(2)}) collective-permute-start(bf16[256,640]{1,0:T(8,128)(2,1)S(1)} %collective-permute-done.5.refs_5_), channel_id=1, source_target_pairs={{0,1},{1,0},{2,3},{3,2},{4,5},{5,4},{6,7},{7,6},{8,9},{9,8},{10,11... | collective-permute-start | bytes 983048 | tf_op jit(solution)/shard_map/ppermute | solution.py:168
  62.0 8.2 %copy-start.2 = (bf16[256,640]{1,0:T(8,128)(2,1)}, bf16[256,640]{1,0:T(8,128)(2,1)S(1)}, u32[]{:S(2)}) copy-start(bf16[256,640]{1,0:T(8,128)(2,1)S(1)} %collective-permute-done.6.refs_6_) | copy-start | bytes 983044
  62.0 6.6 %collective-permute-start.10 = (bf16[256,640]{1,0:T(8,128)(2,1)S(1)}, bf16[256,640]{1,0:T(8,128)(2,1)S(1)}, u32[]{:S(2)}, u32[]{:S(2)}) collective-permute-start(bf16[256,640]{1,0:T(8,128)(2,1)S(1)} %collective-permute-done.6.refs_6_), channel_id=1, source_target_pairs={{0,1},{1,0},{2,3},{3,2},{4,5},{5,4},{6,7},{7,6},{8,9},{9,8},{10,11... | collective-permute-start | bytes 983048 | tf_op jit(solution)/shard_map/ppermute | solution.py:168
  68.6 1.6 %copy-start.3 = (bf16[256,640]{1,0:T(8,128)(2,1)}, bf16[256,640]{1,0:T(8,128)(2,1)S(1)}, u32[]{:S(2)}) copy-start(bf16[256,640]{1,0:T(8,128)(2,1)S(1)} %collective-permute-done.7.refs_7_) | copy-start | bytes 983044
  68.6 1.6 %collective-permute-start.11 = (bf16[256,640]{1,0:T(8,128)(2,1)S(1)}, bf16[256,640]{1,0:T(8,128)(2,1)S(1)}, u32[]{:S(2)}, u32[]{:S(2)}) collective-permute-start(bf16[256,640]{1,0:T(8,128)(2,1)S(1)} %collective-permute-done.7.refs_7_), channel_id=1, source_target_pairs={{0,1},{1,0},{2,3},{3,2},{4,5},{5,4},{6,7},{7,6},{8,9},{9,8},{10,11... | collective-permute-start | bytes 983048 | tf_op jit(solution)/shard_map/ppermute | solution.py:168
  68.6 1.6 %copy-start.4 = (bf16[256,640]{1,0:T(8,128)(2,1)}, bf16[256,640]{1,0:T(8,128)(2,1)S(1)}, u32[]{:S(2)}) copy-start(bf16[256,640]{1,0:T(8,128)(2,1)S(1)} %collective-permute-done.8.refs_8_) | copy-start | bytes 983044
  68.6 1.6 %copy-start.6 = (bf16[256,640]{1,0:T(8,128)(2,1)}, bf16[256,640]{1,0:T(8,128)(2,1)S(1)}, u32[]{:S(2)}) copy-start(bf16[256,640]{1,0:T(8,128)(2,1)S(1)} %collective-permute-done.10.refs_10_) | copy-start | bytes 983044
  68.6 1.6 %copy-start.5 = (bf16[256,640]{1,0:T(8,128)(2,1)}, bf16[256,640]{1,0:T(8,128)(2,1)S(1)}, u32[]{:S(2)}) copy-start(bf16[256,640]{1,0:T(8,128)(2,1)S(1)} %collective-permute-done.9.refs_9_) | copy-start | bytes 983044
  70.2 0.7 copy-start.7

commit v2 on v1

v2 whole, which is shorter than its diff:
```python
import functools

import jax
import jax.numpy as jnp
from jax import lax
from jax.experimental import pallas as pl
from jax.experimental.pallas import tpu as pltpu
from jax.sharding import PartitionSpec as P

HEAD_DIM = 64
PAIR = 2 * HEAD_DIM
VMEM_BYTES = 40 * 2**20
IN_VMEM = pl.BlockSpec(memory_space=pltpu.VMEM)
IN_PLACE = pl.BlockSpec(memory_space=pl.ANY)


def conv_kernel(width, spans, splits, x_hbm, low_ref, high_ref, weight_hbm, bias_ref, *refs):
    outs = refs[: len(splits)]
    rows, weight, taps, sems = refs[len(splits) :]
    tokens, channels = x_hbm.shape
    last_row = tokens // width
    order = (1, 0, 2)

    loads, edges, starts, place = [], [], [], 0
    for first, count in spans:
        begin, end = max(first - 1, 0), min(first + count + 1, last_row)
        starts.append(place)
        if first == 0:
            edges.append((low_ref, place))
            place += 1
        loads.append((begin, end - begin, place))
        place += end - begin
        if first + count == last_row:
            edges.append((high_ref, place))
            place += 1
    copies = [
        pltpu.make_async_copy(
            x_hbm.at[pl.ds(begin * width, count * width)],
            rows.at[pl.ds(spot * width, count * width)],
            sems.at[3 + i],
        )
        for i, (begin, count, spot) in enumerate(loads)
    ]
    for copy in copies:
        copy.start()
    weight_copies = [
        pltpu.make_async_copy(weight_hbm.at[shift], weight.at[shift], sems.at[shift])
        for shift in range(3)
    ]
    for shift in order:
        weight_copies[shift].start()
    for edge_ref, spot in edges:
        rows[spot * width : (spot + 1) * width, :] = edge_ref[...]
    for copy in copies:
        copy.wait()

    padded = place * width
    raw = rows[...].astype(jnp.float32)
    active = raw * jax.nn.sigmoid(raw)
    column = lax.rem(lax.broadcasted_iota(jnp.int32, (padded, 1), 0), width)
    before = jnp.where(column == 0, 0.0, pltpu.roll(active, 1, 0))
    after = jnp.where(column == width - 1, 0.0, pltpu.roll(active, padded - 1, 0))
    taps[:, :channels] = before.astype(jnp.bfloat16)
    taps[:, channels : 2 * channels] = active.astype(jnp.bfloat16)
    taps[:, 2 * channels :] = after.astype(jnp.bfloat16)

    def rows_at(ref, shift):
        parts = [
            ref[(start + shift) * width : (start + shift + count) * width, :]
            for start, (_, count) in zip(starts, spans)
        ]
        return parts[0] if len(parts) == 1 else jnp.concatenate(parts, axis=0)

    total = rows_at(rows, 1).astype(jnp.float32) + bias_ref[...].astype(jnp.float32)[None, :]
    for shift in order:
        weight_copies[shift].wait()
        total = total + jnp.dot(
            rows_at(taps, shift), weight[shift], preferred_element_type=jnp.float32
        )
    place = 0
    for out, size in zip(outs, splits):
        out[...] = total[place : place + size].astype(jnp.bfloat16)
        place += size


def convolve(x, low, high, conv_weight, conv_bias, width, spans, splits, name):
    tokens, channels = x.shape
    made = sum(splits)
    gathered = made + 2 * width * len(spans)
    return pl.pallas_call(
        functools.partial(conv_kernel, width, spans, splits),
        out_shape=tuple(jax.ShapeDtypeStruct((size, channels), jnp.bfloat16) for size in splits),
        in_specs=[IN_PLACE, IN_VMEM, IN_VMEM, IN_PLACE, IN_VMEM],
        out_specs=(IN_VMEM,) * len(splits),
        scratch_shapes=[
            pltpu.VMEM((gathered, channels), jnp.bfloat16),
            pltpu.VMEM((3, 3 * channels, channels), jnp.bfloat16),
            pltpu.VMEM((gathered, 3 * channels), jnp.bfloat16),
            pltpu.SemaphoreType.DMA((3 + len(spans),)),
        ],
        compiler_params=pltpu.CompilerParams(vmem_limit_bytes=VMEM_BYTES),
        cost_estimate=pl.CostEstimate(
            flops=18 * made * channels * channels,
            bytes_accessed=18 * channels * channels + 4 * made * channels,
            transcendentals=0,
        ),
        name=name,
    )(x, low, high, conv_weight, conv_bias)


def query_kernel(layout, *refs):
    count = len(layout)
    pieces, (w_query, hidden_ref, queries_ref) = refs[:count], refs[count:]
    for piece, spots in zip(pieces, layout):
        taken = 0
        for start, size in spots:
            hidden_ref[start : start + size, :] = piece[taken : taken + size, :]
            taken += size
    queries = jnp.dot(hidden_ref[...], w_query[...], preferred_element_type=jnp.float32)
    queries_ref[...] = queries.astype(jnp.bfloat16)


def ask(pieces, layout, w_query):
    tokens, channels = sum(piece.shape[0] for piece in pieces), w_query.shape[0]
    whole = jax.ShapeDtypeStruct((tokens, channels), jnp.bfloat16)
    return pl.pallas_call(
        functools.partial(query_kernel, layout),
        out_shape=(whole, whole),
        in_specs=[IN_VMEM] * (len(pieces) + 1),
        out_specs=(IN_VMEM, IN_VMEM),
        compiler_params=pltpu.CompilerParams(vmem_limit_bytes=16 * 2**20),
        cost_estimate=pl.CostEstimate(
            flops=2 * tokens * channels * channels,
            bytes_accessed=2 * channels * channels + 6 * tokens * channels,
            transcendentals=0,
        ),
        name="ask",
    )(*pieces, w_query)


def attend_kernel(piece_count, first, last, queries_ref, keyval_hbm, *refs):
    refs = list(refs)
    pieces = [refs.pop(0) for _ in range(piece_count)]
    old = None if first else [refs.pop(0) for _ in range(3)]
    ending = [refs.pop(0) for _ in range(2)] if last else None
    new = [refs.pop(0) for _ in range(1 if last else 3)]
    w_keyval, w_out, keys, values, mixed, sems = refs
    tokens, channels = queries_ref.shape
    keyval_copy = pltpu.make_async_copy(keyval_hbm, w_keyval, sems.at[0])
    keyval_copy.start()
    if last:
        out_copy = pltpu.make_async_copy(ending[1], w_out, sems.at[1])
        out_copy.start()
    keyval_copy.wait()
    key_count = 0
    for piece in pieces:
        spot = slice(key_count, key_count + piece.shape[0])
        keyval = jnp.dot(piece[...], w_keyval[...], preferred_element_type=jnp.float32)
        keyval = keyval.astype(jnp.bfloat16)
        keys[spot, :] = keyval[:, :channels]
        values[spot, :] = keyval[:, channels:]
        key_count = spot.stop
    is_low = lax.broadcasted_iota(jnp.int32, (tokens, PAIR), 1) < HEAD_DIM
    ones = jnp.ones((key_count, PAIR), jnp.bfloat16)
    for start in range(0, channels, PAIR):
        lanes = slice(start, start + PAIR)
        both = queries_ref[:, lanes] * HEAD_DIM ** (-0.5)
        nothing = jnp.zeros_like(both)
        split = jnp.concatenate(
            [jnp.where(is_low, both, nothing), jnp.where(is_low, nothing, both)], axis=0
        )
        scores = lax.dot_general(
            split, keys[:, lanes], (((1,), (1,)), ((), ())), preferred_element_type=jnp.float32
        )
        best = jnp.max(scores, axis=1, keepdims=True)
        best_pair = jnp.where(is_low, best[:tokens], best[tokens:])
        if not first:
            best_pair = jnp.maximum(best_pair, old[2][:, lanes])
            best = jnp.concatenate(
                [best_pair[:, :1], best_pair[:, HEAD_DIM : HEAD_DIM + 1]], axis=0
            )
        probability = jnp.exp(scores - best).astype(jnp.bfloat16)
        product = jnp.dot(
            probability,
            jnp.concatenate([values[:, lanes], ones], axis=1),
            preferred_element_type=jnp.float32,
        )
        weighted = jnp.where(is_low, product[:tokens, :PAIR], product[tokens:, :PAIR])
        total = jnp.where(is_low, product[:tokens, PAIR:], product[tokens:, PAIR:])
        if not first:
            fading = jnp.exp(old[2][:, lanes] - best_pair)
            weighted = weighted + old[0][:, lanes] * fading
            total = total + old[1][:, lanes] * fading
        if last:
            mixed[:, lanes] = (weighted / total).astype(jnp.bfloat16)
        else:
            new[0][:, lanes] = weighted
            new[1][:, lanes] = total
            new[2][:, lanes] = best_pair
    if last:
        out_copy.wait()
        result = ending[0][...].astype(jnp.float32) + jnp.dot(
            mixed[...], w_out[...], preferred_element_type=jnp.float32
        )
        new[0][...] = result.astype(jnp.bfloat16)


def attend(queries, w_keyval, pieces, state, ending, name):
    tokens, channels = queries.shape
    key_count = sum(piece.shape[0] for piece in pieces)
    first, last = state is None, ending is not None
    part = jax.ShapeDtypeStruct((tokens, channels), jnp.float32)
    whole = jax.ShapeDtypeStruct((tokens, channels), jnp.bfloat16)
    args = [queries, w_keyval, *pieces, *(() if first else state), *(ending if last else ())]
    in_specs = [IN_VMEM] * len(args)
    in_specs[1] = IN_PLACE
    if last:
        in_specs[-1] = IN_PLACE
    return pl.pallas_call(
        functools.partial(attend_kernel, len(pieces), first, last),
        out_shape=whole if last else (part,) * 3,
        in_specs=in_specs,
        out_specs=IN_VMEM if last else (IN_VMEM,) * 3,
        scratch_shapes=[
            pltpu.VMEM(w_keyval.shape, jnp.bfloat16),
            pltpu.VMEM((channels, channels), jnp.bfloat16),
            pltpu.VMEM((key_count, channels), jnp.bfloat16),
            pltpu.VMEM((key_count, channels), jnp.bfloat16),
            pltpu.VMEM((tokens, channels), jnp.bfloat16),
            pltpu.SemaphoreType.DMA((2,)),
        ],
        compiler_params=pltpu.CompilerParams(vmem_limit_bytes=VMEM_BYTES),
        cost_estimate=pl.CostEstimate(
            flops=4 * tokens * key_count * channels,
            bytes_accessed=2 * channels * (key_count + 3 * tokens),
            transcendentals=tokens * key_count * channels // HEAD_DIM,
        ),
        name=name,
    )(*args)


def from_edges(block, axis):
    count = lax.axis_size(axis)
    forward = [(i, i + 1) for i in range(count - 1)]
    backward = [(target, source) for source, target in forward]
    low = lax.ppermute(block[:, -1], axis, forward)
    high = lax.ppermute(block[:, 0], axis, backward)
    return low, high


def cast(even, odd):
    frame_count = lax.axis_size("frame")
    frame = lax.axis_index("frame")
    held = jnp.zeros_like(even)
    reach = frame_count // 2
    while reach > 1:
        arrived = [
            lax.ppermute(even, "frame", [(0, reach)]),
            lax.ppermute(odd, "frame", [(0, reach + 1)]),
        ]
        relays = [
            (i + y, i + reach + y) for i in range(2 * reach, frame_count, 2 * reach) for y in range(2)
        ]
        if relays:
            arrived.append(lax.ppermute(held, "frame", relays))
            arrived.append(held)
        held = functools.reduce(jnp.add, arrived)
        reach //= 2
    held = held + lax.ppermute(odd, "frame", [(0, 1)])
    return jnp.where(frame == 0, even, held)


def swap(value, axes, distances):
    sizes = [lax.axis_size(axis) for axis in axes]
    pairs = []
    for i in range(sizes[0]):
        for j in range(sizes[1]):
            other = (i ^ distances[0]) * sizes[1] + (j ^ distances[1])
            pairs.append((i * sizes[1] + j, other))
    return lax.ppermute(value, axes, pairs)


def per_device(latents, conv_weight, conv_bias, w_query, w_keyval, w_out):
    frames, row_count, width, channels = latents.shape
    tokens = row_count * width
    half, quarter = row_count // 2, tokens // 4
    taps_weight = conv_weight.reshape(3, 3 * channels, channels)
    no_edge = jnp.zeros((width, channels), latents.dtype)
    low, high = from_edges(latents, "band")
    inner = ((1, half),)
    outer = ((0, 1), (half + 1, row_count - half - 1))
    seam = (half + 1) * width
    layout = (
        ((width, quarter),),
        ((width + quarter, quarter),),
        ((0, width), (seam, quarter - width)),
        ((seam + quarter - width, quarter),),
    )
    parts = []
    for frame in range(frames):
        block = latents[frame].reshape(tokens, channels)
        parts.append(
            convolve(
                block, no_edge, no_edge, taps_weight, conv_bias, width, inner, (quarter,) * 2, "inner"
            )
            + convolve(
                block, low[frame], high[frame], taps_weight, conv_bias, width, outer, (quarter,) * 2,
                "outer",
            )
        )
    asked = [ask(part, layout, w_query) for part in parts]

    axes = ("frame", "band")
    chunks = []
    for even, odd in ((parts[0][0], parts[0][1]), (parts[0][2], parts[0][3])):
        mine = cast(even, odd)
        chunks.append(
            [mine, swap(mine, axes, (1, 0)), swap(mine, axes, (0, 2)), swap(mine, axes, (1, 2))]
        )
    chunks = [[(piece, swap(piece, axes, (0, 1))) for piece in chunk] for chunk in chunks]
    groups = [
        [*chunks[0][0], *chunks[0][1], *chunks[0][2]],
        [*chunks[0][3], *chunks[1][0]],
        [*chunks[1][1], *chunks[1][2], *chunks[1][3]],
    ]
    results = []
    for hidden, queries in asked:
        state = None
        for i, group in enumerate(groups):
            ending = (hidden, w_out) if i == len(groups) - 1 else None
            state = attend(queries, w_keyval, group, state, ending, f"attend{i}")
        results.append(state)
    return jnp.stack(results).reshape(latents.shape)


def solution(mesh):
    return jax.shard_map(
        per_device,
        mesh=mesh,
        in_specs=(P("frame", "band", None, None), P(), P(), P(), P(), P()),
        out_specs=P("frame", "band", None, None),
        check_vma=False,
    )
```

time: 95 us -> 89.6 us (0.943)
  waiting for transfers between devices: 39 us -> 14.2 us
  starting transfers between devices: 14.7 us -> 35.2 us
  local copies, waits for them, and re-layouts: 4.39 us -> 5.69 us
  Pallas kernels: 34.5 us -> 33.2 us
    ppermute x10 -> x26, waiting for transfers between devices: 39 us -> 14.2 us  [the longest x14 8.03 us: swap(): return lax.ppermute(value, axes, pairs)]
    ppermute x10 -> x26, starting transfers between devices: 10.4 us -> 31.6 us  [the longest x14 12.7 us: swap(): return lax.ppermute(value, axes, pairs)]
    unnamed x20 -> x14, local copies, waits for them, and re-layouts: 1.32 us -> 4.88 us
    pallas_call x2 -> x6, Pallas kernels: 34.5 us -> 33.2 us  [the longest x3 23.5 us: attend(): pl.pallas_call(functools.partial(attend_kernel, len(pieces), first, last)...]
    reshape x1 -> x0, local copies, waits for them, and re-layouts: 1.26 us -> none  [convolve(): conv_bias.reshape(1, channels)]
    slice x1 -> x0, local copies, waits for them, and re-layouts: 1 us -> none  [spread(): other = lax.ppermute(hidden[half:], 'frame', [(0, 1)])]
    select_n x3 -> x2, other arithmetic: 1.09 us -> 0.1 us  [cast(): return jnp.where(frame == 0, even, held)]
  transfers between devices with their start and end apart: 12 -> 28, of which waited for: 7 -> 7; matrix products, arithmetic and copies ran while one was open for 1% -> 0% of each run, Pallas kernels for 0% -> 26%
where the time goes in v2:
time: 89.6 us; the launch traced here: 89.1 us
  starting transfers between devices  35.2 us (39%)
  Pallas kernels  33.2 us (37%)
  waiting for transfers between devices  14.2 us (16%)
  local copies, waits for them, and re-layouts  5.69 us (6%)
    pallas_call x3, Pallas kernels, attend(): pl.pallas_call(functools.partial(attend_kernel, len(pieces), first, last)...  23.5 us
    ppermute x14, starting transfers between devices, swap(): return lax.ppermute(value, axes, pairs)  12.7 us
    ppermute x4, starting transfers between devices, cast(): lax.ppermute(even, 'frame', [(0, reach)])  9.22 us
    pallas_call x2, Pallas kernels, convolve(): pl.pallas_call(functools.partial(conv_kernel, width, spans, splits), out_...  8.98 us
    ppermute x14, waiting for transfers between devices, swap(): return lax.ppermute(value, axes, pairs)  8.03 us
    ppermute x4, starting transfers between devices, cast(): lax.ppermute(odd, 'frame', [(0, reach + 1)])  5.51 us
    unnamed x14, local copies, waits for them, and re-layouts  4.88 us
    ppermute x4, waiting for transfers between devices, cast(): lax.ppermute(even, 'frame', [(0, reach)])  3.35 us
  transfers between devices with their start and end apart: 28, of which 7 were waited for; matrix products, arithmetic and copies ran while one was open for 0% of the time, Pallas kernels for 26%

profile of v2, /device:TPU:0, one launch (start us, length us, event | category | flops | bytes accessed | tf_op | source)
XLA Modules:
  0.0 89.1 jit_solution(13784161990147766036)
XLA Ops:
  0.0 0.8 slice_bitcast_fusion
  0.8 2.4 %collective-permute-start = (bf16[1,32,640]{2,1,0:T(8,128)(2,1)S(1)}, bf16[1,32,640]{2,1,0:T(8,128)(2,1)S(1)}, u32[]{:S(2)}, u32[]{:S(2)}) collective-permute-start(bf16[1,32,640]{2,1,0:T(8,128)(2,1)S(1)} %get-tuple-element.30), channel_id=1, source_target_pairs={{0,1},{1,2},{2,3},{4,5},{5,6},{6,7},{8,9},{9,10},{10,11},{12,13},{... | collective-permute-start | bytes 122888 | tf_op jit(solution)/shard_map/ppermute | solution.py:246
  3.2 1.3 %collective-permute-start.1 = (bf16[1,32,640]{2,1,0:T(8,128)(2,1)S(1)}, bf16[1,32,640]{2,1,0:T(8,128)(2,1)S(1)}, u32[]{:S(2)}, u32[]{:S(2)}) collective-permute-start(bf16[1,32,640]{2,1,0:T(8,128)(2,1)S(1)} %get-tuple-element.29), channel_id=1, source_target_pairs={{1,0},{2,1},{3,2},{5,4},{6,5},{7,6},{9,8},{10,9},{11,10},{13,12},{... | collective-permute-start | bytes 122888 | tf_op jit(solution)/shard_map/ppermute | solution.py:247
  4.5 0.0 copy-start
  4.5 3.1 %copy-done = bf16[3,3,640,640]{3,2,1,0:T(8,128)(2,1)S(1)} copy-done((bf16[3,3,640,640]{3,2,1,0:T(8,128)(2,1)S(1)}, bf16[3,3,640,640]{3,2,1,0:T(8,128)(2,1)}, u32[]{:S(2)}) %copy-start) | copy-done | bytes 7372824
  7.6 1.1 %copy-done.3 = bf16[1,16,32,640]{3,2,1,0:T(8,128)(2,1)S(1)} copy-done((bf16[1,16,32,640]{3,2,1,0:T(8,128)(2,1)S(1)}, bf16[1,16,32,640]{3,2,1,0:T(8,128)(2,1)}, u32[]{:S(2)}) %copy-start.3) | copy-done | bytes 655384
  8.7 0.7 copy-done.5
  9.3 4.4 %inner.1 = (bf16[128,640]{1,0:T(8,128)(2,1)S(1)}, bf16[128,640]{1,0:T(8,128)(2,1)S(1)}) custom-call(bf16[512,640]{1,0:T(8,128)(2,1)S(1)} %bitcast.11, bf16[32,640]{1,0:T(8,128)(2,1)S(1)} %broadcast_in_dim.3.low_ref.high_ref, bf16[32,640]{1,0:T(8,128)(2,1)S(1)} %broadcast_in_dim.3.low_ref.high_ref, bf16[3,1920,640]{2,1,0:T(8,128)(2,1)S(1)} %bitcast.9, ...), custom_call_target="tpu_custom_call" | custom-call | flops 1887436800 | bytes 8028160 | tf_op jit(solution)/shard_map/inner/pallas_call | solution.py:90
  13.8 5.3 %collective-permute-start.16 = (bf16[128,640]{1,0:T(8,128)(2,1)S(1)}, bf16[128,640]{1,0:T(8,128)(2,1)S(1)}, u32[]{:S(2)}, u32[]{:S(2)}) collective-permute-start(bf16[128,640]{1,0:T(8,128)(2,1)S(1)} %get-tuple-element.17.refs_0_), channel_id=1, source_target_pairs={{0,16},{1,17},{2,18},{3,19}} | collective-permute-start | bytes 491528 | tf_op jit(solution)/shard_map/ppermute | solution.py:258
  19.1 1.6 %collective-permute-start.17 = (bf16[128,640]{1,0:T(8,128)(2,1)S(1)}, bf16[128,640]{1,0:T(8,128)(2,1)S(1)}, u32[]{:S(2)}, u32[]{:S(2)}) collective-permute-start(bf16[128,640]{1,0:T(8,128)(2,1)S(1)} %get-tuple-element.18.refs_1_), channel_id=1, source_target_pairs={{0,20},{1,21},{2,22},{3,23}} | collective-permute-start | bytes 491528 | tf_op jit(solution)/shard_map/ppermute | solution.py:259
  20.8 0.0 collective-permute-done
  20.8 4.5 %outer.1 = (bf16[128,640]{1,0:T(8,128)(2,1)S(1)}, bf16[128,640]{1,0:T(8,128)(2,1)S(1)}) custom-call(bf16[512,640]{1,0:T(8,128)(2,1)S(1)} %bitcast.12, bf16[32,640]{1,0:T(8,128)(2,1)S(1)} %bitcast.13, bf16[32,640]{1,0:T(8,128)(2,1)S(1)} %bitcast.14, bf16[3,1920,640]{2,1,0:T(8,128)(2,1)S(1)} %bitcast.10, bf16[640]{0:T(1024)(128)(2,1)S(1)} %copy-done.5), custom_call_target="tpu_custom_call" | custom-call | flops 1887436800 | bytes 8028160 | tf_op jit(solution)/shard_map/outer/pallas_call | solution.py:90
  25.3 1.3 %collective-permute-start.4 = (bf16[128,640]{1,0:T(8,128)(2,1)S(1)}, bf16[128,640]{1,0:T(8,128)(2,1)S(1)}, u32[]{:S(2)}, u32[]{:S(2)}) collective-permute-start(bf16[128,640]{1,0:T(8,128)(2,1)S(1)} %get-tuple-element.19.refs_2_), channel_id=1, source_target_pairs={{0,16},{1,17},{2,18},{3,19}} | collective-permute-start | bytes 491528 | tf_op jit(solution)/shard_map/ppermute | solution.py:258
  26.7 1.3 %collective-permute-start.5 = (bf16[128,640]{1,0:T(8,128)(2,1)S(1)}, bf16[128,640]{1,0:T(8,128)(2,1)S(1)}, u32[]{:S(2)}, u32[]{:S(2)}) collective-permute-start(bf16[128,640]{1,0:T(8,128)(2,1)S(1)} %get-tuple-element.20.refs_3_), channel_id=1, source_target_pairs={{0,20},{1,21},{2,22},{3,23}} | collective-permute-start | bytes 491528 | tf_op jit(solution)/shard_map/ppermute | solution.py:259
  28.0 1.3 %collective-permute-start.14 = (bf16[128,640]{1,0:T(8,128)(2,1)S(1)}, bf16[128,640]{1,0:T(8,128)(2,1)S(1)}, u32[]{:S(2)}, u32[]{:S(2)}) collective-permute-start(bf16[128,640]{1,0:T(8,128)(2,1)S(1)} %get-tuple-element.17.refs_0_), channel_id=1, source_target_pairs={{0,8},{1,9},{2,10},{3,11}} | collective-permute-start | bytes 491528 | tf_op jit(solution)/shard_map/ppermute | solution.py:258
  29.3 1.3 %collective-permute-start.15 = (bf16[128,640]{1,0:T(8,128)(2,1)S(1)}, bf16[128,640]{1,0:T(8,128)(2,1)S(1)}, u32[]{:S(2)}, u32[]{:S(2)}) collective-permute-start(bf16[128,640]{1,0:T(8,128)(2,1)S(1)} %get-tuple-element.18.refs_1_), channel_id=1, source_target_pairs={{0,12},{1,13},{2,14},{3,15}} | collective-permute-start | bytes 491528 | tf_op jit(solution)/shard_map/ppermute | solution.py:259
  30.6 1.3 %collective-permute-start.19 = (bf16[128,640]{1,0:T(8,128)(2,1)S(1)}, bf16[128,640]{1,0:T(8,128)(2,1)S(1)}, u32[]{:S(2)}, u32[]{:S(2)}) collective-permute-start(bf16[128,640]{1,0:T(8,128)(2,1)S(1)} %get-tuple-element.18.refs_1_), channel_id=1, source_target_pairs={{0,4},{1,5},{2,6},{3,7}} | collective-permute-start | bytes 491528 | tf_op jit(solution)/shard_map/ppermute | solution.py:269
  32.0 0.7 collective-permute-start.18
  32.7 0.0 copy-start.6
  32.7 0.6 collective-permute-done.5
  33.2 1.3 %collective-permute-start.2 = (bf16[128,640]{1,0:T(8,128)(2,1)S(1)}, bf16[128,640]{1,0:T(8,128)(2,1)S(1)}, u32[]{:S(2)}, u32[]{:S(2)}) collective-permute-start(bf16[128,640]{1,0:T(8,128)(2,1)S(1)} %get-tuple-element.19.refs_2_), channel_id=1, source_target_pairs={{0,8},{1,9},{2,10},{3,11}} | collective-permute-start | bytes 491528 | tf_op jit(solution)/shard_map/ppermute | solution.py:258
  34.6 2.2 %collective-permute-done.14 = bf16[128,640]{1,0:T(8,128)(2,1)S(1)} collective-permute-done((bf16[128,640]{1,0:T(8,128)(2,1)S(1)}, bf16[128,640]{1,0:T(8,128)(2,1)S(1)}, u32[]{:S(2)}, u32[]{:S(2)}) %collective-permute-start.14) | collective-permute-done | bytes 163872 | tf_op jit(solution)/shard_map/ppermute | solution.py:258
  36.7 1.3 %collective-permute-start.3 = (bf16[128,640]{1,0:T(8,128)(2,1)S(1)}, bf16[128,640]{1,0:T(8,128)(2,1)S(1)}, u32[]{:S(2)}, u32[]{:S(2)}) collective-permute-start(bf16[128,640]{1,0:T(8,128)(2,1)S(1)} %get-tuple-element.20.refs_3_), channel_id=1, source_target_pairs={{0,12},{1,13},{2,14},{3,15}} | collective-permute-start | bytes 491528 | tf_op jit(solution)/shard_map/ppermute | solution.py:259
  38.0 2.2 %collective-permute-done.15 = bf16[128,640]{1,0:T(8,128)(2,1)S(1)} collective-permute-done((bf16[128,640]{1,0:T(8,128)(2,1)S(1)}, bf16[128,640]{1,0:T(8,128)(2,1)S(1)}, u32[]{:S(2)}, u32[]{:S(2)}) %collective-permute-start.15) | collective-permute-done | bytes 163872 | tf_op jit(solution)/shard_map/ppermute | solution.py:259
  40.3 1.3 %collective-permute-start.7 = (bf16[128,640]{1,0:T(8,128)(2,1)S(1)}, bf16[128,640]{1,0:T(8,128)(2,1)S(1)}, u32[]{:S(2)}, u32[]{:S(2)}) collective-permute-start(bf16[128,640]{1,0:T(8,128)(2,1)S(1)} %get-tuple-element.20.refs_3_), channel_id=1, source_target_pairs={{0,4},{1,5},{2,6},{3,7}} | collective-permute-start | bytes 491528 | tf_op jit(solution)/shard_map/ppermute | solution.py:269
  41.6 0.9 collective-permute-start.6
  42.4 0.1 add_select_fusion.refs_0_
  42.5 0.0 copy-start.2
  42.5 0.1 collective-permute-start.24
  42.6 1.2 %collective-permute-done.2 = bf16[128,640]{1,0:T(8,128)(2,1)S(1)} collective-permute-done((bf16[128,640]{1,0:T(8,128)(2,1)S(1)}, bf16[128,640]{1,0:T(8,128)(2,1)S(1)}, u32[]{:S(2)}, u32[]{:S(2)}) %collective-permute-start.2) | collective-permute-done | bytes 163872 | tf_op jit(solution)/shard_map/ppermute | solution.py:258
  43.8 5.1 %collective-permute-start.26 = (bf16[128,640]{1,0:T(8,128)(2,1)S(1)}, bf16[128,640]{1,0:T(8,128)(2,1)S(1)}, u32[]{:S(2)}, u32[]{:S(2)}) collective-permute-start(bf16[128,640]{1,0:T(8,128)(2,1)S(1)} %add_select_fusion.refs_0_), channel_id=1, source_target_pairs={{0,2},{1,3},{2,0},{3,1},{4,6},{5,7},{6,4},{7,5},{8,10},{9,11},{10,... | collective-permute-start | bytes 491528 | tf_op jit(solution)/shard_map/ppermute | solution.py:280
  48.8 0.1 collective-permute-start.23
  48.9 2.9 %collective-permute-start.20 = (bf16[128,640]{1,0:T(8,128)(2,1)S(1)}, bf16[128,640]{1,0:T(8,128)(2,1)S(1)}, u32[]{:S(2)}, u32[]{:S(2)}) collective-permute-start(bf16[128,640]{1,0:T(8,128)(2,1)S(1)} %add_select_fusion.refs_0_), channel_id=1, source_target_pairs={{0,6},{1,7},{2,4},{3,5},{4,2},{5,3},{6,0},{7,1},{8,14},{9,15},{10,... | collective-permute-start | bytes 491528 | tf_op jit(solution)/shard_map/ppermute | solution.py:280
  51.9 0.1 add_select_fusion.1.refs_2_
  51.9 0.1 collective-permute-start.10
  52.0 1.7 %collective-permute-start.12 = (bf16[128,640]{1,0:T(8,128)(2,1)S(1)}, bf16[128,640]{1,0:T(8,128)(2,1)S(1)}, u32[]{:S(2)}, u32[]{:S(2)}) collective-permute-start(bf16[128,640]{1,0:T(8,128)(2,1)S(1)} %add_select_fusion.1.refs_2_), channel_id=1, source_target_pairs={{0,6},{1,7},{2,4},{3,5},{4,2},{5,3},{6,0},{7,1},{8,14},{9,15},{10,... | collective-permute-start | bytes 491528 | tf_op jit(solution)/shard_map/ppermute | solution.py:280
  53.7 1.8 %collective-permute-start.8 = (bf16[128,640]{1,0:T(8,128)(2,1)S(1)}, bf16[128,640]{1,0:T(8,128)(2,1)S(1)}, u32[]{:S(2)}, u32[]{:S(2)}) collective-permute-start(bf16[128,640]{1,0:T(8,128)(2,1)S(1)} %add_select_fusion.1.refs_2_), channel_id=1, source_target_pairs={{0,4},{1,5},{2,6},{3,7},{4,0},{5,1},{6,2},{7,3},{8,12},{9,13},{10,... | collective-permute-start | bytes 491528 | tf_op jit(solution)/shard_map/ppermute | solution.py:280
  55.5 1.4 %collective-permute-done.20.refs_0_ = bf16[128,640]{1,0:T(8,128)(2,1)S(1)} collective-permute-done((bf16[128,640]{1,0:T(8,128)(2,1)S(1)}, bf16[128,640]{1,0:T(8,128)(2,1)S(1)}, u32[]{:S(2)}, u32[]{:S(2)}) %collective-permute-start.20) | collective-permute-done | bytes 163872 | tf_op jit(solution)/shard_map/ppermute | solution.py:280
  56.9 3.4 %collective-permute-done.10.refs_2_ = bf16[128,640]{1,0:T(8,128)(2,1)S(1)} collective-permute-done((bf16[128,640]{1,0:T(8,128)(2,1)S(1)}, bf16[128,640]{1,0:T(8,128)(2,1)S(1)}, u32[]{:S(2)}, u32[]{:S(2)}) %collective-permute-start.10) | collective-permute-done | bytes 163872 | tf_op jit(solution)/shard_map/ppermute | solution.py:280
  60.3 3.2 %collective-permute-done.12.refs_4_ = bf16[128,640]{1,0:T(8,128)(2,1)S(1)} collective-permute-done((bf16[128,640]{1,0:T(8,128)(2,1)S(1)}, bf16[128,640]{1,0:T(8,128)(2,1)S(1)}, u32[]{:S(2)}, u32[]{:S(2)}) %collective-permute-start.12) | collective-permute-done | bytes 163872 | tf_op jit(solution)/shard_map/ppermute | solution.py:280
  63.5 0.5 collective-permute-start.11
  64.0 0.1 collective-permute-start.13
  64.1 0.4 collective-permute-start.9
  64.5 0.8 ask.1
  65.3 7.1 %attend0.1 = (f32[512,640]{1,0:T(8,128)S(1)}, f32[512,640]{1,0:T(8,128)S(1)}, f32[512,640]{1,0:T(8,128)S(1)}) custom-call(bf16[512,640]{1,0:T(8,128)(2,1)S(1)} %get-tuple-element.21.queries_ref, bf16[640,1280]{1,0:T(8,128)(2,1)S(1)} %copy-done.2, bf16[128,640]{1,0:T(8,128)(2,1)S(1)} %add_select_fusion.refs_0_, ...), custom_call_target="tpu_custom_call" | custom-call | flops 1006632960 | bytes 2949120 | tf_op jit(solution)/shard_map/attend0/pallas_call | solution.py:219
  72.4 0.0 copy-start.4
  72.4 6.4 %attend1.1 = (f32[512,640]{1,0:T(8,128)S(1)}, f32[512,640]{1,0:T(8,128)S(1)}, f32[512,640]{1,0:T(8,128)S(1)}) custom-call(bf16[512,640]{1,0:T(8,128)(2,1)S(1)} %get-tuple-element.21.queries_ref, bf16[640,1280]{1,0:T(8,128)(2,1)S(1)} %copy-done.2, bf16[128,640]{1,0:T(8,128)(2,1)S(1)} %collective-permute-done.20.refs_0_, ...), custom_call_target="tpu_custom_call" | custom-call | flops 671088640 | bytes 2621440 | tf_op jit(solution)/shard_map/attend1/pallas_call | solution.py:219
  78.9 9.9 %attend2.1 = bf16[512,640]{1,0:T(8,128)(2,1)} custom-call(bf16[512,640]{1,0:T(8,128)(2,1)S(1)} %get-tuple-element.21.queries_ref, bf16[640,1280]{1,0:T(8,128)(2,1)S(1)} %copy-done.2, bf16[128,640]{1,0:T(8,128)(2,1)S(1)} %collective-permute-done.8.refs_0_, bf16[128,640]{1,0:T(8,128)(2,1)S(1)} %collective-permute-done.9.refs_1_, ...), custom_call_target="tpu_custom_call" | custom-call | flops 1006632960 | bytes 2949120 | tf_op jit(solution)/shard_map/attend2/pallas_call | solution.py:219
  (34 shorter events, 0.2 us)
Async XLA Ops:
  0.8 20.0 %collective-permute-start = (bf16[1,32,640]{2,1,0:T(8,128)(2,1)S(1)}, bf16[1,32,640]{2,1,0:T(8,128)(2,1)S(1)}, u32[]{:S(2)}, u32[]{:S(2)}) collective-permute-start(bf16[1,32,640]{2,1,0:T(8,128)(2,1)S(1)} %get-tuple-element.30), channel_id=1, source_target_pairs={{0,1},{1,2},{2,3},{4,5},{5,6},{6,7},{8,9},{9,10},{10,11},{12,13},{... | collective-permute-start | bytes 122888 | tf_op jit(solution)/shard_map/ppermute | solution.py:246
  3.2 17.6 %collective-permute-start.1 = (bf16[1,32,640]{2,1,0:T(8,128)(2,1)S(1)}, bf16[1,32,640]{2,1,0:T(8,128)(2,1)S(1)}, u32[]{:S(2)}, u32[]{:S(2)}) collective-permute-start(bf16[1,32,640]{2,1,0:T(8,128)(2,1)S(1)} %get-tuple-element.29), channel_id=1, source_target_pairs={{1,0},{2,1},{3,2},{5,4},{6,5},{7,6},{9,8},{10,9},{11,10},{13,12},{... | collective-permute-start | bytes 122888 | tf_op jit(solution)/shard_map/ppermute | solution.py:247
  4.5 3.1 %copy-start = (bf16[3,3,640,640]{3,2,1,0:T(8,128)(2,1)S(1)}, bf16[3,3,640,640]{3,2,1,0:T(8,128)(2,1)}, u32[]{:S(2)}) copy-start(bf16[3,3,640,640]{3,2,1,0:T(8,128)(2,1)} %param.7) | copy-start | bytes 22118404
  7.6 1.1 %copy-start.3 = (bf16[1,16,32,640]{3,2,1,0:T(8,128)(2,1)S(1)}, bf16[1,16,32,640]{3,2,1,0:T(8,128)(2,1)}, u32[]{:S(2)}) copy-start(bf16[1,16,32,640]{3,2,1,0:T(8,128)(2,1)} %param.6) | copy-start | bytes 1966084
  8.7 0.7 copy-start.5
  9.3 11.5 %copy-start.1 = (bf16[3,3,640,640]{3,2,1,0:T(8,128)(2,1)S(1)}, bf16[3,3,640,640]{3,2,1,0:T(8,128)(2,1)}, u32[]{:S(2)}) copy-start(bf16[3,3,640,640]{3,2,1,0:T(8,128)(2,1)} %param.7) | copy-start | bytes 22118404
  13.8 15.5 %collective-permute-start.16 = (bf16[128,640]{1,0:T(8,128)(2,1)S(1)}, bf16[128,640]{1,0:T(8,128)(2,1)S(1)}, u32[]{:S(2)}, u32[]{:S(2)}) collective-permute-start(bf16[128,640]{1,0:T(8,128)(2,1)S(1)} %get-tuple-element.17.refs_0_), channel_id=1, source_target_pairs={{0,16},{1,17},{2,18},{3,19}} | collective-permute-start | bytes 491528 | tf_op jit(solution)/shard_map/ppermute | solution.py:258
  19.1 11.5 %collective-permute-start.17 = (bf16[128,640]{1,0:T(8,128)(2,1)S(1)}, bf16[128,640]{1,0:T(8,128)(2,1)S(1)}, u32[]{:S(2)}, u32[]{:S(2)}) collective-permute-start(bf16[128,640]{1,0:T(8,128)(2,1)S(1)} %get-tuple-element.18.refs_1_), channel_id=1, source_target_pairs={{0,20},{1,21},{2,22},{3,23}} | collective-permute-start | bytes 491528 | tf_op jit(solution)/shard_map/ppermute | solution.py:259
  25.3 6.6 %collective-permute-start.4 = (bf16[128,640]{1,0:T(8,128)(2,1)S(1)}, bf16[128,640]{1,0:T(8,128)(2,1)S(1)}, u32[]{:S(2)}, u32[]{:S(2)}) collective-permute-start(bf16[128,640]{1,0:T(8,128)(2,1)S(1)} %get-tuple-element.19.refs_2_), channel_id=1, source_target_pairs={{0,16},{1,17},{2,18},{3,19}} | collective-permute-start | bytes 491528 | tf_op jit(solution)/shard_map/ppermute | solution.py:258
  26.7 6.6 %collective-permute-start.5 = (bf16[128,640]{1,0:T(8,128)(2,1)S(1)}, bf16[128,640]{1,0:T(8,128)(2,1)S(1)}, u32[]{:S(2)}, u32[]{:S(2)}) collective-permute-start(bf16[128,640]{1,0:T(8,128)(2,1)S(1)} %get-tuple-element.20.refs_3_), channel_id=1, source_target_pairs={{0,20},{1,21},{2,22},{3,23}} | collective-permute-start | bytes 491528 | tf_op jit(solution)/shard_map/ppermute | solution.py:259
  28.0 8.8 %collective-permute-start.14 = (bf16[128,640]{1,0:T(8,128)(2,1)S(1)}, bf16[128,640]{1,0:T(8,128)(2,1)S(1)}, u32[]{:S(2)}, u32[]{:S(2)}) collective-permute-start(bf16[128,640]{1,0:T(8,128)(2,1)S(1)} %get-tuple-element.17.refs_0_), channel_id=1, source_target_pairs={{0,8},{1,9},{2,10},{3,11}} | collective-permute-start | bytes 491528 | tf_op jit(solution)/shard_map/ppermute | solution.py:258
  29.3 11.0 %collective-permute-start.15 = (bf16[128,640]{1,0:T(8,128)(2,1)S(1)}, bf16[128,640]{1,0:T(8,128)(2,1)S(1)}, u32[]{:S(2)}, u32[]{:S(2)}) collective-permute-start(bf16[128,640]{1,0:T(8,128)(2,1)S(1)} %get-tuple-element.18.refs_1_), channel_id=1, source_target_pairs={{0,12},{1,13},{2,14},{3,15}} | collective-permute-start | bytes 491528 | tf_op jit(solution)/shard_map/ppermute | solution.py:259
  30.6 11.0 %collective-permute-start.19 = (bf16[128,640]{1,0:T(8,128)(2,1)S(1)}, bf16[128,640]{1,0:T(8,128)(2,1)S(1)}, u32[]{:S(2)}, u32[]{:S(2)}) collective-permute-start(bf16[128,640]{1,0:T(8,128)(2,1)S(1)} %get-tuple-element.18.refs_1_), channel_id=1, source_target_pairs={{0,4},{1,5},{2,6},{3,7}} | collective-permute-start | bytes 491528 | tf_op jit(solution)/shard_map/ppermute | solution.py:269
  32.0 10.5 %collective-permute-start.18 = (bf16[128,640]{1,0:T(8,128)(2,1)S(1)}, bf16[128,640]{1,0:T(8,128)(2,1)S(1)}, u32[]{:S(2)}, u32[]{:S(2)}) collective-permute-start(bf16[128,640]{1,0:T(8,128)(2,1)S(1)} %add.36), channel_id=1, source_target_pairs={{16,24},{20,28},{17,25},{21,29},{18,26},{22,30},{19,27},{23,31}} | collective-permute-start | bytes 491528 | tf_op jit(solution)/shard_map/ppermute | solution.py:265
  32.7 31.9 %copy-start.6 = (bf16[640,640]{1,0:T(8,128)(2,1)S(1)}, bf16[640,640]{1,0:T(8,128)(2,1)}, u32[]{:S(2)}) copy-start(bf16[640,640]{1,0:T(8,128)(2,1)} %refs_4_.1) | copy-start | bytes 2457604
  33.2 10.5 %collective-permute-start.2 = (bf16[128,640]{1,0:T(8,128)(2,1)S(1)}, bf16[128,640]{1,0:T(8,128)(2,1)S(1)}, u32[]{:S(2)}, u32[]{:S(2)}) collective-permute-start(bf16[128,640]{1,0:T(8,128)(2,1)S(1)} %get-tuple-element.19.refs_2_), channel_id=1, source_target_pairs={{0,8},{1,9},{2,10},{3,11}} | collective-permute-start | bytes 491528 | tf_op jit(solution)/shard_map/ppermute | solution.py:258
  36.7 12.1 %collective-permute-start.3 = (bf16[128,640]{1,0:T(8,128)(2,1)S(1)}, bf16[128,640]{1,0:T(8,128)(2,1)S(1)}, u32[]{:S(2)}, u32[]{:S(2)}) collective-permute-start(bf16[128,640]{1,0:T(8,128)(2,1)S(1)} %get-tuple-element.20.refs_3_), channel_id=1, source_target_pairs={{0,12},{1,13},{2,14},{3,15}} | collective-permute-start | bytes 491528 | tf_op jit(solution)/shard_map/ppermute | solution.py:259
  40.3 8.7 %collective-permute-start.7 = (bf16[128,640]{1,0:T(8,128)(2,1)S(1)}, bf16[128,640]{1,0:T(8,128)(2,1)S(1)}, u32[]{:S(2)}, u32[]{:S(2)}) collective-permute-start(bf16[128,640]{1,0:T(8,128)(2,1)S(1)} %get-tuple-element.20.refs_3_), channel_id=1, source_target_pairs={{0,4},{1,5},{2,6},{3,7}} | collective-permute-start | bytes 491528 | tf_op jit(solution)/shard_map/ppermute | solution.py:269
  41.6 10.3 %collective-permute-start.6 = (bf16[128,640]{1,0:T(8,128)(2,1)S(1)}, bf16[128,640]{1,0:T(8,128)(2,1)S(1)}, u32[]{:S(2)}, u32[]{:S(2)}) collective-permute-start(bf16[128,640]{1,0:T(8,128)(2,1)S(1)} %add.31), channel_id=1, source_target_pairs={{16,24},{20,28},{17,25},{21,29},{18,26},{22,30},{19,27},{23,31}} | collective-permute-start | bytes 491528 | tf_op jit(solution)/shard_map/ppermute | solution.py:265
  42.5 22.8 %copy-start.2 = (bf16[640,1280]{1,0:T(8,128)(2,1)S(1)}, bf16[640,1280]{1,0:T(8,128)(2,1)}, u32[]{:S(2)}) copy-start(bf16[640,1280]{1,0:T(8,128)(2,1)} %keyval_hbm.5) | copy-start | bytes 4915204
  42.5 9.5 %collective-permute-start.24 = (bf16[128,640]{1,0:T(8,128)(2,1)S(1)}, bf16[128,640]{1,0:T(8,128)(2,1)S(1)}, u32[]{:S(2)}, u32[]{:S(2)}) collective-permute-start(bf16[128,640]{1,0:T(8,128)(2,1)S(1)} %add_select_fusion.refs_0_), channel_id=1, source_target_pairs={{0,4},{1,5},{2,6},{3,7},{4,0},{5,1},{6,2},{7,3},{8,12},{9,13},{10,... | collective-permute-start | bytes 491528 | tf_op jit(solution)/shard_map/ppermute | solution.py:280
  43.8 9.9 %collective-permute-start.26 = (bf16[128,640]{1,0:T(8,128)(2,1)S(1)}, bf16[128,640]{1,0:T(8,128)(2,1)S(1)}, u32[]{:S(2)}, u32[]{:S(2)}) collective-permute-start(bf16[128,640]{1,0:T(8,128)(2,1)S(1)} %add_select_fusion.refs_0_), channel_id=1, source_target_pairs={{0,2},{1,3},{2,0},{3,1},{4,6},{5,7},{6,4},{7,5},{8,10},{9,11},{10,... | collective-permute-start | bytes 491528 | tf_op jit(solution)/shard_map/ppermute | solution.py:280
  48.8 6.6 %collective-permute-start.23 = (bf16[128,640]{1,0:T(8,128)(2,1)S(1)}, bf16[128,640]{1,0:T(8,128)(2,1)S(1)}, u32[]{:S(2)}, u32[]{:S(2)}) collective-permute-start(bf16[128,640]{1,0:T(8,128)(2,1)S(1)} %add_select_fusion.refs_0_), channel_id=1, source_target_pairs={{0,1},{1,0},{2,3},{3,2},{4,5},{5,4},{6,7},{7,6},{8,9},{9,8},{10,11... | collective-permute-start | bytes 491528 | tf_op jit(solution)/shard_map/ppermute | solution.py:280
  48.9 7.9 %collective-permute-start.20 = (bf16[128,640]{1,0:T(8,128)(2,1)S(1)}, bf16[128,640]{1,0:T(8,128)(2,1)S(1)}, u32[]{:S(2)}, u32[]{:S(2)}) collective-permute-start(bf16[128,640]{1,0:T(8,128)(2,1)S(1)} %add_select_fusion.refs_0_), channel_id=1, source_target_pairs={{0,6},{1,7},{2,4},{3,5},{4,2},{5,3},{6,0},{7,1},{8,14},{9,15},{10,... | collective-permute-start | bytes 491528 | tf_op jit(solution)/shard_map/ppermute | solution.py:280
  51.9 8.4 %collective-permute-start.10 = (bf16[128,640]{1,0:T(8,128)(2,1)S(1)}, bf16[128,640]{1,0:T(8,128)(2,1)S(1)}, u32[]{:S(2)}, u32[]{:S(2)}) collective-permute-start(bf16[128,640]{1,0:T(8,128)(2,1)S(1)} %add_select_fusion.1.refs_2_), channel_id=1, source_target_pairs={{0,2},{1,3},{2,0},{3,1},{4,6},{5,7},{6,4},{7,5},{8,10},{9,11},{10,... | collective-permute-start | bytes 491528 | tf_op jit(solution)/shard_map/ppermute | solution.py:280
  52.0 11.5 %collective-permute-start.12 = (bf16[128,640]{1,0:T(8,128)(2,1)S(1)}, bf16[128,640]{1,0:T(8,128)(2,1)S(1)}, u32[]{:S(2)}, u32[]{:S(2)}) collective-permute-start(bf16[128,640]{1,0:T(8,128)(2,1)S(1)} %add_select_fusion.1.refs_2_), channel_id=1, source_target_pairs={{0,6},{1,7},{2,4},{3,5},{4,2},{5,3},{6,0},{7,1},{8,14},{9,15},{10,... | collective-permute-start | bytes 491528 | tf_op jit(solution)/shard_map/ppermute | solution.py:280
  53.7 9.8 %collective-permute-start.8 = (bf16[128,640]{1,0:T(8,128)(2,1)S(1)}, bf16[128,640]{1,0:T(8,128)(2,1)S(1)}, u32[]{:S(2)}, u32[]{:S(2)}) collective-permute-start(bf16[128,640]{1,0:T(8,128)(2,1)S(1)} %add_select_fusion.1.refs_2_), channel_id=1, source_target_pairs={{0,4},{1,5},{2,6},{3,7},{4,0},{5,1},{6,2},{7,3},{8,12},{9,13},{10,... | collective-permute-start | bytes 491528 | tf_op jit(solution)/shard_map/ppermute | solution.py:280
  55.5 8.5 %collective-permute-start.25 = (bf16[128,640]{1,0:T(8,128)(2,1)S(1)}, bf16[128,640]{1,0:T(8,128)(2,1)S(1)}, u32[]{:S(2)}, u32[]{:S(2)}) collective-permute-start(bf16[128,640]{1,0:T(8,128)(2,1)S(1)} %collective-permute-done.24.refs_2_), channel_id=1, source_target_pairs={{0,1},{1,0},{2,3},{3,2},{4,5},{5,4},{6,7},{7,6},{8,9},{9,8},{10,11... | collective-permute-start | bytes 491528 | tf_op jit(solution)/shard_map/ppermute | solution.py:280
  56.8 7.2 %collective-permute-start.27 = (bf16[128,640]{1,0:T(8,128)(2,1)S(1)}, bf16[128,640]{1,0:T(8,128)(2,1)S(1)}, u32[]{:S(2)}, u32[]{:S(2)}) collective-permute-start(bf16[128,640]{1,0:T(8,128)(2,1)S(1)} %collective-permute-done.26.refs_4_), channel_id=1, source_target_pairs={{0,1},{1,0},{2,3},{3,2},{4,5},{5,4},{6,7},{7,6},{8,9},{9,8},{10,11... | collective-permute-start | bytes 491528 | tf_op jit(solution)/shard_map/ppermute | solution.py:280
  60.3 12.1 %collective-permute-start.22 = (bf16[128,640]{1,0:T(8,128)(2,1)S(1)}, bf16[128,640]{1,0:T(8,128)(2,1)S(1)}, u32[]{:S(2)}, u32[]{:S(2)}) collective-permute-start(bf16[128,640]{1,0:T(8,128)(2,1)S(1)} %add_select_fusion.1.refs_2_), channel_id=1, source_target_pairs={{0,1},{1,0},{2,3},{3,2},{4,5},{5,4},{6,7},{7,6},{8,9},{9,8},{10,11... | collective-permute-start | bytes 491528 | tf_op jit(solution)/shard_map/ppermute | solution.py:280
  63.5 8.9 %collective-permute-start.21 = (bf16[128,640]{1,0:T(8,128)(2,1)S(1)}, bf16[128,640]{1,0:T(8,128)(2,1)S(1)}, u32[]{:S(2)}, u32[]{:S(2)}) collective-permute-start(bf16[128,640]{1,0:T(8,128)(2,1)S(1)} %collective-permute-done.20.refs_0_), channel_id=1, source_target_pairs={{0,1},{1,0},{2,3},{3,2},{4,5},{5,4},{6,7},{7,6},{8,9},{9,8},{10,11... | collective-permute-start | bytes 491528 | tf_op jit(solution)/shard_map/ppermute | solution.py:280
  63.5 15.4 %collective-permute-start.11 = (bf16[128,640]{1,0:T(8,128)(2,1)S(1)}, bf16[128,640]{1,0:T(8,128)(2,1)S(1)}, u32[]{:S(2)}, u32[]{:S(2)}) collective-permute-start(bf16[128,640]{1,0:T(8,128)(2,1)S(1)} %collective-permute-done.10.refs_2_), channel_id=1, source_target_pairs={{0,1},{1,0},{2,3},{3,2},{4,5},{5,4},{6,7},{7,6},{8,9},{9,8},{10,11... | collective-permute-start | bytes 491528 | tf_op jit(solution)/shard_map/ppermute | solution.py:280
  64.0 14.9 %collective-permute-start.13 = (bf16[128,640]{1,0:T(8,128)(2,1)S(1)}, bf16[128,640]{1,0:T(8,128)(2,1)S(1)}, u32[]{:S(2)}, u32[]{:S(2)}) collective-permute-start(bf16[128,640]{1,0:T(8,128)(2,1)S(1)} %collective-permute-done.12.refs_4_), channel_id=1, source_target_pairs={{0,1},{1,0},{2,3},{3,2},{4,5},{5,4},{6,7},{7,6},{8,9},{9,8},{10,11... | collective-permute-start | bytes 491528 | tf_op jit(solution)/shard_map/ppermute | solution.py:280
  64.1 14.8 %collective-permute-start.9 = (bf16[128,640]{1,0:T(8,128)(2,1)S(1)}, bf16[128,640]{1,0:T(8,128)(2,1)S(1)}, u32[]{:S(2)}, u32[]{:S(2)}) collective-permute-start(bf16[128,640]{1,0:T(8,128)(2,1)S(1)} %collective-permute-done.8.refs_0_), channel_id=1, source_target_pairs={{0,1},{1,0},{2,3},{3,2},{4,5},{5,4},{6,7},{7,6},{8,9},{9,8},{10,11... | collective-permute-start | bytes 491528 | tf_op jit(solution)/shard_map/ppermute | solution.py:280
  72.4 6.5 %copy-start.4 = (bf16[640,640]{1,0:T(8,128)(2,1)S(1)}, bf16[640,640]{1,0:T(8,128)(2,1)}, u32[]{:S(2)}) copy-start(bf16[640,640]{1,0:T(8,128)(2,1)} %refs_10_.1) | copy-start | bytes 2457604

commit v3 on v2

v3 whole, which is shorter than its diff:
```python
import functools

import jax
import jax.numpy as jnp
from jax import lax
from jax.experimental import pallas as pl
from jax.experimental.pallas import tpu as pltpu
from jax.sharding import PartitionSpec as P

HEAD_DIM = 64
PAIR = 2 * HEAD_DIM
VMEM_BYTES = 40 * 2**20
CONV_VMEM_BYTES = 44 * 2**20
IN_VMEM = pl.BlockSpec(memory_space=pltpu.VMEM)
IN_PLACE = pl.BlockSpec(memory_space=pl.ANY)
IN_HBM = pl.BlockSpec(memory_space=pltpu.HBM)
SHIFTS = (1, 0, 2)
QUICK = pl.CostEstimate(flops=1, bytes_accessed=1, transcendentals=0)


def conv_span(width, spans, x_hbm, low_ref, high_ref, weight, bias_ref, rows, taps, sems, before_use):
    tokens, channels = x_hbm.shape
    last_row = tokens // width
    loads, edges, starts, place = [], [], [], 0
    for first, count in spans:
        begin, end = max(first - 1, 0), min(first + count + 1, last_row)
        starts.append(place)
        if first == 0:
            edges.append((low_ref, place))
            place += 1
        loads.append((begin, end - begin, place))
        place += end - begin
        if first + count == last_row:
            edges.append((high_ref, place))
            place += 1
    copies = [
        pltpu.make_async_copy(
            x_hbm.at[pl.ds(begin * width, count * width)],
            rows.at[pl.ds(spot * width, count * width)],
            sems.at[i],
        )
        for i, (begin, count, spot) in enumerate(loads)
    ]
    for copy in copies:
        copy.start()
    waits = before_use()
    for edge_ref, spot in edges:
        rows[spot * width : (spot + 1) * width, :] = edge_ref[...]
    for copy in copies:
        copy.wait()

    padded = place * width
    raw = rows[:padded, :].astype(jnp.float32)
    active = raw * jax.nn.sigmoid(raw)
    column = lax.rem(lax.broadcasted_iota(jnp.int32, (padded, 1), 0), width)
    before = jnp.where(column == 0, 0.0, pltpu.roll(active, 1, 0))
    after = jnp.where(column == width - 1, 0.0, pltpu.roll(active, padded - 1, 0))
    taps[:padded, :channels] = before.astype(jnp.bfloat16)
    taps[:padded, channels : 2 * channels] = active.astype(jnp.bfloat16)
    taps[:padded, 2 * channels :] = after.astype(jnp.bfloat16)

    def rows_at(ref, shift):
        parts = [
            ref[(start + shift) * width : (start + shift + count) * width, :]
            for start, (_, count) in zip(starts, spans)
        ]
        return parts[0] if len(parts) == 1 else jnp.concatenate(parts, axis=0)

    total = rows_at(rows, 1).astype(jnp.float32) + bias_ref[...].astype(jnp.float32)[None, :]
    for shift in SHIFTS:
        if waits:
            waits[shift].wait()
        total = total + jnp.dot(
            rows_at(taps, shift), weight[shift], preferred_element_type=jnp.float32
        )
    return total.astype(jnp.bfloat16)


def inner_kernel(width, spans, x_hbm, weight_hbm, bias_ref, out_ref, weight, rows, taps, sems):
    copies = [
        pltpu.make_async_copy(weight_hbm.at[shift], weight.at[shift], sems.at[shift])
        for shift in range(3)
    ]

    def fetch():
        for shift in SHIFTS:
            copies[shift].start()
        return copies

    @pl.when(lax.axis_index("frame") == 0)
    def _():
        out_ref[...] = conv_span(
            width, spans, x_hbm, None, None, weight, bias_ref, rows, taps, sems.at[pl.ds(3, len(spans))], fetch
        )

    @pl.when(lax.axis_index("frame") != 0)
    def _():
        for copy in fetch():
            copy.wait()


def outer_kernel(
    width, inner, outer, redo, x_hbm, low_ref, high_ref, weight, bias_ref, first_ref, out_ref, inner_ref,
    rows, taps, sems,
):
    def compute(spans):
        return conv_span(
            width, spans, x_hbm, low_ref, high_ref, weight, bias_ref, rows, taps,
            sems.at[pl.ds(0, len(spans))], lambda: None,
        )

    out_ref[...] = compute(outer)
    if redo:
        inner_ref[...] = compute(inner)
    else:
        @pl.when(lax.axis_index("frame") != 0)
        def _():
            inner_ref[...] = compute(inner)

        @pl.when(lax.axis_index("frame") == 0)
        def _():
            inner_ref[...] = first_ref[...]


def scratch_for(span_rows, width, channels, copies):
    return [
        pltpu.VMEM((span_rows * width, channels), jnp.bfloat16),
        pltpu.VMEM((span_rows * width, 3 * channels), jnp.bfloat16),
        pltpu.SemaphoreType.DMA((copies,)),
    ]


def convolve_inner(x, taps_weight, bias, width, inner):
    channels = x.shape[1]
    made = sum(count for _, count in inner)
    return pl.pallas_call(
        functools.partial(inner_kernel, width, inner),
        out_shape=(
            jax.ShapeDtypeStruct((made * width, channels), jnp.bfloat16),
            jax.ShapeDtypeStruct(taps_weight.shape, jnp.bfloat16),
        ),
        in_specs=[IN_HBM, IN_HBM, IN_VMEM],
        out_specs=(IN_VMEM, IN_VMEM),
        scratch_shapes=scratch_for(made + 2, width, channels, 3 + len(inner)),
        compiler_params=pltpu.CompilerParams(vmem_limit_bytes=CONV_VMEM_BYTES),
        cost_estimate=QUICK,
        name="inner",
    )(x, taps_weight, bias)


def convolve_outer(x, low, high, taps_weight, bias, first, width, inner, outer, redo):
    channels = x.shape[1]
    made = [sum(count for _, count in spans) for spans in (outer, inner)]
    padded = max(made[0] + 2 * len(outer), made[1] + 2 * len(inner))
    return pl.pallas_call(
        functools.partial(outer_kernel, width, inner, outer, redo),
        out_shape=tuple(jax.ShapeDtypeStruct((n * width, channels), jnp.bfloat16) for n in made),
        in_specs=[IN_HBM, IN_VMEM, IN_VMEM, IN_VMEM, IN_VMEM, IN_VMEM],
        out_specs=(IN_VMEM, IN_VMEM),
        scratch_shapes=scratch_for(padded, width, channels, max(len(inner), len(outer))),
        compiler_params=pltpu.CompilerParams(vmem_limit_bytes=CONV_VMEM_BYTES),
        cost_estimate=QUICK,
        name="outer",
    )(x, low, high, taps_weight, bias, first)


def query_kernel(layout, *refs):
    count = len(layout)
    pieces, (w_query, hidden_ref, queries_ref) = refs[:count], refs[count:]
    for piece, spots in zip(pieces, layout):
        taken = 0
        for start, size in spots:
            hidden_ref[start : start + size, :] = piece[taken : taken + size, :]
            taken += size
    queries = jnp.dot(hidden_ref[...], w_query[...], preferred_element_type=jnp.float32)
    queries_ref[...] = queries.astype(jnp.bfloat16)


def ask(pieces, layout, w_query):
    tokens, channels = sum(piece.shape[0] for piece in pieces), w_query.shape[0]
    whole = jax.ShapeDtypeStruct((tokens, channels), jnp.bfloat16)
    return pl.pallas_call(
        functools.partial(query_kernel, layout),
        out_shape=(whole, whole),
        in_specs=[IN_VMEM] * (len(pieces) + 1),
        out_specs=(IN_VMEM, IN_VMEM),
        compiler_params=pltpu.CompilerParams(vmem_limit_bytes=16 * 2**20),
        cost_estimate=QUICK,
        name="ask",
    )(*pieces, w_query)


def attend_kernel(piece_count, part_count, last, queries_ref, keyval_hbm, *refs):
    refs = list(refs)
    pieces = [refs.pop(0) for _ in range(piece_count)]
    parts = [[refs.pop(0) for _ in range(3)] for _ in range(part_count)]
    ending = [refs.pop(0) for _ in range(2)] if last else None
    new = [refs.pop(0) for _ in range(1 if last else 3)]
    w_keyval, w_out, keys, values, mixed, sems = refs
    tokens, channels = queries_ref.shape
    keyval_copy = pltpu.make_async_copy(keyval_hbm, w_keyval, sems.at[0])
    keyval_copy.start()
    if last:
        out_copy = pltpu.make_async_copy(ending[1], w_out, sems.at[1])
        out_copy.start()
    keyval_copy.wait()
    key_count = 0
    for piece in pieces:
        spot = slice(key_count, key_count + piece.shape[0])
        keyval = jnp.dot(piece[...], w_keyval[...], preferred_element_type=jnp.float32)
        keyval = keyval.astype(jnp.bfloat16)
        keys[spot, :] = keyval[:, :channels]
        values[spot, :] = keyval[:, channels:]
        key_count = spot.stop
    is_low = lax.broadcasted_iota(jnp.int32, (tokens, PAIR), 1) < HEAD_DIM
    ones = jnp.ones((key_count, PAIR), jnp.bfloat16)
    for start in range(0, channels, PAIR):
        lanes = slice(start, start + PAIR)
        both = queries_ref[:, lanes] * HEAD_DIM ** (-0.5)
        nothing = jnp.zeros_like(both)
        split = jnp.concatenate(
            [jnp.where(is_low, both, nothing), jnp.where(is_low, nothing, both)], axis=0
        )
        scores = lax.dot_general(
            split, keys[:, lanes], (((1,), (1,)), ((), ())), preferred_element_type=jnp.float32
        )
        best = jnp.max(scores, axis=1, keepdims=True)
        probability = jnp.exp(scores - best).astype(jnp.bfloat16)
        product = jnp.dot(
            probability,
            jnp.concatenate([values[:, lanes], ones], axis=1),
            preferred_element_type=jnp.float32,
        )
        best = jnp.where(is_low, best[:tokens], best[tokens:])
        weighted = jnp.where(is_low, product[:tokens, :PAIR], product[tokens:, :PAIR])
        total = jnp.where(is_low, product[:tokens, PAIR:], product[tokens:, PAIR:])
        if last:
            top = functools.reduce(jnp.maximum, [part[2][:, lanes] for part in parts], best)
            scale = jnp.exp(best - top)
            weighted, total = weighted * scale, total * scale
            for part in parts:
                scale = jnp.exp(part[2][:, lanes] - top)
                weighted = weighted + part[0][:, lanes] * scale
                total = total + part[1][:, lanes] * scale
            mixed[:, lanes] = (weighted / total).astype(jnp.bfloat16)
        else:
            new[0][:, lanes] = weighted
            new[1][:, lanes] = total
            new[2][:, lanes] = best
    if last:
        out_copy.wait()
        result = ending[0][...].astype(jnp.float32) + jnp.dot(
            mixed[...], w_out[...], preferred_element_type=jnp.float32
        )
        new[0][...] = result.astype(jnp.bfloat16)


def attend(queries, w_keyval, pieces, parts, ending, name):
    tokens, channels = queries.shape
    key_count = sum(piece.shape[0] for piece in pieces)
    last = ending is not None
    part = jax.ShapeDtypeStruct((tokens, channels), jnp.float32)
    whole = jax.ShapeDtypeStruct((tokens, channels), jnp.bfloat16)
    args = [queries, w_keyval, *pieces, *(array for each in parts for array in each), *(ending or ())]
    in_specs = [IN_VMEM] * len(args)
    in_specs[1] = IN_PLACE
    if last:
        in_specs[-1] = IN_PLACE
    return pl.pallas_call(
        functools.partial(attend_kernel, len(pieces), len(parts), last),
        out_shape=whole if last else (part,) * 3,
        in_specs=in_specs,
        out_specs=IN_VMEM if last else (IN_VMEM,) * 3,
        scratch_shapes=[
            pltpu.VMEM(w_keyval.shape, jnp.bfloat16),
            pltpu.VMEM((channels, channels), jnp.bfloat16),
            pltpu.VMEM((key_count, channels), jnp.bfloat16),
            pltpu.VMEM((key_count, channels), jnp.bfloat16),
            pltpu.VMEM((tokens, channels), jnp.bfloat16),
            pltpu.SemaphoreType.DMA((2,)),
        ],
        compiler_params=pltpu.CompilerParams(vmem_limit_bytes=VMEM_BYTES),
        cost_estimate=QUICK,
        name=name,
    )(*args)


def from_edges(block, axis):
    count = lax.axis_size(axis)
    forward = [(i, i + 1) for i in range(count - 1)]
    backward = [(target, source) for source, target in forward]
    low = lax.ppermute(block[:, -1], axis, forward)
    high = lax.ppermute(block[:, 0], axis, backward)
    return low, high


def permute(value, pairs):
    bands = lax.axis_size("band")
    flat = [(source[0] * bands + source[1], target[0] * bands + target[1]) for source, target in pairs]
    return lax.ppermute(value, ("frame", "band"), flat)


def ordered(value, *before):
    return lax.optimization_barrier((value, *before))[0]


def cast(own, before=()):
    frames, bands = lax.axis_size("frame"), lax.axis_size("band")
    columns = frames // 2
    reaches = [columns >> i for i in range(1, columns.bit_length())]
    direct = [
        permute(own, [((0, b), (2 * reach + b % 2, b)) for b in range(bands)]) for reach in reaches
    ]
    if direct:
        held = functools.reduce(jnp.add, lax.optimization_barrier((*direct, *before))[: len(direct)])
    else:
        held = jnp.zeros_like(own)
    for reach in reaches[1:]:
        relays = [
            ((2 * i + b % 2, b), (2 * (i + reach) + b % 2, b))
            for i in range(2 * reach, columns, 2 * reach)
            for b in range(bands)
        ]
        held = held + permute(held, relays)
    held = jnp.where(lax.axis_index("frame") == 0, own, held)
    holders = [(f, b) for f in range(2, frames) for b in range(bands) if f % 2 == b % 2]
    beside = permute(
        held,
        [((f, b), (f ^ 1, b)) for f, b in holders] + [((0, b), (1, b)) for b in range(bands)],
    )
    return held, beside


def swap(value, distance):
    frames, bands = lax.axis_size("frame"), lax.axis_size("band")
    return permute(value, [((f, b), (f, b ^ distance)) for f in range(frames) for b in range(bands)])


def sees_all(chunks, look):
    frames, bands = lax.axis_size("frame"), lax.axis_size("band")
    if frames % 2 or frames & (frames - 1) or bands != 4:
        pieces = [lax.all_gather(chunk, ("frame", "band"))[b] for chunk in chunks for b in range(bands)]
        return [], pieces
    held0, beside0 = cast(chunks[0], (chunks[1],))
    near0 = held0 + beside0
    near0_core, far0 = swap(near0, 1), swap(near0, 2)
    held1, beside1 = cast(chunks[1], (held0,))
    look0 = look([near0, ordered(near0_core, held1)])
    near1 = held1 + ordered(beside1, look0)
    near1_core, far1 = swap(near1, 1), swap(near1, 2)
    far0_core = swap(far0, 1)
    look1 = look([far0, ordered(far0_core, near1)])
    look2 = look([near1, ordered(near1_core, look1)])
    far1 = ordered(far1, look2)
    far1_core = swap(far1, 1)
    return [look0, look1, look2], [far1, far1_core]


def per_device(latents, conv_weight, conv_bias, w_query, w_keyval, w_out):
    frames, row_count, width, channels = latents.shape
    tokens = row_count * width
    half = row_count // 2
    taps_weight = conv_weight.reshape(3, 3 * channels, channels)
    inner = ((1, half),)
    outer = ((0, 1), (half + 1, row_count - half - 1))
    seam = (half + 1) * width
    layout = (((0, width), (seam, tokens - seam)), ((width, half * width),))
    low, high = from_edges(latents, "band")
    blocks = [latents[frame].reshape(tokens, channels) for frame in range(frames)]
    first, at_hand = convolve_inner(blocks[0], taps_weight, conv_bias, width, inner)
    parts = [
        convolve_outer(
            block, low[frame], high[frame], at_hand, conv_bias, first, width, inner, outer, frame > 0
        )
        for frame, block in enumerate(blocks)
    ]
    asked = [ask(part, layout, w_query) for part in parts]
    def look(pieces):
        return tuple(attend(queries, w_keyval, pieces, (), None, "attend") for _, queries in asked)

    looks, pieces = sees_all((first, parts[0][0]), look)
    results = [
        attend(queries, w_keyval, pieces, [each[i] for each in looks], (hidden, w_out), "join")
        for i, (hidden, queries) in enumerate(asked)
    ]
    return jnp.stack(results).reshape(latents.shape)


def solution(mesh):
    return jax.shard_map(
        per_device,
        mesh=mesh,
        in_specs=(P("frame", "band", None, None), P(), P(), P(), P(), P()),
        out_specs=P("frame", "band", None, None),
        check_vma=False,
    )
```

time: 89.6 us -> 78.3 us (0.87)
  the two profiles are of different devices: /device:TPU:0 before, /device:TPU:25 now
where the time goes in v3:
time: 78.3 us; the launch traced here: 77.9 us
  Pallas kernels  33.2 us (42%)
  starting transfers between devices  26 us (33%)
  waiting for transfers between devices  15.9 us (20%)
  local copies, waits for them, and re-layouts  1.8 us (2%)
    pallas_call x4, Pallas kernels, attend(): pl.pallas_call(functools.partial(attend_kernel, len(pieces), len(parts),...  23.5 us
    ppermute x14, starting transfers between devices, permute(): return lax.ppermute(value, ('frame', 'band'), flat)  20.4 us
    ppermute x14, waiting for transfers between devices, permute(): return lax.ppermute(value, ('frame', 'band'), flat)  14.9 us
    pallas_call x1, Pallas kernels, convolve_outer(): pl.pallas_call(functools.partial(outer_kernel, width, inner, outer, redo)...  5.81 us
    pallas_call x1, Pallas kernels, convolve_inner(): pl.pallas_call(functools.partial(inner_kernel, width, inner), out_shape=(...  3.21 us
    ppermute x1, starting transfers between devices, from_edges(): low = lax.ppermute(block[:, -1], axis, forward)  3.02 us
    ppermute x1, starting transfers between devices, from_edges(): high = lax.ppermute(block[:, 0], axis, backward)  2.58 us
    unnamed x10, local copies, waits for them, and re-layouts  1.79 us
  transfers between devices with their start and end apart: 16, of which 3 were waited for; matrix products, arithmetic and copies ran while one was open for 0% of the time, Pallas kernels for 27%

profile of v3, /device:TPU:25, one launch (start us, length us, event | category | flops | bytes accessed | tf_op | source)
XLA Modules:
  0.0 77.9 jit_solution(4706807188052663903)
XLA Ops:
  0.0 1.1 %copy-done.1 = bf16[1,16,32,640]{3,2,1,0:T(8,128)(2,1)S(1)} copy-done((bf16[1,16,32,640]{3,2,1,0:T(8,128)(2,1)S(1)}, bf16[1,16,32,640]{3,2,1,0:T(8,128)(2,1)}, u32[]{:S(2)}) %copy-start.1) | copy-done | bytes 655384
  1.1 0.7 copy-done.4
  1.8 3.2 %inner.1 = (bf16[256,640]{1,0:T(8,128)(2,1)S(1)}, bf16[3,1920,640]{2,1,0:T(8,128)(2,1)S(1)}) custom-call(bf16[512,640]{1,0:T(8,128)(2,1)S(1)} %bitcast.9, bf16[3,1920,640]{2,1,0:T(8,128)(2,1)} %bitcast.13, bf16[640]{0:T(1024)(128)(2,1)S(1)} %copy-done.4), custom_call_target="tpu_custom_call" | custom-call | flops 1 | bytes 1 | tf_op jit(solution)/shard_map/inner/pallas_call | solution.py:136
  5.0 0.7 collective-permute-start.5
  5.7 0.7 collective-permute-start.4
  6.4 2.6 %collective-permute-start.1 = (bf16[1,32,640]{2,1,0:T(8,128)(2,1)S(1)}, bf16[1,32,640]{2,1,0:T(8,128)(2,1)S(1)}, u32[]{:S(2)}, u32[]{:S(2)}) collective-permute-start(bf16[1,32,640]{2,1,0:T(8,128)(2,1)S(1)} %get-tuple-element.53), channel_id=1, source_target_pairs={{1,0},{2,1},{3,2},{5,4},{6,5},{7,6},{9,8},{10,9},{11,10},{13,12},{... | collective-permute-start | bytes 122888 | tf_op jit(solution)/shard_map/ppermute | solution.py:293
  9.0 3.0 %collective-permute-start = (bf16[1,32,640]{2,1,0:T(8,128)(2,1)S(1)}, bf16[1,32,640]{2,1,0:T(8,128)(2,1)S(1)}, u32[]{:S(2)}, u32[]{:S(2)}) collective-permute-start(bf16[1,32,640]{2,1,0:T(8,128)(2,1)S(1)} %get-tuple-element.54), channel_id=1, source_target_pairs={{0,1},{1,2},{2,3},{4,5},{5,6},{6,7},{8,9},{9,10},{10,11},{12,13},{... | collective-permute-start | bytes 122888 | tf_op jit(solution)/shard_map/ppermute | solution.py:292
  12.0 0.0 collective-permute-done.1
  12.0 1.1 %collective-permute-done = bf16[1,32,640]{2,1,0:T(8,128)(2,1)S(1)} collective-permute-done((bf16[1,32,640]{2,1,0:T(8,128)(2,1)S(1)}, bf16[1,32,640]{2,1,0:T(8,128)(2,1)S(1)}, u32[]{:S(2)}, u32[]{:S(2)}) %collective-permute-start) | collective-permute-done | bytes 40992 | tf_op jit(solution)/shard_map/ppermute | solution.py:292
  13.1 5.8 %outer.1 = (bf16[256,640]{1,0:T(8,128)(2,1)S(1)}, bf16[256,640]{1,0:T(8,128)(2,1)S(1)}) custom-call(bf16[512,640]{1,0:T(8,128)(2,1)S(1)} %bitcast.10, bf16[32,640]{1,0:T(8,128)(2,1)S(1)} %bitcast.12, bf16[32,640]{1,0:T(8,128)(2,1)S(1)} %bitcast.11, bf16[3,1920,640]{2,1,0:T(8,128)(2,1)S(1)} %get-tuple-element.29.weight, bf16[640]{0:T(1024)(128)(2,1)S(1)} %copy-done.4, ...), custom_call_target="tpu_custom_call" | custom-call | flops 1 | bytes 1 | tf_op jit(solution)/shard_map/outer/pallas_call | solution.py:155
  18.9 0.0 collective-permute-done.5
  18.9 0.0 collective-permute-done.4
  18.9 0.1 add.18
  19.0 0.7 collective-permute-start.6
  19.7 0.7 collective-permute-start.3
  20.4 0.7 collective-permute-start.2
  21.1 0.0 collective-permute-done.6
  21.1 0.1 add_select_fusion.1
  21.2 1.3 %collective-permute-start.9 = (bf16[256,640]{1,0:T(8,128)(2,1)S(1)}, bf16[256,640]{1,0:T(8,128)(2,1)S(1)}, u32[]{:S(2)}, u32[]{:S(2)}) collective-permute-start(bf16[256,640]{1,0:T(8,128)(2,1)S(1)} %add_select_fusion.1), channel_id=1, source_target_pairs={{8,12},{10,14},{13,9},{15,11},{16,20},{18,22},{21,17},{23,19},{24,... | collective-permute-start | bytes 983048 | tf_op jit(solution)/shard_map/ppermute | solution.py:300
  22.5 0.0 collective-permute-done.3
  22.5 0.0 collective-permute-done.2
  22.5 0.1 add.20
  22.6 0.0 copy-start.2
  22.6 0.8 %collective-permute-start.7 = (bf16[256,640]{1,0:T(8,128)(2,1)S(1)}, bf16[256,640]{1,0:T(8,128)(2,1)S(1)}, u32[]{:S(2)}, u32[]{:S(2)}) collective-permute-start(bf16[256,640]{1,0:T(8,128)(2,1)S(1)} %add.20), channel_id=1, source_target_pairs={{16,24},{21,29},{18,26},{23,31}} | collective-permute-start | bytes 983048 | tf_op jit(solution)/shard_map/ppermute | solution.py:300
  23.4 13.6 %collective-permute-done.9 = bf16[256,640]{1,0:T(8,128)(2,1)S(1)} collective-permute-done((bf16[256,640]{1,0:T(8,128)(2,1)S(1)}, bf16[256,640]{1,0:T(8,128)(2,1)S(1)}, u32[]{:S(2)}, u32[]{:S(2)}) %collective-permute-start.9) | collective-permute-done | bytes 327712 | tf_op jit(solution)/shard_map/ppermute | solution.py:300
  37.0 0.1 add.22.refs_0_
  37.1 0.0 copy-start
  37.1 1.3 %collective-permute-start.13 = (bf16[256,640]{1,0:T(8,128)(2,1)S(1)}, bf16[256,640]{1,0:T(8,128)(2,1)S(1)}, u32[]{:S(2)}, u32[]{:S(2)}) collective-permute-start(bf16[256,640]{1,0:T(8,128)(2,1)S(1)} %add.22.refs_0_), channel_id=1, source_target_pairs={{0,2},{1,3},{2,0},{3,1},{4,6},{5,7},{6,4},{7,5},{8,10},{9,11},{10,... | collective-permute-start | bytes 983048 | tf_op jit(solution)/shard_map/ppermute | solution.py:300
  38.3 1.0 %collective-permute-start.10 = (bf16[256,640]{1,0:T(8,128)(2,1)S(1)}, bf16[256,640]{1,0:T(8,128)(2,1)S(1)}, u32[]{:S(2)}, u32[]{:S(2)}) collective-permute-start(bf16[256,640]{1,0:T(8,128)(2,1)S(1)} %add.22.refs_0_), channel_id=1, source_target_pairs={{0,1},{1,0},{2,3},{3,2},{4,5},{5,4},{6,7},{7,6},{8,9},{9,8},{10,11... | collective-permute-start | bytes 983048 | tf_op jit(solution)/shard_map/ppermute | solution.py:300
  39.3 0.0 collective-permute-done.7
  39.3 0.1 add_select_fusion
  39.4 1.5 %collective-permute-start.8 = (bf16[256,640]{1,0:T(8,128)(2,1)S(1)}, bf16[256,640]{1,0:T(8,128)(2,1)S(1)}, u32[]{:S(2)}, u32[]{:S(2)}) collective-permute-start(bf16[256,640]{1,0:T(8,128)(2,1)S(1)} %add_select_fusion), channel_id=1, source_target_pairs={{8,12},{10,14},{13,9},{15,11},{16,20},{18,22},{21,17},{23,19},{24,... | collective-permute-start | bytes 983048 | tf_op jit(solution)/shard_map/ppermute | solution.py:300
  40.9 0.8 ask.1
  41.6 0.0 collective-permute-done.10.refs_1_
  41.7 4.8 %attend.3 = (f32[512,640]{1,0:T(8,128)S(1)}, f32[512,640]{1,0:T(8,128)S(1)}, f32[512,640]{1,0:T(8,128)S(1)}) custom-call(bf16[512,640]{1,0:T(8,128)(2,1)S(1)} %get-tuple-element.33.queries_ref, bf16[640,1280]{1,0:T(8,128)(2,1)S(1)} %copy-done, bf16[256,640]{1,0:T(8,128)(2,1)S(1)} %add.22.refs_0_, bf16[256,640]{1,0:T(8,128)(2,1)S(1)} %collective-permute-done.10.refs_1_), custom_call_target="tpu_custom_call" | custom-call | flops 1 | bytes 1 | tf_op jit(solution)/shard_map/attend/pallas_call | solution.py:269
  46.5 0.0 collective-permute-done.13.refs_0_
  46.5 9.1 %collective-permute-start.14 = (bf16[256,640]{1,0:T(8,128)(2,1)S(1)}, bf16[256,640]{1,0:T(8,128)(2,1)S(1)}, u32[]{:S(2)}, u32[]{:S(2)}) collective-permute-start(bf16[256,640]{1,0:T(8,128)(2,1)S(1)} %collective-permute-done.13.refs_0_), channel_id=1, source_target_pairs={{0,1},{1,0},{2,3},{3,2},{4,5},{5,4},{6,7},{7,6},{8,9},{9,8},{10,11... | collective-permute-start | bytes 983048 | tf_op jit(solution)/shard_map/ppermute | solution.py:300
  55.6 0.0 collective-permute-done.8
  55.6 0.1 add.23.refs_0_
  55.6 0.1 collective-permute-start.12
  55.7 1.3 %collective-permute-start.11 = (bf16[256,640]{1,0:T(8,128)(2,1)S(1)}, bf16[256,640]{1,0:T(8,128)(2,1)S(1)}, u32[]{:S(2)}, u32[]{:S(2)}) collective-permute-start(bf16[256,640]{1,0:T(8,128)(2,1)S(1)} %add.23.refs_0_), channel_id=1, source_target_pairs={{0,2},{1,3},{2,0},{3,1},{4,6},{5,7},{6,4},{7,5},{8,10},{9,11},{10,... | collective-permute-start | bytes 983048 | tf_op jit(solution)/shard_map/ppermute | solution.py:300
  57.0 0.0 collective-permute-done.14.refs_1_
  57.0 4.8 %attend.4 = (f32[512,640]{1,0:T(8,128)S(1)}, f32[512,640]{1,0:T(8,128)S(1)}, f32[512,640]{1,0:T(8,128)S(1)}) custom-call(bf16[512,640]{1,0:T(8,128)(2,1)S(1)} %get-tuple-element.33.queries_ref, bf16[640,1280]{1,0:T(8,128)(2,1)S(1)} %copy-done, bf16[256,640]{1,0:T(8,128)(2,1)S(1)} %collective-permute-done.13.refs_0_, ...), custom_call_target="tpu_custom_call" | custom-call | flops 1 | bytes 1 | tf_op jit(solution)/shard_map/attend/pallas_call | solution.py:269
  61.8 0.0 copy-start.3
  61.8 5.0 %attend.5 = (f32[512,640]{1,0:T(8,128)S(1)}, f32[512,640]{1,0:T(8,128)S(1)}, f32[512,640]{1,0:T(8,128)S(1)}) custom-call(bf16[512,640]{1,0:T(8,128)(2,1)S(1)} %get-tuple-element.33.queries_ref, bf16[640,1280]{1,0:T(8,128)(2,1)S(1)} %copy-done, bf16[256,640]{1,0:T(8,128)(2,1)S(1)} %add.23.refs_0_, bf16[256,640]{1,0:T(8,128)(2,1)S(1)} %collective-permute-done.12.refs_1_), custom_call_target="tpu_custom_call" | custom-call | flops 1 | bytes 1 | tf_op jit(solution)/shard_map/attend/pallas_call | solution.py:269
  66.9 0.8 collective-permute-start.15
  67.6 1.3 %collective-permute-done.15.refs_1_ = bf16[256,640]{1,0:T(8,128)(2,1)S(1)} collective-permute-done((bf16[256,640]{1,0:T(8,128)(2,1)S(1)}, bf16[256,640]{1,0:T(8,128)(2,1)S(1)}, u32[]{:S(2)}, u32[]{:S(2)}) %collective-permute-start.15) | collective-permute-done | bytes 327712 | tf_op jit(solution)/shard_map/ppermute | solution.py:300
  68.9 8.8 %join.1 = bf16[512,640]{1,0:T(8,128)(2,1)} custom-call(bf16[512,640]{1,0:T(8,128)(2,1)S(1)} %get-tuple-element.33.queries_ref, bf16[640,1280]{1,0:T(8,128)(2,1)} %keyval_hbm.7, bf16[256,640]{1,0:T(8,128)(2,1)S(1)} %collective-permute-done.11.refs_0_, bf16[256,640]{1,0:T(8,128)(2,1)S(1)} %collective-permute-done.15.refs_1_, ...), custom_call_target="tpu_custom_call" | custom-call | flops 1 | bytes 1 | tf_op jit(solution)/shard_map/join/pallas_call | solution.py:269
  (8 shorter events, 0.0 us)
Async XLA Ops:
  0.0 1.1 %copy-start.1 = (bf16[1,16,32,640]{3,2,1,0:T(8,128)(2,1)S(1)}, bf16[1,16,32,640]{3,2,1,0:T(8,128)(2,1)}, u32[]{:S(2)}) copy-start(bf16[1,16,32,640]{3,2,1,0:T(8,128)(2,1)} %param.6) | copy-start | bytes 1966084
  1.1 0.7 copy-start.4
  5.0 13.9 %collective-permute-start.5 = (bf16[256,640]{1,0:T(8,128)(2,1)S(1)}, bf16[256,640]{1,0:T(8,128)(2,1)S(1)}, u32[]{:S(2)}, u32[]{:S(2)}) collective-permute-start(bf16[256,640]{1,0:T(8,128)(2,1)S(1)} %get-tuple-element.30.first_ref), channel_id=1, source_target_pairs={{0,8},{1,13},{2,10},{3,15}} | collective-permute-start | bytes 983048 | tf_op jit(solution)/shard_map/ppermute | solution.py:300
  5.7 13.2 %collective-permute-start.4 = (bf16[256,640]{1,0:T(8,128)(2,1)S(1)}, bf16[256,640]{1,0:T(8,128)(2,1)S(1)}, u32[]{:S(2)}, u32[]{:S(2)}) collective-permute-start(bf16[256,640]{1,0:T(8,128)(2,1)S(1)} %get-tuple-element.30.first_ref), channel_id=1, source_target_pairs={{0,16},{1,21},{2,18},{3,23}} | collective-permute-start | bytes 983048 | tf_op jit(solution)/shard_map/ppermute | solution.py:300
  6.4 5.6 %collective-permute-start.1 = (bf16[1,32,640]{2,1,0:T(8,128)(2,1)S(1)}, bf16[1,32,640]{2,1,0:T(8,128)(2,1)S(1)}, u32[]{:S(2)}, u32[]{:S(2)}) collective-permute-start(bf16[1,32,640]{2,1,0:T(8,128)(2,1)S(1)} %get-tuple-element.53), channel_id=1, source_target_pairs={{1,0},{2,1},{3,2},{5,4},{6,5},{7,6},{9,8},{10,9},{11,10},{13,12},{... | collective-permute-start | bytes 122888 | tf_op jit(solution)/shard_map/ppermute | solution.py:293
  9.0 4.1 %collective-permute-start = (bf16[1,32,640]{2,1,0:T(8,128)(2,1)S(1)}, bf16[1,32,640]{2,1,0:T(8,128)(2,1)S(1)}, u32[]{:S(2)}, u32[]{:S(2)}) collective-permute-start(bf16[1,32,640]{2,1,0:T(8,128)(2,1)S(1)} %get-tuple-element.54), channel_id=1, source_target_pairs={{0,1},{1,2},{2,3},{4,5},{5,6},{6,7},{8,9},{9,10},{10,11},{12,13},{... | collective-permute-start | bytes 122888 | tf_op jit(solution)/shard_map/ppermute | solution.py:292
  19.0 2.1 %collective-permute-start.6 = (bf16[256,640]{1,0:T(8,128)(2,1)S(1)}, bf16[256,640]{1,0:T(8,128)(2,1)S(1)}, u32[]{:S(2)}, u32[]{:S(2)}) collective-permute-start(bf16[256,640]{1,0:T(8,128)(2,1)S(1)} %add.18), channel_id=1, source_target_pairs={{16,24},{21,29},{18,26},{23,31}} | collective-permute-start | bytes 983048 | tf_op jit(solution)/shard_map/ppermute | solution.py:300
  19.7 2.8 %collective-permute-start.3 = (bf16[256,640]{1,0:T(8,128)(2,1)S(1)}, bf16[256,640]{1,0:T(8,128)(2,1)S(1)}, u32[]{:S(2)}, u32[]{:S(2)}) collective-permute-start(bf16[256,640]{1,0:T(8,128)(2,1)S(1)} %get-tuple-element.31.refs_0_), channel_id=1, source_target_pairs={{0,8},{1,13},{2,10},{3,15}} | collective-permute-start | bytes 983048 | tf_op jit(solution)/shard_map/ppermute | solution.py:300
  20.4 2.1 %collective-permute-start.2 = (bf16[256,640]{1,0:T(8,128)(2,1)S(1)}, bf16[256,640]{1,0:T(8,128)(2,1)S(1)}, u32[]{:S(2)}, u32[]{:S(2)}) collective-permute-start(bf16[256,640]{1,0:T(8,128)(2,1)S(1)} %get-tuple-element.31.refs_0_), channel_id=1, source_target_pairs={{0,16},{1,21},{2,18},{3,23}} | collective-permute-start | bytes 983048 | tf_op jit(solution)/shard_map/ppermute | solution.py:300
  21.2 15.8 %collective-permute-start.9 = (bf16[256,640]{1,0:T(8,128)(2,1)S(1)}, bf16[256,640]{1,0:T(8,128)(2,1)S(1)}, u32[]{:S(2)}, u32[]{:S(2)}) collective-permute-start(bf16[256,640]{1,0:T(8,128)(2,1)S(1)} %add_select_fusion.1), channel_id=1, source_target_pairs={{8,12},{10,14},{13,9},{15,11},{16,20},{18,22},{21,17},{23,19},{24,... | collective-permute-start | bytes 983048 | tf_op jit(solution)/shard_map/ppermute | solution.py:300
  22.6 18.3 %copy-start.2 = (bf16[640,640]{1,0:T(8,128)(2,1)S(1)}, bf16[640,640]{1,0:T(8,128)(2,1)}, u32[]{:S(2)}) copy-start(bf16[640,640]{1,0:T(8,128)(2,1)} %refs_2_.1) | copy-start | bytes 2457604
  22.6 16.7 %collective-permute-start.7 = (bf16[256,640]{1,0:T(8,128)(2,1)S(1)}, bf16[256,640]{1,0:T(8,128)(2,1)S(1)}, u32[]{:S(2)}, u32[]{:S(2)}) collective-permute-start(bf16[256,640]{1,0:T(8,128)(2,1)S(1)} %add.20), channel_id=1, source_target_pairs={{16,24},{21,29},{18,26},{23,31}} | collective-permute-start | bytes 983048 | tf_op jit(solution)/shard_map/ppermute | solution.py:300
  37.1 4.6 %copy-start = (bf16[640,1280]{1,0:T(8,128)(2,1)S(1)}, bf16[640,1280]{1,0:T(8,128)(2,1)}, u32[]{:S(2)}) copy-start(bf16[640,1280]{1,0:T(8,128)(2,1)} %keyval_hbm.7) | copy-start | bytes 4915204
  37.1 9.4 %collective-permute-start.13 = (bf16[256,640]{1,0:T(8,128)(2,1)S(1)}, bf16[256,640]{1,0:T(8,128)(2,1)S(1)}, u32[]{:S(2)}, u32[]{:S(2)}) collective-permute-start(bf16[256,640]{1,0:T(8,128)(2,1)S(1)} %add.22.refs_0_), channel_id=1, source_target_pairs={{0,2},{1,3},{2,0},{3,1},{4,6},{5,7},{6,4},{7,5},{8,10},{9,11},{10,... | collective-permute-start | bytes 983048 | tf_op jit(solution)/shard_map/ppermute | solution.py:300
  38.3 3.3 %collective-permute-start.10 = (bf16[256,640]{1,0:T(8,128)(2,1)S(1)}, bf16[256,640]{1,0:T(8,128)(2,1)S(1)}, u32[]{:S(2)}, u32[]{:S(2)}) collective-permute-start(bf16[256,640]{1,0:T(8,128)(2,1)S(1)} %add.22.refs_0_), channel_id=1, source_target_pairs={{0,1},{1,0},{2,3},{3,2},{4,5},{5,4},{6,7},{7,6},{8,9},{9,8},{10,11... | collective-permute-start | bytes 983048 | tf_op jit(solution)/shard_map/ppermute | solution.py:300
  39.4 16.2 %collective-permute-start.8 = (bf16[256,640]{1,0:T(8,128)(2,1)S(1)}, bf16[256,640]{1,0:T(8,128)(2,1)S(1)}, u32[]{:S(2)}, u32[]{:S(2)}) collective-permute-start(bf16[256,640]{1,0:T(8,128)(2,1)S(1)} %add_select_fusion), channel_id=1, source_target_pairs={{8,12},{10,14},{13,9},{15,11},{16,20},{18,22},{21,17},{23,19},{24,... | collective-permute-start | bytes 983048 | tf_op jit(solution)/shard_map/ppermute | solution.py:300
  46.5 10.5 %collective-permute-start.14 = (bf16[256,640]{1,0:T(8,128)(2,1)S(1)}, bf16[256,640]{1,0:T(8,128)(2,1)S(1)}, u32[]{:S(2)}, u32[]{:S(2)}) collective-permute-start(bf16[256,640]{1,0:T(8,128)(2,1)S(1)} %collective-permute-done.13.refs_0_), channel_id=1, source_target_pairs={{0,1},{1,0},{2,3},{3,2},{4,5},{5,4},{6,7},{7,6},{8,9},{9,8},{10,11... | collective-permute-start | bytes 983048 | tf_op jit(solution)/shard_map/ppermute | solution.py:300
  55.6 6.2 %collective-permute-start.12 = (bf16[256,640]{1,0:T(8,128)(2,1)S(1)}, bf16[256,640]{1,0:T(8,128)(2,1)S(1)}, u32[]{:S(2)}, u32[]{:S(2)}) collective-permute-start(bf16[256,640]{1,0:T(8,128)(2,1)S(1)} %add.23.refs_0_), channel_id=1, source_target_pairs={{0,1},{1,0},{2,3},{3,2},{4,5},{5,4},{6,7},{7,6},{8,9},{9,8},{10,11... | collective-permute-start | bytes 983048 | tf_op jit(solution)/shard_map/ppermute | solution.py:300
  55.7 11.1 %collective-permute-start.11 = (bf16[256,640]{1,0:T(8,128)(2,1)S(1)}, bf16[256,640]{1,0:T(8,128)(2,1)S(1)}, u32[]{:S(2)}, u32[]{:S(2)}) collective-permute-start(bf16[256,640]{1,0:T(8,128)(2,1)S(1)} %add.23.refs_0_), channel_id=1, source_target_pairs={{0,2},{1,3},{2,0},{3,1},{4,6},{5,7},{6,4},{7,5},{8,10},{9,11},{10,... | collective-permute-start | bytes 983048 | tf_op jit(solution)/shard_map/ppermute | solution.py:300
  61.8 7.1 %copy-start.3 = (bf16[640,640]{1,0:T(8,128)(2,1)S(1)}, bf16[640,640]{1,0:T(8,128)(2,1)}, u32[]{:S(2)}) copy-start(bf16[640,640]{1,0:T(8,128)(2,1)} %refs_12_.1) | copy-start | bytes 2457604
  66.9 2.0 %collective-permute-start.15 = (bf16[256,640]{1,0:T(8,128)(2,1)S(1)}, bf16[256,640]{1,0:T(8,128)(2,1)S(1)}, u32[]{:S(2)}, u32[]{:S(2)}) collective-permute-start(bf16[256,640]{1,0:T(8,128)(2,1)S(1)} %collective-permute-done.11.refs_0_), channel_id=1, source_target_pairs={{0,1},{1,0},{2,3},{3,2},{4,5},{5,4},{6,7},{7,6},{8,9},{9,8},{10,11... | collective-permute-start | bytes 983048 | tf_op jit(solution)/shard_map/ppermute | solution.py:300

commit v4 on v3

v4 whole, which is shorter than its diff:
```python
import functools

import jax
import jax.numpy as jnp
from jax import lax
from jax.experimental import pallas as pl
from jax.experimental.pallas import tpu as pltpu
from jax.sharding import PartitionSpec as P

HEAD_DIM = 64
PAIR = 2 * HEAD_DIM
VMEM_BYTES = 40 * 2**20
CONV_VMEM_BYTES = 28 * 2**20
IN_VMEM = pl.BlockSpec(memory_space=pltpu.VMEM)
IN_PLACE = pl.BlockSpec(memory_space=pl.ANY)
IN_HBM = pl.BlockSpec(memory_space=pltpu.HBM)
SHIFTS = (1, 0, 2)
QUICK = pl.CostEstimate(flops=1, bytes_accessed=1, transcendentals=0)


def conv_span(width, spans, x_ref, low_ref, high_ref, weight, bias_ref, taps, waits=None):
    tokens, channels = x_ref.shape
    last_row = tokens // width
    blocks, starts, place = [], [], 0
    for first, count in spans:
        begin, end = max(first - 1, 0), min(first + count + 1, last_row)
        starts.append(place)
        if first == 0:
            blocks.append(low_ref[...])
        blocks.append(x_ref[begin * width : end * width, :])
        if first + count == last_row:
            blocks.append(high_ref[...])
        place += count + 2
    padded = place * width
    raw = (blocks[0] if len(blocks) == 1 else jnp.concatenate(blocks, axis=0)).astype(jnp.float32)
    active = raw * jax.nn.sigmoid(raw)
    column = lax.rem(lax.broadcasted_iota(jnp.int32, (padded, 1), 0), width)
    before = jnp.where(column == 0, 0.0, pltpu.roll(active, 1, 0))
    after = jnp.where(column == width - 1, 0.0, pltpu.roll(active, padded - 1, 0))
    taps[:padded, :channels] = before.astype(jnp.bfloat16)
    taps[:padded, channels : 2 * channels] = active.astype(jnp.bfloat16)
    taps[:padded, 2 * channels :] = after.astype(jnp.bfloat16)

    def joined(parts):
        return parts[0] if len(parts) == 1 else jnp.concatenate(parts, axis=0)

    own = joined([x_ref[first * width : (first + count) * width, :] for first, count in spans])
    total = own.astype(jnp.float32) + bias_ref[...].astype(jnp.float32)[None, :]
    for shift in SHIFTS:
        if waits:
            waits[shift].wait()
        rows = joined(
            [
                taps[(start + shift) * width : (start + shift + count) * width, :]
                for start, (_, count) in zip(starts, spans)
            ]
        )
        total = total + jnp.dot(rows, weight[shift], preferred_element_type=jnp.float32)
    return total.astype(jnp.bfloat16)


def inner_kernel(
    width, spans, x_hbm, weight_hbm, bias_hbm, out_ref, x_ref, top_ref, bottom_ref, weight, bias_ref, taps, sems
):
    x_copy = pltpu.make_async_copy(x_hbm, x_ref, sems.at[3])
    bias_copy = pltpu.make_async_copy(bias_hbm, bias_ref, sems.at[4])
    copies = [
        pltpu.make_async_copy(weight_hbm.at[shift], weight.at[shift], sems.at[shift])
        for shift in range(3)
    ]
    is_source = lax.axis_index("frame") == 0
    x_copy.start()

    @pl.when(is_source)
    def _():
        bias_copy.start()
        for shift in SHIFTS:
            copies[shift].start()

    x_copy.wait()
    top_ref[...] = x_ref[:width, :]
    bottom_ref[...] = x_ref[x_ref.shape[0] - width :, :]

    @pl.when(is_source)
    def _():
        bias_copy.wait()
        out_ref[...] = conv_span(width, spans, x_ref, None, None, weight, bias_ref, taps, copies)


def outer_kernel(
    width, outer, x_ref, low_ref, high_ref, weight, bias_ref, out_ref, taps
):
    def compute(spans):
        return conv_span(width, spans, x_ref, low_ref, high_ref, weight, bias_ref, taps)

    @pl.when(lax.axis_index("frame") == 0)
    def _():
        out_ref[...] = compute(outer)


def convolve_inner(x, taps_weight, bias, width, inner):
    channels = x.shape[1]
    made = sum(count for _, count in inner)
    part = jax.ShapeDtypeStruct((width, channels), jnp.bfloat16)
    return pl.pallas_call(
        functools.partial(inner_kernel, width, inner),
        out_shape=(
            jax.ShapeDtypeStruct((made * width, channels), jnp.bfloat16),
            pltpu.VMEM(x.shape, jnp.bfloat16),
            part,
            part,
            pltpu.VMEM(taps_weight.shape, jnp.bfloat16),
            pltpu.VMEM(bias.shape, jnp.bfloat16),
        ),
        in_specs=[IN_HBM] * 3,
        out_specs=(IN_VMEM,) * 6,
        scratch_shapes=[
            pltpu.VMEM(((made + 2 * len(inner)) * width, 3 * channels), jnp.bfloat16),
            pltpu.SemaphoreType.DMA((5,)),
        ],
        compiler_params=pltpu.CompilerParams(vmem_limit_bytes=CONV_VMEM_BYTES),
        cost_estimate=QUICK,
        name="inner",
    )(*(pltpu.with_memory_space_constraint(each, pltpu.HBM) for each in (x, taps_weight, bias)))


def padded_rows(*many):
    return max(sum(count + 2 for _, count in spans) for spans in many)


def convolve_outer(x, low, high, weight, bias, width, outer):
    channels = x.shape[1]
    made = sum(count for _, count in outer)
    return pl.pallas_call(
        functools.partial(outer_kernel, width, outer),
        out_shape=jax.ShapeDtypeStruct((made * width, channels), jnp.bfloat16),
        in_specs=[IN_VMEM] * 5,
        out_specs=IN_VMEM,
        scratch_shapes=[pltpu.VMEM((padded_rows(outer) * width, 3 * channels), jnp.bfloat16)],
        compiler_params=pltpu.CompilerParams(vmem_limit_bytes=CONV_VMEM_BYTES),
        cost_estimate=QUICK,
        name="outer",
    )(x, low, high, *(pltpu.with_memory_space_constraint(each, pltpu.VMEM) for each in (weight, bias)))


def ask_kernel(
    width, spans, layout, w_query, x_ref, low_ref, high_ref, weight, bias_ref, *refs
):
    pieces, (hidden_ref, queries_ref, taps) = refs[:-3], refs[-3:]

    def lay(values):
        for value, spots in zip(values, layout):
            taken = 0
            for start, size in spots:
                hidden_ref[start : start + size, :] = value[taken : taken + size, :]
                taken += size

    def compute():
        for each, spots in zip(spans, layout):
            lay_one = conv_span(width, each, x_ref, low_ref, high_ref, weight, bias_ref, taps)
            taken = 0
            for start, size in spots:
                hidden_ref[start : start + size, :] = lay_one[taken : taken + size]
                taken += size

    if pieces:
        pl.when(lax.axis_index("frame") == 0)(lambda: lay(pieces))
        pl.when(lax.axis_index("frame") != 0)(compute)
    else:
        compute()
    queries = jnp.dot(hidden_ref[...], w_query[...], preferred_element_type=jnp.float32)
    queries_ref[...] = queries.astype(jnp.bfloat16)


def ask(pieces, x, low, high, weight, bias, w_query, width, spans, layout):
    channels = x.shape[1]
    whole = jax.ShapeDtypeStruct(x.shape, jnp.bfloat16)
    return pl.pallas_call(
        functools.partial(ask_kernel, width, spans, layout),
        out_shape=(whole, whole),
        in_specs=[IN_VMEM] * (len(pieces) + 6),
        out_specs=(IN_VMEM, IN_VMEM),
        scratch_shapes=[pltpu.VMEM((padded_rows(*spans) * width, 3 * channels), jnp.bfloat16)],
        compiler_params=pltpu.CompilerParams(vmem_limit_bytes=CONV_VMEM_BYTES),
        cost_estimate=QUICK,
        name="ask",
    )(w_query, x, low, high, weight, bias, *pieces)


def attend_kernel(piece_count, part_count, last, queries_ref, keyval_hbm, *refs):
    refs = list(refs)
    pieces = [refs.pop(0) for _ in range(piece_count)]
    parts = [[refs.pop(0) for _ in range(3)] for _ in range(part_count)]
    ending = [refs.pop(0) for _ in range(2)] if last else None
    new = [refs.pop(0) for _ in range(1 if last else 3)]
    w_keyval, w_out, keys, values, mixed, sems = refs
    tokens, channels = queries_ref.shape
    keyval_copy = pltpu.make_async_copy(keyval_hbm, w_keyval, sems.at[0])
    keyval_copy.start()
    if last:
        out_copy = pltpu.make_async_copy(ending[1], w_out, sems.at[1])
        out_copy.start()
    keyval_copy.wait()
    key_count = 0
    for piece in pieces:
        spot = slice(key_count, key_count + piece.shape[0])
        keyval = jnp.dot(piece[...], w_keyval[...], preferred_element_type=jnp.float32)
        keyval = keyval.astype(jnp.bfloat16)
        keys[spot, :] = keyval[:, :channels]
        values[spot, :] = keyval[:, channels:]
        key_count = spot.stop
    is_low = lax.broadcasted_iota(jnp.int32, (tokens, PAIR), 1) < HEAD_DIM
    ones = jnp.ones((key_count, PAIR), jnp.bfloat16)
    for start in range(0, channels, PAIR):
        lanes = slice(start, start + PAIR)
        both = queries_ref[:, lanes] * HEAD_DIM ** (-0.5)
        nothing = jnp.zeros_like(both)
        split = jnp.concatenate(
            [jnp.where(is_low, both, nothing), jnp.where(is_low, nothing, both)], axis=0
        )
        scores = lax.dot_general(
            split, keys[:, lanes], (((1,), (1,)), ((), ())), preferred_element_type=jnp.float32
        )
        best = jnp.max(scores, axis=1, keepdims=True)
        probability = jnp.exp(scores - best).astype(jnp.bfloat16)
        product = jnp.dot(
            probability,
            jnp.concatenate([values[:, lanes], ones], axis=1),
            preferred_element_type=jnp.float32,
        )
        best = jnp.where(is_low, best[:tokens], best[tokens:])
        weighted = jnp.where(is_low, product[:tokens, :PAIR], product[tokens:, :PAIR])
        total = jnp.where(is_low, product[:tokens, PAIR:], product[tokens:, PAIR:])
        if last:
            top = functools.reduce(jnp.maximum, [part[2][:, lanes] for part in parts], best)
            scale = jnp.exp(best - top)
            weighted, total = weighted * scale, total * scale
            for part in parts:
                scale = jnp.exp(part[2][:, lanes] - top)
                weighted = weighted + part[0][:, lanes] * scale
                total = total + part[1][:, lanes] * scale
            mixed[:, lanes] = (weighted / total).astype(jnp.bfloat16)
        else:
            new[0][:, lanes] = weighted
            new[1][:, lanes] = total
            new[2][:, lanes] = best
    if last:
        out_copy.wait()
        result = ending[0][...].astype(jnp.float32) + jnp.dot(
            mixed[...], w_out[...], preferred_element_type=jnp.float32
        )
        new[0][...] = result.astype(jnp.bfloat16)


def attend(queries, w_keyval, pieces, parts, ending, name):
    tokens, channels = queries.shape
    key_count = sum(piece.shape[0] for piece in pieces)
    last = ending is not None
    part = jax.ShapeDtypeStruct((tokens, channels), jnp.float32)
    whole = jax.ShapeDtypeStruct((tokens, channels), jnp.bfloat16)
    args = [queries, w_keyval, *pieces, *(array for each in parts for array in each), *(ending or ())]
    in_specs = [IN_VMEM] * len(args)
    in_specs[1] = IN_PLACE
    if last:
        in_specs[-1] = IN_PLACE
    return pl.pallas_call(
        functools.partial(attend_kernel, len(pieces), len(parts), last),
        out_shape=whole if last else (part,) * 3,
        in_specs=in_specs,
        out_specs=IN_VMEM if last else (IN_VMEM,) * 3,
        scratch_shapes=[
            pltpu.VMEM(w_keyval.shape, jnp.bfloat16),
            pltpu.VMEM((channels, channels), jnp.bfloat16),
            pltpu.VMEM((key_count, channels), jnp.bfloat16),
            pltpu.VMEM((key_count, channels), jnp.bfloat16),
            pltpu.VMEM((tokens, channels), jnp.bfloat16),
            pltpu.SemaphoreType.DMA((2,)),
        ],
        compiler_params=pltpu.CompilerParams(vmem_limit_bytes=VMEM_BYTES),
        cost_estimate=QUICK,
        name=name,
    )(*args)


def from_edges(top, bottom):
    count = lax.axis_size("band")
    forward = [(i, i + 1) for i in range(count - 1)]
    backward = [(target, source) for source, target in forward]
    return lax.ppermute(bottom, "band", forward), lax.ppermute(top, "band", backward)


def permute(value, pairs):
    bands = lax.axis_size("band")
    flat = [(source[0] * bands + source[1], target[0] * bands + target[1]) for source, target in pairs]
    return lax.ppermute(value, ("frame", "band"), flat)


def ordered(value, *before):
    return lax.optimization_barrier((value, *before))[0]


def step_across(own, is_source, before=()):
    pairs = [((0, b), (1, b)) for b in range(lax.axis_size("band")) if b % 2]
    if lax.axis_size("frame") == 1:
        return own
    return jnp.where(is_source, own, ordered(permute(own, pairs), *before))


def cast(roots, before=()):
    frames, bands = lax.axis_size("frame"), lax.axis_size("band")
    places = frames // 2
    held, reach = list(roots), places
    while reach > 1:
        reach //= 2
        pairs = [
            ((2 * i + b % 2, b), (2 * (i + reach) + b % 2, b))
            for i in range(0, places, 2 * reach)
            for b in range(bands)
        ]
        arrived = [permute(each, pairs) for each in held]
        if before:
            arrived[0] = ordered(arrived[0], *before)
        held = [have + new for have, new in zip(held, arrived)]
        before = ()
    return held


def exchange(held):
    frames, bands = lax.axis_size("frame"), lax.axis_size("band")
    holders = [(f, b) for f in range(frames) for b in range(bands) if f % 2 == b % 2]
    beside = permute(held, [((f, b), (f ^ 1, b)) for f, b in holders if f != 1])
    far = permute(
        held,
        [((f, b), (f, b ^ 2)) for f, b in holders] + [((0, b), (0, b ^ 2)) for b in range(bands) if b % 2],
    )
    diagonal = permute(held, [((f, b), (f ^ 1, b ^ 2)) for f, b in holders if f != 1])
    return beside, far, diagonal


def swap_cores(value):
    frames, bands = lax.axis_size("frame"), lax.axis_size("band")
    return permute(value, [((f, b), (f, b ^ 1)) for f in range(frames) for b in range(bands)])


def own_side(held, parts):
    beside, far, diagonal = parts
    return [held + beside, far + diagonal]


def sees_all(chunks, starts, look, early):
    frames, bands = lax.axis_size("frame"), lax.axis_size("band")
    if frames < 2 or frames & (frames - 1) or bands != 4:
        pieces = [lax.all_gather(chunk, ("frame", "band"))[b] for chunk in chunks for b in range(bands)]
        return [], pieces
    held0, held1 = cast(starts, (*early, starts[1]))
    parts0 = exchange(held0)
    held1 = ordered(held1, held0)
    parts1 = exchange(held1)
    here0 = own_side(held0, ordered(parts0, held1))
    there0 = [swap_cores(piece) for piece in here0]
    look0 = look(here0)
    here1 = own_side(held1, ordered(parts1, look0))
    look1 = look(ordered(there0, look0, here1))
    there1 = [swap_cores(piece) for piece in here1]
    look2 = look(ordered(here1, look1))
    return [look0, look1, look2], ordered(there1, look2)


def per_device(latents, conv_weight, conv_bias, w_query, w_keyval, w_out):
    frames, row_count, width, channels = latents.shape
    tokens = row_count * width
    half = row_count // 2
    taps_weight = conv_weight.reshape(3, 3 * channels, channels)
    inner = ((1, half),)
    outer = ((0, 1), (half + 1, row_count - half - 1))
    seam = (half + 1) * width
    layout = (((0, width), (seam, tokens - seam)), ((width, half * width),))
    latents, is_source = lax.optimization_barrier((latents, lax.axis_index("frame") == 0))
    blocks = [latents[frame].reshape(tokens, channels) for frame in range(frames)]
    first, at_hand, top, bottom, *weight_bias = convolve_inner(
        blocks[0], taps_weight, conv_bias, width, inner
    )
    low, high = from_edges(top, bottom)
    begun = step_across(first, is_source, (low, high))
    second = convolve_outer(at_hand, low, high, *weight_bias, width, outer)
    asked = [
        ask((second, first), at_hand, low, high, taps_weight, conv_bias, w_query, width, (outer, inner), layout)
    ]
    for block in blocks[1:]:
        edges = from_edges(block[:width], block[-width:])
        asked.append(ask((), block, *edges, taps_weight, conv_bias, w_query, width, (outer, inner), layout))
    chunks = (first, second)
    starts = (begun, step_across(second, is_source))

    def look(pieces):
        return tuple(attend(queries, w_keyval, pieces, (), None, "attend") for _, queries in asked)

    looks, pieces = sees_all(chunks, starts, look, [queries for _, queries in asked])
    results = [
        attend(queries, w_keyval, pieces, [each[i] for each in looks], (hidden, w_out), "join")
        for i, (hidden, queries) in enumerate(asked)
    ]
    return jnp.stack(results).reshape(latents.shape)


def solution(mesh):
    return jax.shard_map(
        per_device,
        mesh=mesh,
        in_specs=(P("frame", "band", None, None), P(), P(), P(), P(), P()),
        out_specs=P("frame", "band", None, None),
        check_vma=False,
    )
```

time: 78.3 us -> 74 us (0.945)
  the two profiles are of different devices: /device:TPU:25 before, /device:TPU:0 now
where the time goes in v4:
time: 74 us; the launch traced here: 73.6 us
  Pallas kernels  32.1 us (43%)
  starting transfers between devices  26.4 us (36%)
  waiting for transfers between devices  13.8 us (19%)
  other arithmetic  0.75 us (1%)
    pallas_call x4, Pallas kernels, attend(): pl.pallas_call(functools.partial(attend_kernel, len(pieces), len(parts),...  23.5 us
    ppermute x16, starting transfers between devices, permute(): return lax.ppermute(value, ('frame', 'band'), flat)  22.1 us
    ppermute x16, waiting for transfers between devices, permute(): return lax.ppermute(value, ('frame', 'band'), flat)  10.5 us
    pallas_call x1, Pallas kernels, convolve_inner(): pl.pallas_call(functools.partial(inner_kernel, width, inner), out_shape=(...  5.12 us
    ppermute x1, waiting for transfers between devices, from_edges(): lax.ppermute(top, 'band', backward)  3.28 us
    ppermute x1, starting transfers between devices, from_edges(): lax.ppermute(bottom, 'band', forward)  2.98 us
    pallas_call x1, Pallas kernels, convolve_outer(): pl.pallas_call(functools.partial(outer_kernel, width, outer), out_shape=j...  2.74 us
  transfers between devices with their start and end apart: 18, of which 8 were waited for; matrix products, arithmetic and copies ran while one was open for 1% of the time, Pallas kernels for 25%

profile of v4, /device:TPU:0, one launch (start us, length us, event | category | flops | bytes accessed | tf_op | source)
XLA Modules:
  0.0 73.6 jit_solution(2858922579506006196)
XLA Ops:
  0.0 5.1 %inner.1 = (bf16[256,640]{1,0:T(8,128)(2,1)S(1)}, bf16[512,640]{1,0:T(8,128)(2,1)S(1)}, bf16[32,640]{1,0:T(8,128)(2,1)S(1)}, bf16[32,640]{1,0:T(8,128)(2,1)S(1)}...) custom-call(bf16[512,640]{1,0:T(8,128)(2,1)} %bitcast.7, bf16[3,1920,640]{2,1,0:T(8,128)(2,1)} %bitcast.3, ...), custom_call_target="tpu_custom_call" | custom-call | flops 1 | bytes 1 | tf_op jit(solution)/shard_map/inner/pallas_call | solution.py:105
  5.1 0.7 collective-permute-start.5
  5.8 3.0 %collective-permute-start = (bf16[32,640]{1,0:T(8,128)(2,1)S(1)}, bf16[32,640]{1,0:T(8,128)(2,1)S(1)}, u32[]{:S(2)}, u32[]{:S(2)}) collective-permute-start(bf16[32,640]{1,0:T(8,128)(2,1)S(1)} %get-tuple-element.41), channel_id=1, source_target_pairs={{0,1},{1,2},{2,3},{4,5},{5,6},{6,7},{8,9},{9,10},{10,11},{12,13},{... | collective-permute-start | bytes 122888 | tf_op jit(solution)/shard_map/ppermute | solution.py:289
  8.8 1.3 %collective-permute-start.1 = (bf16[32,640]{1,0:T(8,128)(2,1)S(1)}, bf16[32,640]{1,0:T(8,128)(2,1)S(1)}, u32[]{:S(2)}, u32[]{:S(2)}) collective-permute-start(bf16[32,640]{1,0:T(8,128)(2,1)S(1)} %get-tuple-element.42), channel_id=1, source_target_pairs={{1,0},{2,1},{3,2},{5,4},{6,5},{7,6},{9,8},{10,9},{11,10},{13,12},{... | collective-permute-start | bytes 122888 | tf_op jit(solution)/shard_map/ppermute | solution.py:289
  10.1 0.0 collective-permute-done.low_ref
  10.1 3.3 %collective-permute-done.1.high_ref = bf16[32,640]{1,0:T(8,128)(2,1)S(1)} collective-permute-done((bf16[32,640]{1,0:T(8,128)(2,1)S(1)}, bf16[32,640]{1,0:T(8,128)(2,1)S(1)}, u32[]{:S(2)}, u32[]{:S(2)}) %collective-permute-start.1) | collective-permute-done | bytes 40992 | tf_op jit(solution)/shard_map/ppermute | solution.py:289
  13.4 2.7 %outer.1.refs_0_ = bf16[256,640]{1,0:T(8,128)(2,1)S(1)} custom-call(bf16[512,640]{1,0:T(8,128)(2,1)S(1)} %get-tuple-element.40.x_ref, bf16[32,640]{1,0:T(8,128)(2,1)S(1)} %collective-permute-done.low_ref, bf16[32,640]{1,0:T(8,128)(2,1)S(1)} %collective-permute-done.1.high_ref, bf16[3,1920,640]{2,1,0:T(8,128)(2,1)S(1)} %get-tuple-element.43.weight, ...), custom_call_target="tpu_custom_call" | custom-call | flops 1 | bytes 1 | tf_op jit(solution)/shard_map/outer/pallas_call | solution.py:134
  16.2 0.0 copy-start.1
  16.2 0.8 %collective-permute-start.2 = (bf16[256,640]{1,0:T(8,128)(2,1)S(1)}, bf16[256,640]{1,0:T(8,128)(2,1)S(1)}, u32[]{:S(2)}, u32[]{:S(2)}) collective-permute-start(bf16[256,640]{1,0:T(8,128)(2,1)S(1)} %outer.1.refs_0_), channel_id=1, source_target_pairs={{1,5},{3,7}} | collective-permute-start | bytes 983048 | tf_op jit(solution)/shard_map/ppermute | solution.py:295
  17.0 0.1 broadcast_select_fusion
  17.1 1.3 %collective-permute-start.6 = (bf16[256,640]{1,0:T(8,128)(2,1)S(1)}, bf16[256,640]{1,0:T(8,128)(2,1)S(1)}, u32[]{:S(2)}, u32[]{:S(2)}) collective-permute-start(bf16[256,640]{1,0:T(8,128)(2,1)S(1)} %broadcast_select_fusion), channel_id=1, source_target_pairs={{0,16},{5,21},{2,18},{7,23}} | collective-permute-start | bytes 983048 | tf_op jit(solution)/shard_map/ppermute | solution.py:295
  18.4 0.8 %ask.1 = (bf16[512,640]{1,0:T(8,128)(2,1)S(1)}, bf16[512,640]{1,0:T(8,128)(2,1)S(1)}) custom-call(bf16[640,640]{1,0:T(8,128)(2,1)S(1)} %copy-done.1, bf16[512,640]{1,0:T(8,128)(2,1)S(1)} %get-tuple-element.40.x_ref, bf16[32,640]{1,0:T(8,128)(2,1)S(1)} %collective-permute-done.low_ref, bf16[32,640]{1,0:T(8,128)(2,1)S(1)} %collective-permute-done.1.high_ref, ...), custom_call_target="tpu_custom_call" | custom-call | flops 1 | bytes 1 | tf_op jit(solution)/shard_map/ask/pallas_call | solution.py:178
  19.3 3.6 %collective-permute-start.3 = (bf16[256,640]{1,0:T(8,128)(2,1)S(1)}, bf16[256,640]{1,0:T(8,128)(2,1)S(1)}, u32[]{:S(2)}, u32[]{:S(2)}) collective-permute-start(bf16[256,640]{1,0:T(8,128)(2,1)S(1)} %broadcast_select_fusion.1), channel_id=1, source_target_pairs={{0,16},{5,21},{2,18},{7,23}} | collective-permute-start | bytes 983048 | tf_op jit(solution)/shard_map/ppermute | solution.py:295
  22.9 0.1 collective-permute-done.6
  22.9 0.1 add.26
  23.0 1.3 %collective-permute-start.7 = (bf16[256,640]{1,0:T(8,128)(2,1)S(1)}, bf16[256,640]{1,0:T(8,128)(2,1)S(1)}, u32[]{:S(2)}, u32[]{:S(2)}) collective-permute-start(bf16[256,640]{1,0:T(8,128)(2,1)S(1)} %add.26), channel_id=1, source_target_pairs={{0,8},{5,13},{2,10},{7,15},{16,24},{21,29},{18,26},{23,31}} | collective-permute-start | bytes 983048 | tf_op jit(solution)/shard_map/ppermute | solution.py:295
  24.3 3.1 %collective-permute-done.3 = bf16[256,640]{1,0:T(8,128)(2,1)S(1)} collective-permute-done((bf16[256,640]{1,0:T(8,128)(2,1)S(1)}, bf16[256,640]{1,0:T(8,128)(2,1)S(1)}, u32[]{:S(2)}, u32[]{:S(2)}) %collective-permute-start.3) | collective-permute-done | bytes 327712 | tf_op jit(solution)/shard_map/ppermute | solution.py:295
  27.4 0.1 add.24
  27.5 1.3 %collective-permute-start.4 = (bf16[256,640]{1,0:T(8,128)(2,1)S(1)}, bf16[256,640]{1,0:T(8,128)(2,1)S(1)}, u32[]{:S(2)}, u32[]{:S(2)}) collective-permute-start(bf16[256,640]{1,0:T(8,128)(2,1)S(1)} %add.24), channel_id=1, source_target_pairs={{0,8},{5,13},{2,10},{7,15},{16,24},{21,29},{18,26},{23,31}} | collective-permute-start | bytes 983048 | tf_op jit(solution)/shard_map/ppermute | solution.py:295
  28.8 2.1 %collective-permute-done.7 = bf16[256,640]{1,0:T(8,128)(2,1)S(1)} collective-permute-done((bf16[256,640]{1,0:T(8,128)(2,1)S(1)}, bf16[256,640]{1,0:T(8,128)(2,1)S(1)}, u32[]{:S(2)}, u32[]{:S(2)}) %collective-permute-start.7) | collective-permute-done | bytes 327712 | tf_op jit(solution)/shard_map/ppermute | solution.py:295
  30.9 0.1 add.27
  31.0 0.0 copy-start
  31.0 1.4 %collective-permute-start.11 = (bf16[256,640]{1,0:T(8,128)(2,1)S(1)}, bf16[256,640]{1,0:T(8,128)(2,1)S(1)}, u32[]{:S(2)}, u32[]{:S(2)}) collective-permute-start(bf16[256,640]{1,0:T(8,128)(2,1)S(1)} %add.27), channel_id=1, source_target_pairs={{0,4},{2,6},{8,12},{10,14},{13,9},{15,11},{16,20},{18,22},{21,17},... | collective-permute-start | bytes 983048 | tf_op jit(solution)/shard_map/ppermute | solution.py:295
  32.5 4.5 %collective-permute-start.12 = (bf16[256,640]{1,0:T(8,128)(2,1)S(1)}, bf16[256,640]{1,0:T(8,128)(2,1)S(1)}, u32[]{:S(2)}, u32[]{:S(2)}) collective-permute-start(bf16[256,640]{1,0:T(8,128)(2,1)S(1)} %add.27), channel_id=1, source_target_pairs={{0,2},{2,0},{5,7},{7,5},{8,10},{10,8},{13,15},{15,13},{16,18},{18,... | collective-permute-start | bytes 983048 | tf_op jit(solution)/shard_map/ppermute | solution.py:295
  37.0 1.3 %collective-permute-start.13 = (bf16[256,640]{1,0:T(8,128)(2,1)S(1)}, bf16[256,640]{1,0:T(8,128)(2,1)S(1)}, u32[]{:S(2)}, u32[]{:S(2)}) collective-permute-start(bf16[256,640]{1,0:T(8,128)(2,1)S(1)} %add.27), channel_id=1, source_target_pairs={{0,6},{2,4},{8,14},{10,12},{13,11},{15,9},{16,22},{18,20},{21,19},... | collective-permute-start | bytes 983048 | tf_op jit(solution)/shard_map/ppermute | solution.py:295
  38.3 0.0 collective-permute-done.4
  38.3 0.1 add.25
  38.4 1.3 %collective-permute-start.10 = (bf16[256,640]{1,0:T(8,128)(2,1)S(1)}, bf16[256,640]{1,0:T(8,128)(2,1)S(1)}, u32[]{:S(2)}, u32[]{:S(2)}) collective-permute-start(bf16[256,640]{1,0:T(8,128)(2,1)S(1)} %add.25), channel_id=1, source_target_pairs={{0,6},{2,4},{8,14},{10,12},{13,11},{15,9},{16,22},{18,20},{21,19},... | collective-permute-start | bytes 983048 | tf_op jit(solution)/shard_map/ppermute | solution.py:295
  39.7 1.5 %collective-permute-start.8 = (bf16[256,640]{1,0:T(8,128)(2,1)S(1)}, bf16[256,640]{1,0:T(8,128)(2,1)S(1)}, u32[]{:S(2)}, u32[]{:S(2)}) collective-permute-start(bf16[256,640]{1,0:T(8,128)(2,1)S(1)} %add.25), channel_id=1, source_target_pairs={{0,4},{2,6},{8,12},{10,14},{13,9},{15,11},{16,20},{18,22},{21,17},... | collective-permute-start | bytes 983048 | tf_op jit(solution)/shard_map/ppermute | solution.py:295
  41.2 0.0 collective-permute-done.11
  41.2 1.9 %collective-permute-start.9 = (bf16[256,640]{1,0:T(8,128)(2,1)S(1)}, bf16[256,640]{1,0:T(8,128)(2,1)S(1)}, u32[]{:S(2)}, u32[]{:S(2)}) collective-permute-start(bf16[256,640]{1,0:T(8,128)(2,1)S(1)} %add.25), channel_id=1, source_target_pairs={{0,2},{2,0},{5,7},{7,5},{8,10},{10,8},{13,15},{15,13},{16,18},{18,... | collective-permute-start | bytes 983048 | tf_op jit(solution)/shard_map/ppermute | solution.py:295
  43.2 0.2 collective-permute-done.12
  43.4 2.8 %collective-permute-done.13 = bf16[256,640]{1,0:T(8,128)(2,1)S(1)} collective-permute-done((bf16[256,640]{1,0:T(8,128)(2,1)S(1)}, bf16[256,640]{1,0:T(8,128)(2,1)S(1)}, u32[]{:S(2)}, u32[]{:S(2)}) %collective-permute-start.13) | collective-permute-done | bytes 327712 | tf_op jit(solution)/shard_map/ppermute | solution.py:295
  46.2 0.1 add.28.refs_0_
  46.2 0.1 add.29.refs_1_
  46.3 0.1 collective-permute-start.17
  46.4 0.5 collective-permute-start.16
  46.9 4.8 %attend.3 = (f32[512,640]{1,0:T(8,128)S(1)}, f32[512,640]{1,0:T(8,128)S(1)}, f32[512,640]{1,0:T(8,128)S(1)}) custom-call(bf16[512,640]{1,0:T(8,128)(2,1)S(1)} %get-tuple-element.46.queries_ref, bf16[640,1280]{1,0:T(8,128)(2,1)S(1)} %copy-done, bf16[256,640]{1,0:T(8,128)(2,1)S(1)} %add.28.refs_0_, bf16[256,640]{1,0:T(8,128)(2,1)S(1)} %add.29.refs_1_), custom_call_target="tpu_custom_call" | custom-call | flops 1 | bytes 1 | tf_op jit(solution)/shard_map/attend/pallas_call | solution.py:266
  51.7 1.1 %collective-permute-done.8 = bf16[256,640]{1,0:T(8,128)(2,1)S(1)} collective-permute-done((bf16[256,640]{1,0:T(8,128)(2,1)S(1)}, bf16[256,640]{1,0:T(8,128)(2,1)S(1)}, u32[]{:S(2)}, u32[]{:S(2)}) %collective-permute-start.8) | collective-permute-done | bytes 327712 | tf_op jit(solution)/shard_map/ppermute | solution.py:295
  52.8 1.1 %collective-permute-done.9 = bf16[256,640]{1,0:T(8,128)(2,1)S(1)} collective-permute-done((bf16[256,640]{1,0:T(8,128)(2,1)S(1)}, bf16[256,640]{1,0:T(8,128)(2,1)S(1)}, u32[]{:S(2)}, u32[]{:S(2)}) %collective-permute-start.9) | collective-permute-done | bytes 327712 | tf_op jit(solution)/shard_map/ppermute | solution.py:295
  53.9 0.1 add.30.refs_0_
  54.0 0.1 add.31.refs_1_
  54.1 0.1 collective-permute-start.15
  54.2 0.5 collective-permute-start.14
  54.7 4.8 %attend.4 = (f32[512,640]{1,0:T(8,128)S(1)}, f32[512,640]{1,0:T(8,128)S(1)}, f32[512,640]{1,0:T(8,128)S(1)}) custom-call(bf16[512,640]{1,0:T(8,128)(2,1)S(1)} %get-tuple-element.46.queries_ref, bf16[640,1280]{1,0:T(8,128)(2,1)S(1)} %copy-done, bf16[256,640]{1,0:T(8,128)(2,1)S(1)} %collective-permute-done.16.refs_0_, ...), custom_call_target="tpu_custom_call" | custom-call | flops 1 | bytes 1 | tf_op jit(solution)/shard_map/attend/pallas_call | solution.py:266
  59.5 0.0 copy-start.2
  59.5 5.0 %attend.5 = (f32[512,640]{1,0:T(8,128)S(1)}, f32[512,640]{1,0:T(8,128)S(1)}, f32[512,640]{1,0:T(8,128)S(1)}) custom-call(bf16[512,640]{1,0:T(8,128)(2,1)S(1)} %get-tuple-element.46.queries_ref, bf16[640,1280]{1,0:T(8,128)(2,1)S(1)} %copy-done, bf16[256,640]{1,0:T(8,128)(2,1)S(1)} %add.30.refs_0_, bf16[256,640]{1,0:T(8,128)(2,1)S(1)} %add.31.refs_1_), custom_call_target="tpu_custom_call" | custom-call | flops 1 | bytes 1 | tf_op jit(solution)/shard_map/attend/pallas_call | solution.py:266
  64.6 8.8 %join.1 = bf16[512,640]{1,0:T(8,128)(2,1)} custom-call(bf16[512,640]{1,0:T(8,128)(2,1)S(1)} %get-tuple-element.46.queries_ref, bf16[640,1280]{1,0:T(8,128)(2,1)} %keyval_hbm.7, bf16[256,640]{1,0:T(8,128)(2,1)S(1)} %collective-permute-done.14.refs_0_, bf16[256,640]{1,0:T(8,128)(2,1)S(1)} %collective-permute-done.15.refs_1_, ...), custom_call_target="tpu_custom_call" | custom-call | flops 1 | bytes 1 | tf_op jit(solution)/shard_map/join/pallas_call | solution.py:266
  (18 shorter events, 0.1 us)
Async XLA Ops:
  0.0 18.4 %slice-start = ((s8[7372800]{0:T(1024)(128)(4,1)}), s8[4194304]{0:T(1024)(128)(4,1)S(1)}, s32[]{:S(2)}) async-start(s8[7372800]{0:T(1024)(128)(4,1)} %bitcast.4), calls=%async_computation | async-start | bytes 8388608
  5.1 11.9 %collective-permute-start.5 = (bf16[256,640]{1,0:T(8,128)(2,1)S(1)}, bf16[256,640]{1,0:T(8,128)(2,1)S(1)}, u32[]{:S(2)}, u32[]{:S(2)}) collective-permute-start(bf16[256,640]{1,0:T(8,128)(2,1)S(1)} %get-tuple-element.45.refs_1_), channel_id=1, source_target_pairs={{1,5},{3,7}} | collective-permute-start | bytes 983048 | tf_op jit(solution)/shard_map/ppermute | solution.py:295
  5.8 4.3 %collective-permute-start = (bf16[32,640]{1,0:T(8,128)(2,1)S(1)}, bf16[32,640]{1,0:T(8,128)(2,1)S(1)}, u32[]{:S(2)}, u32[]{:S(2)}) collective-permute-start(bf16[32,640]{1,0:T(8,128)(2,1)S(1)} %get-tuple-element.41), channel_id=1, source_target_pairs={{0,1},{1,2},{2,3},{4,5},{5,6},{6,7},{8,9},{9,10},{10,11},{12,13},{... | collective-permute-start | bytes 122888 | tf_op jit(solution)/shard_map/ppermute | solution.py:289
  8.8 4.6 %collective-permute-start.1 = (bf16[32,640]{1,0:T(8,128)(2,1)S(1)}, bf16[32,640]{1,0:T(8,128)(2,1)S(1)}, u32[]{:S(2)}, u32[]{:S(2)}) collective-permute-start(bf16[32,640]{1,0:T(8,128)(2,1)S(1)} %get-tuple-element.42), channel_id=1, source_target_pairs={{1,0},{2,1},{3,2},{5,4},{6,5},{7,6},{9,8},{10,9},{11,10},{13,12},{... | collective-permute-start | bytes 122888 | tf_op jit(solution)/shard_map/ppermute | solution.py:289
  13.4 5.0 %slice-start.1 = ((s8[7372800]{0:T(1024)(128)(4,1)}), s8[3178496]{0:T(1024)(128)(4,1)S(1)}, s32[]{:S(2)}) async-start(s8[7372800]{0:T(1024)(128)(4,1)} %bitcast.4), calls=%async_computation.1 | async-start | bytes 6356992
  13.4 5.0 %copy-start.3 = (bf16[640]{0:T(1024)(128)(2,1)S(1)}, bf16[640]{0:T(1024)(128)(2,1)}, u32[]{:S(2)}) copy-start(bf16[640]{0:T(1024)(128)(2,1)} %bias_ref.1) | copy-start | bytes 3844
  16.2 2.2 %copy-start.1 = (bf16[640,640]{1,0:T(8,128)(2,1)S(1)}, bf16[640,640]{1,0:T(8,128)(2,1)}, u32[]{:S(2)}) copy-start(bf16[640,640]{1,0:T(8,128)(2,1)} %w_query.1) | copy-start | bytes 2457604
  16.2 3.1 %collective-permute-start.2 = (bf16[256,640]{1,0:T(8,128)(2,1)S(1)}, bf16[256,640]{1,0:T(8,128)(2,1)S(1)}, u32[]{:S(2)}, u32[]{:S(2)}) collective-permute-start(bf16[256,640]{1,0:T(8,128)(2,1)S(1)} %outer.1.refs_0_), channel_id=1, source_target_pairs={{1,5},{3,7}} | collective-permute-start | bytes 983048 | tf_op jit(solution)/shard_map/ppermute | solution.py:295
  17.1 5.9 %collective-permute-start.6 = (bf16[256,640]{1,0:T(8,128)(2,1)S(1)}, bf16[256,640]{1,0:T(8,128)(2,1)S(1)}, u32[]{:S(2)}, u32[]{:S(2)}) collective-permute-start(bf16[256,640]{1,0:T(8,128)(2,1)S(1)} %broadcast_select_fusion), channel_id=1, source_target_pairs={{0,16},{5,21},{2,18},{7,23}} | collective-permute-start | bytes 983048 | tf_op jit(solution)/shard_map/ppermute | solution.py:295
  19.3 8.1 %collective-permute-start.3 = (bf16[256,640]{1,0:T(8,128)(2,1)S(1)}, bf16[256,640]{1,0:T(8,128)(2,1)S(1)}, u32[]{:S(2)}, u32[]{:S(2)}) collective-permute-start(bf16[256,640]{1,0:T(8,128)(2,1)S(1)} %broadcast_select_fusion.1), channel_id=1, source_target_pairs={{0,16},{5,21},{2,18},{7,23}} | collective-permute-start | bytes 983048 | tf_op jit(solution)/shard_map/ppermute | solution.py:295
  23.0 7.9 %collective-permute-start.7 = (bf16[256,640]{1,0:T(8,128)(2,1)S(1)}, bf16[256,640]{1,0:T(8,128)(2,1)S(1)}, u32[]{:S(2)}, u32[]{:S(2)}) collective-permute-start(bf16[256,640]{1,0:T(8,128)(2,1)S(1)} %add.26), channel_id=1, source_target_pairs={{0,8},{5,13},{2,10},{7,15},{16,24},{21,29},{18,26},{23,31}} | collective-permute-start | bytes 983048 | tf_op jit(solution)/shard_map/ppermute | solution.py:295
  27.5 10.8 %collective-permute-start.4 = (bf16[256,640]{1,0:T(8,128)(2,1)S(1)}, bf16[256,640]{1,0:T(8,128)(2,1)S(1)}, u32[]{:S(2)}, u32[]{:S(2)}) collective-permute-start(bf16[256,640]{1,0:T(8,128)(2,1)S(1)} %add.24), channel_id=1, source_target_pairs={{0,8},{5,13},{2,10},{7,15},{16,24},{21,29},{18,26},{23,31}} | collective-permute-start | bytes 983048 | tf_op jit(solution)/shard_map/ppermute | solution.py:295
  31.0 15.9 %copy-start = (bf16[640,1280]{1,0:T(8,128)(2,1)S(1)}, bf16[640,1280]{1,0:T(8,128)(2,1)}, u32[]{:S(2)}) copy-start(bf16[640,1280]{1,0:T(8,128)(2,1)} %keyval_hbm.7) | copy-start | bytes 4915204
  31.0 10.2 %collective-permute-start.11 = (bf16[256,640]{1,0:T(8,128)(2,1)S(1)}, bf16[256,640]{1,0:T(8,128)(2,1)S(1)}, u32[]{:S(2)}, u32[]{:S(2)}) collective-permute-start(bf16[256,640]{1,0:T(8,128)(2,1)S(1)} %add.27), channel_id=1, source_target_pairs={{0,4},{2,6},{8,12},{10,14},{13,9},{15,11},{16,20},{18,22},{21,17},... | collective-permute-start | bytes 983048 | tf_op jit(solution)/shard_map/ppermute | solution.py:295
  32.5 10.9 %collective-permute-start.12 = (bf16[256,640]{1,0:T(8,128)(2,1)S(1)}, bf16[256,640]{1,0:T(8,128)(2,1)S(1)}, u32[]{:S(2)}, u32[]{:S(2)}) collective-permute-start(bf16[256,640]{1,0:T(8,128)(2,1)S(1)} %add.27), channel_id=1, source_target_pairs={{0,2},{2,0},{5,7},{7,5},{8,10},{10,8},{13,15},{15,13},{16,18},{18,... | collective-permute-start | bytes 983048 | tf_op jit(solution)/shard_map/ppermute | solution.py:295
  37.0 9.2 %collective-permute-start.13 = (bf16[256,640]{1,0:T(8,128)(2,1)S(1)}, bf16[256,640]{1,0:T(8,128)(2,1)S(1)}, u32[]{:S(2)}, u32[]{:S(2)}) collective-permute-start(bf16[256,640]{1,0:T(8,128)(2,1)S(1)} %add.27), channel_id=1, source_target_pairs={{0,6},{2,4},{8,14},{10,12},{13,11},{15,9},{16,22},{18,20},{21,19},... | collective-permute-start | bytes 983048 | tf_op jit(solution)/shard_map/ppermute | solution.py:295
  38.4 13.3 %collective-permute-start.10 = (bf16[256,640]{1,0:T(8,128)(2,1)S(1)}, bf16[256,640]{1,0:T(8,128)(2,1)S(1)}, u32[]{:S(2)}, u32[]{:S(2)}) collective-permute-start(bf16[256,640]{1,0:T(8,128)(2,1)S(1)} %add.25), channel_id=1, source_target_pairs={{0,6},{2,4},{8,14},{10,12},{13,11},{15,9},{16,22},{18,20},{21,19},... | collective-permute-start | bytes 983048 | tf_op jit(solution)/shard_map/ppermute | solution.py:295
  39.7 13.1 %collective-permute-start.8 = (bf16[256,640]{1,0:T(8,128)(2,1)S(1)}, bf16[256,640]{1,0:T(8,128)(2,1)S(1)}, u32[]{:S(2)}, u32[]{:S(2)}) collective-permute-start(bf16[256,640]{1,0:T(8,128)(2,1)S(1)} %add.25), channel_id=1, source_target_pairs={{0,4},{2,6},{8,12},{10,14},{13,9},{15,11},{16,20},{18,22},{21,17},... | collective-permute-start | bytes 983048 | tf_op jit(solution)/shard_map/ppermute | solution.py:295
  41.2 12.7 %collective-permute-start.9 = (bf16[256,640]{1,0:T(8,128)(2,1)S(1)}, bf16[256,640]{1,0:T(8,128)(2,1)S(1)}, u32[]{:S(2)}, u32[]{:S(2)}) collective-permute-start(bf16[256,640]{1,0:T(8,128)(2,1)S(1)} %add.25), channel_id=1, source_target_pairs={{0,2},{2,0},{5,7},{7,5},{8,10},{10,8},{13,15},{15,13},{16,18},{18,... | collective-permute-start | bytes 983048 | tf_op jit(solution)/shard_map/ppermute | solution.py:295
  46.3 8.3 %collective-permute-start.17 = (bf16[256,640]{1,0:T(8,128)(2,1)S(1)}, bf16[256,640]{1,0:T(8,128)(2,1)S(1)}, u32[]{:S(2)}, u32[]{:S(2)}) collective-permute-start(bf16[256,640]{1,0:T(8,128)(2,1)S(1)} %add.29.refs_1_), channel_id=1, source_target_pairs={{0,1},{1,0},{2,3},{3,2},{4,5},{5,4},{6,7},{7,6},{8,9},{9,8},{10,11... | collective-permute-start | bytes 983048 | tf_op jit(solution)/shard_map/ppermute | solution.py:295
  46.4 8.3 %collective-permute-start.16 = (bf16[256,640]{1,0:T(8,128)(2,1)S(1)}, bf16[256,640]{1,0:T(8,128)(2,1)S(1)}, u32[]{:S(2)}, u32[]{:S(2)}) collective-permute-start(bf16[256,640]{1,0:T(8,128)(2,1)S(1)} %add.28.refs_0_), channel_id=1, source_target_pairs={{0,1},{1,0},{2,3},{3,2},{4,5},{5,4},{6,7},{7,6},{8,9},{9,8},{10,11... | collective-permute-start | bytes 983048 | tf_op jit(solution)/shard_map/ppermute | solution.py:295
  54.1 10.4 %collective-permute-start.15 = (bf16[256,640]{1,0:T(8,128)(2,1)S(1)}, bf16[256,640]{1,0:T(8,128)(2,1)S(1)}, u32[]{:S(2)}, u32[]{:S(2)}) collective-permute-start(bf16[256,640]{1,0:T(8,128)(2,1)S(1)} %add.31.refs_1_), channel_id=1, source_target_pairs={{0,1},{1,0},{2,3},{3,2},{4,5},{5,4},{6,7},{7,6},{8,9},{9,8},{10,11... | collective-permute-start | bytes 983048 | tf_op jit(solution)/shard_map/ppermute | solution.py:295
  54.2 10.4 %collective-permute-start.14 = (bf16[256,640]{1,0:T(8,128)(2,1)S(1)}, bf16[256,640]{1,0:T(8,128)(2,1)S(1)}, u32[]{:S(2)}, u32[]{:S(2)}) collective-permute-start(bf16[256,640]{1,0:T(8,128)(2,1)S(1)} %add.30.refs_0_), channel_id=1, source_target_pairs={{0,1},{1,0},{2,3},{3,2},{4,5},{5,4},{6,7},{7,6},{8,9},{9,8},{10,11... | collective-permute-start | bytes 983048 | tf_op jit(solution)/shard_map/ppermute | solution.py:295
  59.5 5.1 %copy-start.2 = (bf16[640,640]{1,0:T(8,128)(2,1)S(1)}, bf16[640,640]{1,0:T(8,128)(2,1)}, u32[]{:S(2)}) copy-start(bf16[640,640]{1,0:T(8,128)(2,1)} %refs_12_.1) | copy-start | bytes 2457604

commit v5 on v4

--- a/solution.py
+++ b/solution.py
@@ -9,7 +9,7 @@
 
 HEAD_DIM = 64
 PAIR = 2 * HEAD_DIM
-VMEM_BYTES = 40 * 2**20
+VMEM_BYTES = 36 * 2**20
 CONV_VMEM_BYTES = 28 * 2**20
 IN_VMEM = pl.BlockSpec(memory_space=pltpu.VMEM)
 IN_PLACE = pl.BlockSpec(memory_space=pl.ANY)
@@ -187,20 +187,23 @@
     )(w_query, x, low, high, weight, bias, *pieces)
 
 
-def attend_kernel(piece_count, part_count, last, queries_ref, keyval_hbm, *refs):
+def attend_kernel(piece_count, part_count, last, queries_ref, w_keyval, *refs):
     refs = list(refs)
     pieces = [refs.pop(0) for _ in range(piece_count)]
     parts = [[refs.pop(0) for _ in range(3)] for _ in range(part_count)]
     ending = [refs.pop(0) for _ in range(2)] if last else None
     new = [refs.pop(0) for _ in range(1 if last else 3)]
-    w_keyval, w_out, keys, values, mixed, sems = refs
+    keys, values, mixed, joined = refs
     tokens, channels = queries_ref.shape
-    keyval_copy = pltpu.make_async_copy(keyval_hbm, w_keyval, sems.at[0])
-    keyval_copy.start()
-    if last:
-        out_copy = pltpu.make_async_copy(ending[1], w_out, sems.at[1])
-        out_copy.start()
-    keyval_copy.wait()
+    all_lanes = [slice(start, start + PAIR) for start in range(0, channels, PAIR)]
+    if parts:
+        for lanes in all_lanes:
+            top = functools.reduce(jnp.maximum, [part[2][:, lanes] for part in parts])
+            scales = [jnp.exp(part[2][:, lanes] - top) for part in parts]
+            for i in range(2):
+                scaled = [part[i][:, lanes] * scale for part, scale in zip(parts, scales)]
+                joined[i, :, lanes] = functools.reduce(jnp.add, scaled)
+            joined[2, :, lanes] = top
     key_count = 0
     for piece in pieces:
         spot = slice(key_count, key_count + piece.shape[0])
@@ -211,16 +214,22 @@
         key_count = spot.stop
     is_low = lax.broadcasted_iota(jnp.int32, (tokens, PAIR), 1) < HEAD_DIM
     ones = jnp.ones((key_count, PAIR), jnp.bfloat16)
-    for start in range(0, channels, PAIR):
-        lanes = slice(start, start + PAIR)
+
+    def scores_of(lanes):
         both = queries_ref[:, lanes] * HEAD_DIM ** (-0.5)
         nothing = jnp.zeros_like(both)
         split = jnp.concatenate(
             [jnp.where(is_low, both, nothing), jnp.where(is_low, nothing, both)], axis=0
         )
-        scores = lax.dot_general(
+        return lax.dot_general(
             split, keys[:, lanes], (((1,), (1,)), ((), ())), preferred_element_type=jnp.float32
         )
+
+    next_scores = scores_of(all_lanes[0])
+    for lanes, next_lanes in zip(all_lanes, all_lanes[1:] + [None]):
+        scores = next_scores
+        if next_lanes is not None:
+            next_scores = scores_of(next_lanes)
         best = jnp.max(scores, axis=1, keepdims=True)
         probability = jnp.exp(scores - best).astype(jnp.bfloat16)
         product = jnp.dot(
@@ -231,23 +240,20 @@
         best = jnp.where(is_low, best[:tokens], best[tokens:])
         weighted = jnp.where(is_low, product[:tokens, :PAIR], product[tokens:, :PAIR])
         total = jnp.where(is_low, product[:tokens, PAIR:], product[tokens:, PAIR:])
+        if parts:
+            top = jnp.maximum(best, joined[2, :, lanes])
+            scale, old_scale = jnp.exp(best - top), jnp.exp(joined[2, :, lanes] - top)
+            weighted = weighted * scale + joined[0, :, lanes] * old_scale
+            total = total * scale + joined[1, :, lanes] * old_scale
         if last:
-            top = functools.reduce(jnp.maximum, [part[2][:, lanes] for part in parts], best)
-            scale = jnp.exp(best - top)
-            weighted, total = weighted * scale, total * scale
-            for part in parts:
-                scale = jnp.exp(part[2][:, lanes] - top)
-                weighted = weighted + part[0][:, lanes] * scale
-                total = total + part[1][:, lanes] * scale
             mixed[:, lanes] = (weighted / total).astype(jnp.bfloat16)
         else:
             new[0][:, lanes] = weighted
             new[1][:, lanes] = total
             new[2][:, lanes] = best
     if last:
-        out_copy.wait()
         result = ending[0][...].astype(jnp.float32) + jnp.dot(
-            mixed[...], w_out[...], preferred_element_type=jnp.float32
+            mixed[...], ending[1][...], preferred_element_type=jnp.float32
         )
         new[0][...] = result.astype(jnp.bfloat16)
 
@@ -259,22 +265,16 @@
     part = jax.ShapeDtypeStruct((tokens, channels), jnp.float32)
     whole = jax.ShapeDtypeStruct((tokens, channels), jnp.bfloat16)
     args = [queries, w_keyval, *pieces, *(array for each in parts for array in each), *(ending or ())]
-    in_specs = [IN_VMEM] * len(args)
-    in_specs[1] = IN_PLACE
-    if last:
-        in_specs[-1] = IN_PLACE
     return pl.pallas_call(
         functools.partial(attend_kernel, len(pieces), len(parts), last),
         out_shape=whole if last else (part,) * 3,
-        in_specs=in_specs,
+        in_specs=[IN_VMEM] * len(args),
         out_specs=IN_VMEM if last else (IN_VMEM,) * 3,
         scratch_shapes=[
-            pltpu.VMEM(w_keyval.shape, jnp.bfloat16),
-            pltpu.VMEM((channels, channels), jnp.bfloat16),
             pltpu.VMEM((key_count, channels), jnp.bfloat16),
             pltpu.VMEM((key_count, channels), jnp.bfloat16),
             pltpu.VMEM((tokens, channels), jnp.bfloat16),
-            pltpu.SemaphoreType.DMA((2,)),
+            pltpu.VMEM((3, tokens, channels) if parts else (3, 8, PAIR), jnp.float32),
         ],
         compiler_params=pltpu.CompilerParams(vmem_limit_bytes=VMEM_BYTES),
         cost_estimate=QUICK,
@@ -328,13 +328,13 @@
 def exchange(held):
     frames, bands = lax.axis_size("frame"), lax.axis_size("band")
     holders = [(f, b) for f in range(frames) for b in range(bands) if f % 2 == b % 2]
+    diagonal = permute(held, [((f, b), (f ^ 1, b ^ 2)) for f, b in holders if f != 1])
     beside = permute(held, [((f, b), (f ^ 1, b)) for f, b in holders if f != 1])
     far = permute(
         held,
         [((f, b), (f, b ^ 2)) for f, b in holders] + [((0, b), (0, b ^ 2)) for b in range(bands) if b % 2],
     )
-    diagonal = permute(held, [((f, b), (f ^ 1, b ^ 2)) for f, b in holders if f != 1])
-    return beside, far, diagonal
+    return beside, diagonal, far
 
 
 def swap_cores(value):
@@ -343,7 +343,7 @@
 
 
 def own_side(held, parts):
-    beside, far, diagonal = parts
+    beside, diagonal, far = parts
     return [held + beside, far + diagonal]
 
 

time: 74 us -> 69.2 us (0.935)
  waiting for transfers between devices: 13.8 us -> 8.57 us
  starting transfers between devices: 26.4 us -> 30.4 us
  Pallas kernels: 32.1 us -> 28.5 us
    ppermute x16, waiting for transfers between devices: 10.5 us -> 5.28 us  [permute(): return lax.ppermute(value, ('frame', 'band'), flat)]
    ppermute x16, starting transfers between devices: 22.1 us -> 26.1 us  [permute(): return lax.ppermute(value, ('frame', 'band'), flat)]
    pallas_call x4, Pallas kernels: 23.5 us -> 19.9 us  [attend(): pl.pallas_call(functools.partial(attend_kernel, len(pieces), len(parts),...]
  transfers between devices with their start and end apart: 18 -> 18, of which waited for: 8 -> 4; matrix products, arithmetic and copies ran while one was open for 1% -> 1% of each run, Pallas kernels for 25% -> 25%
where the time goes in v5:
time: 69.2 us; the launch traced here: 68.6 us
  starting transfers between devices  30.4 us (44%)
  Pallas kernels  28.5 us (41%)
  waiting for transfers between devices  8.57 us (12%)
  other arithmetic  0.74 us (1%)
    ppermute x16, starting transfers between devices, permute(): return lax.ppermute(value, ('frame', 'band'), flat)  26.1 us
    pallas_call x4, Pallas kernels, attend(): pl.pallas_call(functools.partial(attend_kernel, len(pieces), len(parts),...  19.9 us
    ppermute x16, waiting for transfers between devices, permute(): return lax.ppermute(value, ('frame', 'band'), flat)  5.28 us
    pallas_call x1, Pallas kernels, convolve_inner(): pl.pallas_call(functools.partial(inner_kernel, width, inner), out_shape=(...  5.12 us
    ppermute x1, waiting for transfers between devices, from_edges(): lax.ppermute(top, 'band', backward)  3.28 us
    ppermute x1, starting transfers between devices, from_edges(): lax.ppermute(bottom, 'band', forward)  2.98 us
    pallas_call x1, Pallas kernels, convolve_outer(): pl.pallas_call(functools.partial(outer_kernel, width, outer), out_shape=j...  2.74 us
  transfers between devices with their start and end apart: 18, of which 4 were waited for; matrix products, arithmetic and copies ran while one was open for 1% of the time, Pallas kernels for 25%

profile of v5, /device:TPU:0, one launch (start us, length us, event | category | flops | bytes accessed | tf_op | source)
XLA Modules:
  0.0 68.6 jit_solution(5422020928848421242)
XLA Ops:
  0.0 5.1 %inner.1 = (bf16[256,640]{1,0:T(8,128)(2,1)S(1)}, bf16[512,640]{1,0:T(8,128)(2,1)S(1)}, bf16[32,640]{1,0:T(8,128)(2,1)S(1)}, bf16[32,640]{1,0:T(8,128)(2,1)S(1)}...) custom-call(bf16[512,640]{1,0:T(8,128)(2,1)} %bitcast.7, bf16[3,1920,640]{2,1,0:T(8,128)(2,1)} %bitcast.3, ...), custom_call_target="tpu_custom_call" | custom-call | flops 1 | bytes 1 | tf_op jit(solution)/shard_map/inner/pallas_call | solution.py:105
  5.1 0.7 collective-permute-start.5
  5.8 3.0 %collective-permute-start = (bf16[32,640]{1,0:T(8,128)(2,1)S(1)}, bf16[32,640]{1,0:T(8,128)(2,1)S(1)}, u32[]{:S(2)}, u32[]{:S(2)}) collective-permute-start(bf16[32,640]{1,0:T(8,128)(2,1)S(1)} %get-tuple-element.41), channel_id=1, source_target_pairs={{0,1},{1,2},{2,3},{4,5},{5,6},{6,7},{8,9},{9,10},{10,11},{12,13},{... | collective-permute-start | bytes 122888 | tf_op jit(solution)/shard_map/ppermute | solution.py:289
  8.8 1.3 %collective-permute-start.1 = (bf16[32,640]{1,0:T(8,128)(2,1)S(1)}, bf16[32,640]{1,0:T(8,128)(2,1)S(1)}, u32[]{:S(2)}, u32[]{:S(2)}) collective-permute-start(bf16[32,640]{1,0:T(8,128)(2,1)S(1)} %get-tuple-element.42), channel_id=1, source_target_pairs={{1,0},{2,1},{3,2},{5,4},{6,5},{7,6},{9,8},{10,9},{11,10},{13,12},{... | collective-permute-start | bytes 122888 | tf_op jit(solution)/shard_map/ppermute | solution.py:289
  10.1 0.0 collective-permute-done.low_ref
  10.1 3.3 %collective-permute-done.1.high_ref = bf16[32,640]{1,0:T(8,128)(2,1)S(1)} collective-permute-done((bf16[32,640]{1,0:T(8,128)(2,1)S(1)}, bf16[32,640]{1,0:T(8,128)(2,1)S(1)}, u32[]{:S(2)}, u32[]{:S(2)}) %collective-permute-start.1) | collective-permute-done | bytes 40992 | tf_op jit(solution)/shard_map/ppermute | solution.py:289
  13.4 2.7 %outer.1.refs_0_ = bf16[256,640]{1,0:T(8,128)(2,1)S(1)} custom-call(bf16[512,640]{1,0:T(8,128)(2,1)S(1)} %get-tuple-element.40.x_ref, bf16[32,640]{1,0:T(8,128)(2,1)S(1)} %collective-permute-done.low_ref, bf16[32,640]{1,0:T(8,128)(2,1)S(1)} %collective-permute-done.1.high_ref, bf16[3,1920,640]{2,1,0:T(8,128)(2,1)S(1)} %get-tuple-element.43.weight, ...), custom_call_target="tpu_custom_call" | custom-call | flops 1 | bytes 1 | tf_op jit(solution)/shard_map/outer/pallas_call | solution.py:134
  16.2 0.0 copy-start.1
  16.2 0.8 %collective-permute-start.2 = (bf16[256,640]{1,0:T(8,128)(2,1)S(1)}, bf16[256,640]{1,0:T(8,128)(2,1)S(1)}, u32[]{:S(2)}, u32[]{:S(2)}) collective-permute-start(bf16[256,640]{1,0:T(8,128)(2,1)S(1)} %outer.1.refs_0_), channel_id=1, source_target_pairs={{1,5},{3,7}} | collective-permute-start | bytes 983048 | tf_op jit(solution)/shard_map/ppermute | solution.py:295
  17.1 1.3 %collective-permute-start.6 = (bf16[256,640]{1,0:T(8,128)(2,1)S(1)}, bf16[256,640]{1,0:T(8,128)(2,1)S(1)}, u32[]{:S(2)}, u32[]{:S(2)}) collective-permute-start(bf16[256,640]{1,0:T(8,128)(2,1)S(1)} %broadcast_select_fusion), channel_id=1, source_target_pairs={{0,16},{5,21},{2,18},{7,23}} | collective-permute-start | bytes 983048 | tf_op jit(solution)/shard_map/ppermute | solution.py:295
  18.4 0.8 %ask.1 = (bf16[512,640]{1,0:T(8,128)(2,1)S(1)}, bf16[512,640]{1,0:T(8,128)(2,1)S(1)}) custom-call(bf16[640,640]{1,0:T(8,128)(2,1)S(1)} %copy-done.1, bf16[512,640]{1,0:T(8,128)(2,1)S(1)} %get-tuple-element.40.x_ref, bf16[32,640]{1,0:T(8,128)(2,1)S(1)} %collective-permute-done.low_ref, bf16[32,640]{1,0:T(8,128)(2,1)S(1)} %collective-permute-done.1.high_ref, ...), custom_call_target="tpu_custom_call" | custom-call | flops 1 | bytes 1 | tf_op jit(solution)/shard_map/ask/pallas_call | solution.py:178
  19.2 0.0 collective-permute-done.2
  19.3 3.6 %collective-permute-start.3 = (bf16[256,640]{1,0:T(8,128)(2,1)S(1)}, bf16[256,640]{1,0:T(8,128)(2,1)S(1)}, u32[]{:S(2)}, u32[]{:S(2)}) collective-permute-start(bf16[256,640]{1,0:T(8,128)(2,1)S(1)} %broadcast_select_fusion.1), channel_id=1, source_target_pairs={{0,16},{5,21},{2,18},{7,23}} | collective-permute-start | bytes 983048 | tf_op jit(solution)/shard_map/ppermute | solution.py:295
  22.9 0.1 collective-permute-done.6
  22.9 0.1 add.26
  23.0 1.3 %collective-permute-start.7 = (bf16[256,640]{1,0:T(8,128)(2,1)S(1)}, bf16[256,640]{1,0:T(8,128)(2,1)S(1)}, u32[]{:S(2)}, u32[]{:S(2)}) collective-permute-start(bf16[256,640]{1,0:T(8,128)(2,1)S(1)} %add.26), channel_id=1, source_target_pairs={{0,8},{5,13},{2,10},{7,15},{16,24},{21,29},{18,26},{23,31}} | collective-permute-start | bytes 983048 | tf_op jit(solution)/shard_map/ppermute | solution.py:295
  24.3 3.1 %collective-permute-done.3 = bf16[256,640]{1,0:T(8,128)(2,1)S(1)} collective-permute-done((bf16[256,640]{1,0:T(8,128)(2,1)S(1)}, bf16[256,640]{1,0:T(8,128)(2,1)S(1)}, u32[]{:S(2)}, u32[]{:S(2)}) %collective-permute-start.3) | collective-permute-done | bytes 327712 | tf_op jit(solution)/shard_map/ppermute | solution.py:295
  27.4 0.1 add.24
  27.5 1.3 %collective-permute-start.4 = (bf16[256,640]{1,0:T(8,128)(2,1)S(1)}, bf16[256,640]{1,0:T(8,128)(2,1)S(1)}, u32[]{:S(2)}, u32[]{:S(2)}) collective-permute-start(bf16[256,640]{1,0:T(8,128)(2,1)S(1)} %add.24), channel_id=1, source_target_pairs={{0,8},{5,13},{2,10},{7,15},{16,24},{21,29},{18,26},{23,31}} | collective-permute-start | bytes 983048 | tf_op jit(solution)/shard_map/ppermute | solution.py:295
  28.8 2.1 %collective-permute-done.7 = bf16[256,640]{1,0:T(8,128)(2,1)S(1)} collective-permute-done((bf16[256,640]{1,0:T(8,128)(2,1)S(1)}, bf16[256,640]{1,0:T(8,128)(2,1)S(1)}, u32[]{:S(2)}, u32[]{:S(2)}) %collective-permute-start.7) | collective-permute-done | bytes 327712 | tf_op jit(solution)/shard_map/ppermute | solution.py:295
  30.9 0.1 add.27
  31.0 0.0 copy-start
  31.0 1.4 %collective-permute-start.11 = (bf16[256,640]{1,0:T(8,128)(2,1)S(1)}, bf16[256,640]{1,0:T(8,128)(2,1)S(1)}, u32[]{:S(2)}, u32[]{:S(2)}) collective-permute-start(bf16[256,640]{1,0:T(8,128)(2,1)S(1)} %add.27), channel_id=1, source_target_pairs={{0,4},{2,6},{8,12},{10,14},{13,9},{15,11},{16,20},{18,22},{21,17},... | collective-permute-start | bytes 983048 | tf_op jit(solution)/shard_map/ppermute | solution.py:295
  32.5 1.3 %collective-permute-start.12 = (bf16[256,640]{1,0:T(8,128)(2,1)S(1)}, bf16[256,640]{1,0:T(8,128)(2,1)S(1)}, u32[]{:S(2)}, u32[]{:S(2)}) collective-permute-start(bf16[256,640]{1,0:T(8,128)(2,1)S(1)} %add.27), channel_id=1, source_target_pairs={{0,6},{2,4},{8,14},{10,12},{13,11},{15,9},{16,22},{18,20},{21,19},... | collective-permute-start | bytes 983048 | tf_op jit(solution)/shard_map/ppermute | solution.py:295
  33.8 4.5 %collective-permute-start.13 = (bf16[256,640]{1,0:T(8,128)(2,1)S(1)}, bf16[256,640]{1,0:T(8,128)(2,1)S(1)}, u32[]{:S(2)}, u32[]{:S(2)}) collective-permute-start(bf16[256,640]{1,0:T(8,128)(2,1)S(1)} %add.27), channel_id=1, source_target_pairs={{0,2},{2,0},{5,7},{7,5},{8,10},{10,8},{13,15},{15,13},{16,18},{18,... | collective-permute-start | bytes 983048 | tf_op jit(solution)/shard_map/ppermute | solution.py:295
  38.3 0.0 collective-permute-done.4
  38.3 0.1 add.25
  38.4 1.9 %collective-permute-start.10 = (bf16[256,640]{1,0:T(8,128)(2,1)S(1)}, bf16[256,640]{1,0:T(8,128)(2,1)S(1)}, u32[]{:S(2)}, u32[]{:S(2)}) collective-permute-start(bf16[256,640]{1,0:T(8,128)(2,1)S(1)} %add.25), channel_id=1, source_target_pairs={{0,2},{2,0},{5,7},{7,5},{8,10},{10,8},{13,15},{15,13},{16,18},{18,... | collective-permute-start | bytes 983048 | tf_op jit(solution)/shard_map/ppermute | solution.py:295
  40.3 1.3 %collective-permute-start.8 = (bf16[256,640]{1,0:T(8,128)(2,1)S(1)}, bf16[256,640]{1,0:T(8,128)(2,1)S(1)}, u32[]{:S(2)}, u32[]{:S(2)}) collective-permute-start(bf16[256,640]{1,0:T(8,128)(2,1)S(1)} %add.25), channel_id=1, source_target_pairs={{0,4},{2,6},{8,12},{10,14},{13,9},{15,11},{16,20},{18,22},{21,17},... | collective-permute-start | bytes 983048 | tf_op jit(solution)/shard_map/ppermute | solution.py:295
  41.7 5.5 %collective-permute-start.9 = (bf16[256,640]{1,0:T(8,128)(2,1)S(1)}, bf16[256,640]{1,0:T(8,128)(2,1)S(1)}, u32[]{:S(2)}, u32[]{:S(2)}) collective-permute-start(bf16[256,640]{1,0:T(8,128)(2,1)S(1)} %add.25), channel_id=1, source_target_pairs={{0,6},{2,4},{8,14},{10,12},{13,11},{15,9},{16,22},{18,20},{21,19},... | collective-permute-start | bytes 983048 | tf_op jit(solution)/shard_map/ppermute | solution.py:295
  47.2 0.0 collective-permute-done.13
  47.2 0.1 add.28.refs_0_
  47.3 0.1 add.29.refs_1_
  47.3 0.1 collective-permute-start.17
  47.4 0.5 collective-permute-start.16
  47.9 4.4 %attend.3 = (f32[512,640]{1,0:T(8,128)S(1)}, f32[512,640]{1,0:T(8,128)S(1)}, f32[512,640]{1,0:T(8,128)S(1)}) custom-call(bf16[512,640]{1,0:T(8,128)(2,1)S(1)} %get-tuple-element.46.queries_ref, bf16[640,1280]{1,0:T(8,128)(2,1)S(1)} %copy-done, bf16[256,640]{1,0:T(8,128)(2,1)S(1)} %add.28.refs_0_, bf16[256,640]{1,0:T(8,128)(2,1)S(1)} %add.29.refs_1_), custom_call_target="tpu_custom_call" | custom-call | flops 1 | bytes 1 | tf_op jit(solution)/shard_map/attend/pallas_call | solution.py:268
  52.3 0.0 collective-permute-done.10
  52.3 0.0 collective-permute-done.9
  52.4 0.1 add.30.refs_0_
  52.4 0.1 add.31.refs_1_
  52.5 0.1 collective-permute-start.15
  52.7 0.4 collective-permute-start.14
  53.1 0.0 collective-permute-done.17.refs_1_
  53.1 4.4 %attend.4 = (f32[512,640]{1,0:T(8,128)S(1)}, f32[512,640]{1,0:T(8,128)S(1)}, f32[512,640]{1,0:T(8,128)S(1)}) custom-call(bf16[512,640]{1,0:T(8,128)(2,1)S(1)} %get-tuple-element.46.queries_ref, bf16[640,1280]{1,0:T(8,128)(2,1)S(1)} %copy-done, bf16[256,640]{1,0:T(8,128)(2,1)S(1)} %collective-permute-done.16.refs_0_, ...), custom_call_target="tpu_custom_call" | custom-call | flops 1 | bytes 1 | tf_op jit(solution)/shard_map/attend/pallas_call | solution.py:268
  57.5 0.0 copy-start.2
  57.5 4.6 %attend.5 = (f32[512,640]{1,0:T(8,128)S(1)}, f32[512,640]{1,0:T(8,128)S(1)}, f32[512,640]{1,0:T(8,128)S(1)}) custom-call(bf16[512,640]{1,0:T(8,128)(2,1)S(1)} %get-tuple-element.46.queries_ref, bf16[640,1280]{1,0:T(8,128)(2,1)S(1)} %copy-done, bf16[256,640]{1,0:T(8,128)(2,1)S(1)} %add.30.refs_0_, bf16[256,640]{1,0:T(8,128)(2,1)S(1)} %add.31.refs_1_), custom_call_target="tpu_custom_call" | custom-call | flops 1 | bytes 1 | tf_op jit(solution)/shard_map/attend/pallas_call | solution.py:268
  62.2 0.0 collective-permute-done.14.refs_0_
  62.2 6.4 %join.1 = bf16[512,640]{1,0:T(8,128)(2,1)} custom-call(bf16[512,640]{1,0:T(8,128)(2,1)S(1)} %get-tuple-element.46.queries_ref, bf16[640,1280]{1,0:T(8,128)(2,1)S(1)} %copy-done, bf16[256,640]{1,0:T(8,128)(2,1)S(1)} %collective-permute-done.14.refs_0_, bf16[256,640]{1,0:T(8,128)(2,1)S(1)} %collective-permute-done.15.refs_1_, ...), custom_call_target="tpu_custom_call" | custom-call | flops 1 | bytes 1 | tf_op jit(solution)/shard_map/join/pallas_call | solution.py:268
  (18 shorter events, 0.1 us)
Async XLA Ops:
  0.0 18.4 %slice-start = ((s8[7372800]{0:T(1024)(128)(4,1)}), s8[4194304]{0:T(1024)(128)(4,1)S(1)}, s32[]{:S(2)}) async-start(s8[7372800]{0:T(1024)(128)(4,1)} %bitcast.4), calls=%async_computation | async-start | bytes 8388608
  5.1 11.9 %collective-permute-start.5 = (bf16[256,640]{1,0:T(8,128)(2,1)S(1)}, bf16[256,640]{1,0:T(8,128)(2,1)S(1)}, u32[]{:S(2)}, u32[]{:S(2)}) collective-permute-start(bf16[256,640]{1,0:T(8,128)(2,1)S(1)} %get-tuple-element.45.refs_1_), channel_id=1, source_target_pairs={{1,5},{3,7}} | collective-permute-start | bytes 983048 | tf_op jit(solution)/shard_map/ppermute | solution.py:295
  5.8 4.3 %collective-permute-start = (bf16[32,640]{1,0:T(8,128)(2,1)S(1)}, bf16[32,640]{1,0:T(8,128)(2,1)S(1)}, u32[]{:S(2)}, u32[]{:S(2)}) collective-permute-start(bf16[32,640]{1,0:T(8,128)(2,1)S(1)} %get-tuple-element.41), channel_id=1, source_target_pairs={{0,1},{1,2},{2,3},{4,5},{5,6},{6,7},{8,9},{9,10},{10,11},{12,13},{... | collective-permute-start | bytes 122888 | tf_op jit(solution)/shard_map/ppermute | solution.py:289
  8.8 4.6 %collective-permute-start.1 = (bf16[32,640]{1,0:T(8,128)(2,1)S(1)}, bf16[32,640]{1,0:T(8,128)(2,1)S(1)}, u32[]{:S(2)}, u32[]{:S(2)}) collective-permute-start(bf16[32,640]{1,0:T(8,128)(2,1)S(1)} %get-tuple-element.42), channel_id=1, source_target_pairs={{1,0},{2,1},{3,2},{5,4},{6,5},{7,6},{9,8},{10,9},{11,10},{13,12},{... | collective-permute-start | bytes 122888 | tf_op jit(solution)/shard_map/ppermute | solution.py:289
  13.4 5.0 %slice-start.1 = ((s8[7372800]{0:T(1024)(128)(4,1)}), s8[3178496]{0:T(1024)(128)(4,1)S(1)}, s32[]{:S(2)}) async-start(s8[7372800]{0:T(1024)(128)(4,1)} %bitcast.4), calls=%async_computation.1 | async-start | bytes 6356992
  13.4 5.0 %copy-start.3 = (bf16[640]{0:T(1024)(128)(2,1)S(1)}, bf16[640]{0:T(1024)(128)(2,1)}, u32[]{:S(2)}) copy-start(bf16[640]{0:T(1024)(128)(2,1)} %bias_ref.1) | copy-start | bytes 3844
  16.2 2.2 %copy-start.1 = (bf16[640,640]{1,0:T(8,128)(2,1)S(1)}, bf16[640,640]{1,0:T(8,128)(2,1)}, u32[]{:S(2)}) copy-start(bf16[640,640]{1,0:T(8,128)(2,1)} %w_query.1) | copy-start | bytes 2457604
  16.2 3.1 %collective-permute-start.2 = (bf16[256,640]{1,0:T(8,128)(2,1)S(1)}, bf16[256,640]{1,0:T(8,128)(2,1)S(1)}, u32[]{:S(2)}, u32[]{:S(2)}) collective-permute-start(bf16[256,640]{1,0:T(8,128)(2,1)S(1)} %outer.1.refs_0_), channel_id=1, source_target_pairs={{1,5},{3,7}} | collective-permute-start | bytes 983048 | tf_op jit(solution)/shard_map/ppermute | solution.py:295
  17.1 5.9 %collective-permute-start.6 = (bf16[256,640]{1,0:T(8,128)(2,1)S(1)}, bf16[256,640]{1,0:T(8,128)(2,1)S(1)}, u32[]{:S(2)}, u32[]{:S(2)}) collective-permute-start(bf16[256,640]{1,0:T(8,128)(2,1)S(1)} %broadcast_select_fusion), channel_id=1, source_target_pairs={{0,16},{5,21},{2,18},{7,23}} | collective-permute-start | bytes 983048 | tf_op jit(solution)/shard_map/ppermute | solution.py:295
  19.3 8.1 %collective-permute-start.3 = (bf16[256,640]{1,0:T(8,128)(2,1)S(1)}, bf16[256,640]{1,0:T(8,128)(2,1)S(1)}, u32[]{:S(2)}, u32[]{:S(2)}) collective-permute-start(bf16[256,640]{1,0:T(8,128)(2,1)S(1)} %broadcast_select_fusion.1), channel_id=1, source_target_pairs={{0,16},{5,21},{2,18},{7,23}} | collective-permute-start | bytes 983048 | tf_op jit(solution)/shard_map/ppermute | solution.py:295
  23.0 7.9 %collective-permute-start.7 = (bf16[256,640]{1,0:T(8,128)(2,1)S(1)}, bf16[256,640]{1,0:T(8,128)(2,1)S(1)}, u32[]{:S(2)}, u32[]{:S(2)}) collective-permute-start(bf16[256,640]{1,0:T(8,128)(2,1)S(1)} %add.26), channel_id=1, source_target_pairs={{0,8},{5,13},{2,10},{7,15},{16,24},{21,29},{18,26},{23,31}} | collective-permute-start | bytes 983048 | tf_op jit(solution)/shard_map/ppermute | solution.py:295
  27.5 10.8 %collective-permute-start.4 = (bf16[256,640]{1,0:T(8,128)(2,1)S(1)}, bf16[256,640]{1,0:T(8,128)(2,1)S(1)}, u32[]{:S(2)}, u32[]{:S(2)}) collective-permute-start(bf16[256,640]{1,0:T(8,128)(2,1)S(1)} %add.24), channel_id=1, source_target_pairs={{0,8},{5,13},{2,10},{7,15},{16,24},{21,29},{18,26},{23,31}} | collective-permute-start | bytes 983048 | tf_op jit(solution)/shard_map/ppermute | solution.py:295
  31.0 16.9 %copy-start = (bf16[640,1280]{1,0:T(8,128)(2,1)S(1)}, bf16[640,1280]{1,0:T(8,128)(2,1)}, u32[]{:S(2)}) copy-start(bf16[640,1280]{1,0:T(8,128)(2,1)} %w_keyval.7) | copy-start | bytes 4915204
  31.0 10.6 %collective-permute-start.11 = (bf16[256,640]{1,0:T(8,128)(2,1)S(1)}, bf16[256,640]{1,0:T(8,128)(2,1)S(1)}, u32[]{:S(2)}, u32[]{:S(2)}) collective-permute-start(bf16[256,640]{1,0:T(8,128)(2,1)S(1)} %add.27), channel_id=1, source_target_pairs={{0,4},{2,6},{8,12},{10,14},{13,9},{15,11},{16,20},{18,22},{21,17},... | collective-permute-start | bytes 983048 | tf_op jit(solution)/shard_map/ppermute | solution.py:295
  32.5 14.7 %collective-permute-start.12 = (bf16[256,640]{1,0:T(8,128)(2,1)S(1)}, bf16[256,640]{1,0:T(8,128)(2,1)S(1)}, u32[]{:S(2)}, u32[]{:S(2)}) collective-permute-start(bf16[256,640]{1,0:T(8,128)(2,1)S(1)} %add.27), channel_id=1, source_target_pairs={{0,6},{2,4},{8,14},{10,12},{13,11},{15,9},{16,22},{18,20},{21,19},... | collective-permute-start | bytes 983048 | tf_op jit(solution)/shard_map/ppermute | solution.py:295
  33.8 13.4 %collective-permute-start.13 = (bf16[256,640]{1,0:T(8,128)(2,1)S(1)}, bf16[256,640]{1,0:T(8,128)(2,1)S(1)}, u32[]{:S(2)}, u32[]{:S(2)}) collective-permute-start(bf16[256,640]{1,0:T(8,128)(2,1)S(1)} %add.27), channel_id=1, source_target_pairs={{0,2},{2,0},{5,7},{7,5},{8,10},{10,8},{13,15},{15,13},{16,18},{18,... | collective-permute-start | bytes 983048 | tf_op jit(solution)/shard_map/ppermute | solution.py:295
  38.4 13.9 %collective-permute-start.10 = (bf16[256,640]{1,0:T(8,128)(2,1)S(1)}, bf16[256,640]{1,0:T(8,128)(2,1)S(1)}, u32[]{:S(2)}, u32[]{:S(2)}) collective-permute-start(bf16[256,640]{1,0:T(8,128)(2,1)S(1)} %add.25), channel_id=1, source_target_pairs={{0,2},{2,0},{5,7},{7,5},{8,10},{10,8},{13,15},{15,13},{16,18},{18,... | collective-permute-start | bytes 983048 | tf_op jit(solution)/shard_map/ppermute | solution.py:295
  40.3 12.0 %collective-permute-start.8 = (bf16[256,640]{1,0:T(8,128)(2,1)S(1)}, bf16[256,640]{1,0:T(8,128)(2,1)S(1)}, u32[]{:S(2)}, u32[]{:S(2)}) collective-permute-start(bf16[256,640]{1,0:T(8,128)(2,1)S(1)} %add.25), channel_id=1, source_target_pairs={{0,4},{2,6},{8,12},{10,14},{13,9},{15,11},{16,20},{18,22},{21,17},... | collective-permute-start | bytes 983048 | tf_op jit(solution)/shard_map/ppermute | solution.py:295
  41.7 10.7 %collective-permute-start.9 = (bf16[256,640]{1,0:T(8,128)(2,1)S(1)}, bf16[256,640]{1,0:T(8,128)(2,1)S(1)}, u32[]{:S(2)}, u32[]{:S(2)}) collective-permute-start(bf16[256,640]{1,0:T(8,128)(2,1)S(1)} %add.25), channel_id=1, source_target_pairs={{0,6},{2,4},{8,14},{10,12},{13,11},{15,9},{16,22},{18,20},{21,19},... | collective-permute-start | bytes 983048 | tf_op jit(solution)/shard_map/ppermute | solution.py:295
  47.3 5.8 %collective-permute-start.17 = (bf16[256,640]{1,0:T(8,128)(2,1)S(1)}, bf16[256,640]{1,0:T(8,128)(2,1)S(1)}, u32[]{:S(2)}, u32[]{:S(2)}) collective-permute-start(bf16[256,640]{1,0:T(8,128)(2,1)S(1)} %add.29.refs_1_), channel_id=1, source_target_pairs={{0,1},{1,0},{2,3},{3,2},{4,5},{5,4},{6,7},{7,6},{8,9},{9,8},{10,11... | collective-permute-start | bytes 983048 | tf_op jit(solution)/shard_map/ppermute | solution.py:295
  47.4 5.7 %collective-permute-start.16 = (bf16[256,640]{1,0:T(8,128)(2,1)S(1)}, bf16[256,640]{1,0:T(8,128)(2,1)S(1)}, u32[]{:S(2)}, u32[]{:S(2)}) collective-permute-start(bf16[256,640]{1,0:T(8,128)(2,1)S(1)} %add.28.refs_0_), channel_id=1, source_target_pairs={{0,1},{1,0},{2,3},{3,2},{4,5},{5,4},{6,7},{7,6},{8,9},{9,8},{10,11... | collective-permute-start | bytes 983048 | tf_op jit(solution)/shard_map/ppermute | solution.py:295
  52.5 9.6 %collective-permute-start.15 = (bf16[256,640]{1,0:T(8,128)(2,1)S(1)}, bf16[256,640]{1,0:T(8,128)(2,1)S(1)}, u32[]{:S(2)}, u32[]{:S(2)}) collective-permute-start(bf16[256,640]{1,0:T(8,128)(2,1)S(1)} %add.31.refs_1_), channel_id=1, source_target_pairs={{0,1},{1,0},{2,3},{3,2},{4,5},{5,4},{6,7},{7,6},{8,9},{9,8},{10,11... | collective-permute-start | bytes 983048 | tf_op jit(solution)/shard_map/ppermute | solution.py:295
  52.7 9.5 %collective-permute-start.14 = (bf16[256,640]{1,0:T(8,128)(2,1)S(1)}, bf16[256,640]{1,0:T(8,128)(2,1)S(1)}, u32[]{:S(2)}, u32[]{:S(2)}) collective-permute-start(bf16[256,640]{1,0:T(8,128)(2,1)S(1)} %add.30.refs_0_), channel_id=1, source_target_pairs={{0,1},{1,0},{2,3},{3,2},{4,5},{5,4},{6,7},{7,6},{8,9},{9,8},{10,11... | collective-permute-start | bytes 983048 | tf_op jit(solution)/shard_map/ppermute | solution.py:295
  57.5 4.7 %copy-start.2 = (bf16[640,640]{1,0:T(8,128)(2,1)S(1)}, bf16[640,640]{1,0:T(8,128)(2,1)}, u32[]{:S(2)}) copy-start(bf16[640,640]{1,0:T(8,128)(2,1)} %refs_12_.1) | copy-start | bytes 2457604

commit v6 on v5

--- a/solution.py
+++ b/solution.py
@@ -187,14 +187,37 @@
     )(w_query, x, low, high, weight, bias, *pieces)
 
 
-def attend_kernel(piece_count, part_count, last, queries_ref, w_keyval, *refs):
+def project_kernel(piece_count, w_keyval, *refs):
+    pieces, keyval_ref = refs[:piece_count], refs[piece_count]
+    start = 0
+    for piece in pieces:
+        stop = start + piece.shape[0]
+        keyval = jnp.dot(piece[...], w_keyval[...], preferred_element_type=jnp.float32)
+        keyval_ref[start:stop, :] = keyval.astype(jnp.bfloat16)
+        start = stop
+
+
+def project(pieces, w_keyval):
+    tokens = sum(piece.shape[0] for piece in pieces)
+    return pl.pallas_call(
+        functools.partial(project_kernel, len(pieces)),
+        out_shape=jax.ShapeDtypeStruct((tokens, w_keyval.shape[1]), jnp.bfloat16),
+        in_specs=[IN_VMEM] * (len(pieces) + 1),
+        out_specs=IN_VMEM,
+        compiler_params=pltpu.CompilerParams(vmem_limit_bytes=CONV_VMEM_BYTES),
+        cost_estimate=QUICK,
+        name="project",
+    )(w_keyval, *pieces)
+
+
+def attend_kernel(part_count, last, queries_ref, keyval, *refs):
     refs = list(refs)
-    pieces = [refs.pop(0) for _ in range(piece_count)]
     parts = [[refs.pop(0) for _ in range(3)] for _ in range(part_count)]
     ending = [refs.pop(0) for _ in range(2)] if last else None
     new = [refs.pop(0) for _ in range(1 if last else 3)]
-    keys, values, mixed, joined = refs
+    mixed, joined = refs
     tokens, channels = queries_ref.shape
+    key_count = keyval.shape[0]
     all_lanes = [slice(start, start + PAIR) for start in range(0, channels, PAIR)]
     if parts:
         for lanes in all_lanes:
@@ -204,14 +227,6 @@
                 scaled = [part[i][:, lanes] * scale for part, scale in zip(parts, scales)]
                 joined[i, :, lanes] = functools.reduce(jnp.add, scaled)
             joined[2, :, lanes] = top
-    key_count = 0
-    for piece in pieces:
-        spot = slice(key_count, key_count + piece.shape[0])
-        keyval = jnp.dot(piece[...], w_keyval[...], preferred_element_type=jnp.float32)
-        keyval = keyval.astype(jnp.bfloat16)
-        keys[spot, :] = keyval[:, :channels]
-        values[spot, :] = keyval[:, channels:]
-        key_count = spot.stop
     is_low = lax.broadcasted_iota(jnp.int32, (tokens, PAIR), 1) < HEAD_DIM
     ones = jnp.ones((key_count, PAIR), jnp.bfloat16)
 
@@ -222,7 +237,7 @@
             [jnp.where(is_low, both, nothing), jnp.where(is_low, nothing, both)], axis=0
         )
         return lax.dot_general(
-            split, keys[:, lanes], (((1,), (1,)), ((), ())), preferred_element_type=jnp.float32
+            split, keyval[:, lanes], (((1,), (1,)), ((), ())), preferred_element_type=jnp.float32
         )
 
     next_scores = scores_of(all_lanes[0])
@@ -232,9 +247,10 @@
             next_scores = scores_of(next_lanes)
         best = jnp.max(scores, axis=1, keepdims=True)
         probability = jnp.exp(scores - best).astype(jnp.bfloat16)
+        values = keyval[:, channels + lanes.start : channels + lanes.stop]
         product = jnp.dot(
             probability,
-            jnp.concatenate([values[:, lanes], ones], axis=1),
+            jnp.concatenate([values, ones], axis=1),
             preferred_element_type=jnp.float32,
         )
         best = jnp.where(is_low, best[:tokens], best[tokens:])
@@ -258,21 +274,18 @@
         new[0][...] = result.astype(jnp.bfloat16)
 
 
-def attend(queries, w_keyval, pieces, parts, ending, name):
+def attend(queries, keyval, parts, ending, name):
     tokens, channels = queries.shape
-    key_count = sum(piece.shape[0] for piece in pieces)
     last = ending is not None
     part = jax.ShapeDtypeStruct((tokens, channels), jnp.float32)
     whole = jax.ShapeDtypeStruct((tokens, channels), jnp.bfloat16)
-    args = [queries, w_keyval, *pieces, *(array for each in parts for array in each), *(ending or ())]
+    args = [queries, keyval, *(array for each in parts for array in each), *(ending or ())]
     return pl.pallas_call(
-        functools.partial(attend_kernel, len(pieces), len(parts), last),
+        functools.partial(attend_kernel, len(parts), last),
         out_shape=whole if last else (part,) * 3,
         in_specs=[IN_VMEM] * len(args),
         out_specs=IN_VMEM if last else (IN_VMEM,) * 3,
         scratch_shapes=[
-            pltpu.VMEM((key_count, channels), jnp.bfloat16),
-            pltpu.VMEM((key_count, channels), jnp.bfloat16),
             pltpu.VMEM((tokens, channels), jnp.bfloat16),
             pltpu.VMEM((3, tokens, channels) if parts else (3, 8, PAIR), jnp.float32),
         ],
@@ -347,21 +360,22 @@
     return [held + beside, far + diagonal]
 
 
-def sees_all(chunks, starts, look, early):
+def sees_all(chunks, starts, early, keyval_of, look):
     frames, bands = lax.axis_size("frame"), lax.axis_size("band")
     if frames < 2 or frames & (frames - 1) or bands != 4:
-        pieces = [lax.all_gather(chunk, ("frame", "band"))[b] for chunk in chunks for b in range(bands)]
-        return [], pieces
+        return [], keyval_of([lax.all_gather(chunk, ("frame", "band"))[b] for chunk in chunks for b in range(bands)])
     held0, held1 = cast(starts, (*early, starts[1]))
     parts0 = exchange(held0)
+    parts0 = (parts0[2], parts0[1], parts0[0])
     held1 = ordered(held1, held0)
     parts1 = exchange(held1)
-    here0 = own_side(held0, ordered(parts0, held1))
-    there0 = [swap_cores(piece) for piece in here0]
+    parts1 = (parts1[2], parts1[1], parts1[0])
+    here0 = keyval_of(own_side(held0, [ordered(parts0, held1)[i] for i in (2, 1, 0)]))
+    there0 = swap_cores(here0)
     look0 = look(here0)
-    here1 = own_side(held1, ordered(parts1, look0))
+    here1 = keyval_of(own_side(held1, [ordered(parts1, look0)[i] for i in (2, 1, 0)]))
+    there1 = swap_cores(here1)
     look1 = look(ordered(there0, look0, here1))
-    there1 = [swap_cores(piece) for piece in here1]
     look2 = look(ordered(here1, look1))
     return [look0, look1, look2], ordered(there1, look2)
 
@@ -392,12 +406,15 @@
     chunks = (first, second)
     starts = (begun, step_across(second, is_source))
 
-    def look(pieces):
-        return tuple(attend(queries, w_keyval, pieces, (), None, "attend") for _, queries in asked)
-
-    looks, pieces = sees_all(chunks, starts, look, [queries for _, queries in asked])
+    def keyval_of(pieces):
+        return project(pieces, w_keyval)
+
+    def look(keyval):
+        return tuple(attend(queries, keyval, (), None, "attend") for _, queries in asked)
+
+    looks, keyval = sees_all(chunks, starts, [queries for _, queries in asked], keyval_of, look)
     results = [
-        attend(queries, w_keyval, pieces, [each[i] for each in looks], (hidden, w_out), "join")
+        attend(queries, keyval, [each[i] for each in looks], (hidden, w_out), "join")
         for i, (hidden, queries) in enumerate(asked)
     ]
     return jnp.stack(results).reshape(latents.shape)

time: 69.2 us -> 68.1 us (0.984)
  waiting for transfers between devices: 8.57 us -> 12.2 us
  starting transfers between devices: 30.4 us -> 27.5 us
  Pallas kernels: 28.5 us -> 26.9 us
    ppermute x16 -> x14, waiting for transfers between devices: 5.28 us -> 8.95 us  [permute(): return lax.ppermute(value, ('frame', 'band'), flat)]
    ppermute x16 -> x14, starting transfers between devices: 26.1 us -> 23.2 us  [permute(): return lax.ppermute(value, ('frame', 'band'), flat)]
    pallas_call x4 -> x6, Pallas kernels: 19.9 us -> 18.2 us  [the longest x4 15.8 us: attend(): pl.pallas_call(functools.partial(attend_kernel, len(parts), last), out_sh...]
  transfers between devices with their start and end apart: 18 -> 16, of which waited for: 4 -> 6; matrix products, arithmetic and copies ran while one was open for 1% -> 1% of each run, Pallas kernels for 25% -> 24%
where the time goes in v6:
time: 68.1 us; the launch traced here: 67.7 us
  starting transfers between devices  27.5 us (40%)
  Pallas kernels  26.9 us (40%)
  waiting for transfers between devices  12.2 us (18%)
  other arithmetic  0.76 us (1%)
    ppermute x14, starting transfers between devices, permute(): return lax.ppermute(value, ('frame', 'band'), flat)  23.2 us
    pallas_call x4, Pallas kernels, attend(): pl.pallas_call(functools.partial(attend_kernel, len(parts), last), out_sh...  15.8 us
    ppermute x14, waiting for transfers between devices, permute(): return lax.ppermute(value, ('frame', 'band'), flat)  8.95 us
    pallas_call x1, Pallas kernels, convolve_inner(): pl.pallas_call(functools.partial(inner_kernel, width, inner), out_shape=(...  5.12 us
    ppermute x1, waiting for transfers between devices, from_edges(): lax.ppermute(top, 'band', backward)  3.28 us
    ppermute x1, starting transfers between devices, from_edges(): lax.ppermute(bottom, 'band', forward)  2.98 us
    pallas_call x1, Pallas kernels, convolve_outer(): pl.pallas_call(functools.partial(outer_kernel, width, outer), out_shape=j...  2.74 us
    pallas_call x2, Pallas kernels, project(): pl.pallas_call(functools.partial(project_kernel, len(pieces)), out_shape=...  2.37 us
  transfers between devices with their start and end apart: 16, of which 6 were waited for; matrix products, arithmetic and copies ran while one was open for 1% of the time, Pallas kernels for 24%

profile of v6, /device:TPU:0, one launch (start us, length us, event | category | flops | bytes accessed | tf_op | source)
XLA Modules:
  0.0 67.7 jit_solution(4691746288231499345)
XLA Ops:
  0.0 5.1 %inner.1 = (bf16[256,640]{1,0:T(8,128)(2,1)S(1)}, bf16[512,640]{1,0:T(8,128)(2,1)S(1)}, bf16[32,640]{1,0:T(8,128)(2,1)S(1)}, bf16[32,640]{1,0:T(8,128)(2,1)S(1)}...) custom-call(bf16[512,640]{1,0:T(8,128)(2,1)} %bitcast.7, bf16[3,1920,640]{2,1,0:T(8,128)(2,1)} %bitcast.3, ...), custom_call_target="tpu_custom_call" | custom-call | flops 1 | bytes 1 | tf_op jit(solution)/shard_map/inner/pallas_call | solution.py:105
  5.1 0.7 %collective-permute-start.5 = (bf16[256,640]{1,0:T(8,128)(2,1)S(1)}, bf16[256,640]{1,0:T(8,128)(2,1)S(1)}, u32[]{:S(2)}, u32[]{:S(2)}) collective-permute-start(bf16[256,640]{1,0:T(8,128)(2,1)S(1)} %get-tuple-element.42.refs_1_), channel_id=1, source_target_pairs={{1,5},{3,7}} | collective-permute-start | bytes 983048 | tf_op jit(solution)/shard_map/ppermute | solution.py:308
  5.8 3.0 %collective-permute-start = (bf16[32,640]{1,0:T(8,128)(2,1)S(1)}, bf16[32,640]{1,0:T(8,128)(2,1)S(1)}, u32[]{:S(2)}, u32[]{:S(2)}) collective-permute-start(bf16[32,640]{1,0:T(8,128)(2,1)S(1)} %get-tuple-element.38), channel_id=1, source_target_pairs={{0,1},{1,2},{2,3},{4,5},{5,6},{6,7},{8,9},{9,10},{10,11},{12,13},{... | collective-permute-start | bytes 122888 | tf_op jit(solution)/shard_map/ppermute | solution.py:302
  8.8 1.3 %collective-permute-start.1 = (bf16[32,640]{1,0:T(8,128)(2,1)S(1)}, bf16[32,640]{1,0:T(8,128)(2,1)S(1)}, u32[]{:S(2)}, u32[]{:S(2)}) collective-permute-start(bf16[32,640]{1,0:T(8,128)(2,1)S(1)} %get-tuple-element.39), channel_id=1, source_target_pairs={{1,0},{2,1},{3,2},{5,4},{6,5},{7,6},{9,8},{10,9},{11,10},{13,12},{... | collective-permute-start | bytes 122888 | tf_op jit(solution)/shard_map/ppermute | solution.py:302
  10.1 0.0 collective-permute-done.low_ref
  10.1 3.3 %collective-permute-done.1.high_ref = bf16[32,640]{1,0:T(8,128)(2,1)S(1)} collective-permute-done((bf16[32,640]{1,0:T(8,128)(2,1)S(1)}, bf16[32,640]{1,0:T(8,128)(2,1)S(1)}, u32[]{:S(2)}, u32[]{:S(2)}) %collective-permute-start.1) | collective-permute-done | bytes 40992 | tf_op jit(solution)/shard_map/ppermute | solution.py:302
  13.4 2.7 %outer.1.refs_0_ = bf16[256,640]{1,0:T(8,128)(2,1)S(1)} custom-call(bf16[512,640]{1,0:T(8,128)(2,1)S(1)} %get-tuple-element.37.x_ref, bf16[32,640]{1,0:T(8,128)(2,1)S(1)} %collective-permute-done.low_ref, bf16[32,640]{1,0:T(8,128)(2,1)S(1)} %collective-permute-done.1.high_ref, bf16[3,1920,640]{2,1,0:T(8,128)(2,1)S(1)} %get-tuple-element.40.weight, ...), custom_call_target="tpu_custom_call" | custom-call | flops 1 | bytes 1 | tf_op jit(solution)/shard_map/outer/pallas_call | solution.py:134
  16.2 0.0 copy-start.1
  16.2 0.8 %collective-permute-start.2 = (bf16[256,640]{1,0:T(8,128)(2,1)S(1)}, bf16[256,640]{1,0:T(8,128)(2,1)S(1)}, u32[]{:S(2)}, u32[]{:S(2)}) collective-permute-start(bf16[256,640]{1,0:T(8,128)(2,1)S(1)} %outer.1.refs_0_), channel_id=1, source_target_pairs={{1,5},{3,7}} | collective-permute-start | bytes 983048 | tf_op jit(solution)/shard_map/ppermute | solution.py:308
  17.0 0.1 broadcast_select_fusion
  17.1 1.3 %collective-permute-start.6 = (bf16[256,640]{1,0:T(8,128)(2,1)S(1)}, bf16[256,640]{1,0:T(8,128)(2,1)S(1)}, u32[]{:S(2)}, u32[]{:S(2)}) collective-permute-start(bf16[256,640]{1,0:T(8,128)(2,1)S(1)} %broadcast_select_fusion), channel_id=1, source_target_pairs={{0,16},{5,21},{2,18},{7,23}} | collective-permute-start | bytes 983048 | tf_op jit(solution)/shard_map/ppermute | solution.py:308
  18.4 0.8 %ask.1 = (bf16[512,640]{1,0:T(8,128)(2,1)S(1)}, bf16[512,640]{1,0:T(8,128)(2,1)S(1)}) custom-call(bf16[640,640]{1,0:T(8,128)(2,1)S(1)} %copy-done.1, bf16[512,640]{1,0:T(8,128)(2,1)S(1)} %get-tuple-element.37.x_ref, bf16[32,640]{1,0:T(8,128)(2,1)S(1)} %collective-permute-done.low_ref, bf16[32,640]{1,0:T(8,128)(2,1)S(1)} %collective-permute-done.1.high_ref, ...), custom_call_target="tpu_custom_call" | custom-call | flops 1 | bytes 1 | tf_op jit(solution)/shard_map/ask/pallas_call | solution.py:178
  19.3 3.6 %collective-permute-start.3 = (bf16[256,640]{1,0:T(8,128)(2,1)S(1)}, bf16[256,640]{1,0:T(8,128)(2,1)S(1)}, u32[]{:S(2)}, u32[]{:S(2)}) collective-permute-start(bf16[256,640]{1,0:T(8,128)(2,1)S(1)} %broadcast_select_fusion.1), channel_id=1, source_target_pairs={{0,16},{5,21},{2,18},{7,23}} | collective-permute-start | bytes 983048 | tf_op jit(solution)/shard_map/ppermute | solution.py:308
  22.9 0.1 collective-permute-done.6
  22.9 0.1 add.26
  23.0 1.3 %collective-permute-start.7 = (bf16[256,640]{1,0:T(8,128)(2,1)S(1)}, bf16[256,640]{1,0:T(8,128)(2,1)S(1)}, u32[]{:S(2)}, u32[]{:S(2)}) collective-permute-start(bf16[256,640]{1,0:T(8,128)(2,1)S(1)} %add.26), channel_id=1, source_target_pairs={{0,8},{5,13},{2,10},{7,15},{16,24},{21,29},{18,26},{23,31}} | collective-permute-start | bytes 983048 | tf_op jit(solution)/shard_map/ppermute | solution.py:308
  24.3 3.1 %collective-permute-done.3 = bf16[256,640]{1,0:T(8,128)(2,1)S(1)} collective-permute-done((bf16[256,640]{1,0:T(8,128)(2,1)S(1)}, bf16[256,640]{1,0:T(8,128)(2,1)S(1)}, u32[]{:S(2)}, u32[]{:S(2)}) %collective-permute-start.3) | collective-permute-done | bytes 327712 | tf_op jit(solution)/shard_map/ppermute | solution.py:308
  27.4 0.1 add.24
  27.5 1.3 %collective-permute-start.4 = (bf16[256,640]{1,0:T(8,128)(2,1)S(1)}, bf16[256,640]{1,0:T(8,128)(2,1)S(1)}, u32[]{:S(2)}, u32[]{:S(2)}) collective-permute-start(bf16[256,640]{1,0:T(8,128)(2,1)S(1)} %add.24), channel_id=1, source_target_pairs={{0,8},{5,13},{2,10},{7,15},{16,24},{21,29},{18,26},{23,31}} | collective-permute-start | bytes 983048 | tf_op jit(solution)/shard_map/ppermute | solution.py:308
  28.8 2.1 %collective-permute-done.7 = bf16[256,640]{1,0:T(8,128)(2,1)S(1)} collective-permute-done((bf16[256,640]{1,0:T(8,128)(2,1)S(1)}, bf16[256,640]{1,0:T(8,128)(2,1)S(1)}, u32[]{:S(2)}, u32[]{:S(2)}) %collective-permute-start.7) | collective-permute-done | bytes 327712 | tf_op jit(solution)/shard_map/ppermute | solution.py:308
  30.9 0.1 add.27
  31.0 0.0 copy-start
  31.0 1.4 %collective-permute-start.13 = (bf16[256,640]{1,0:T(8,128)(2,1)S(1)}, bf16[256,640]{1,0:T(8,128)(2,1)S(1)}, u32[]{:S(2)}, u32[]{:S(2)}) collective-permute-start(bf16[256,640]{1,0:T(8,128)(2,1)S(1)} %add.27), channel_id=1, source_target_pairs={{0,4},{2,6},{8,12},{10,14},{13,9},{15,11},{16,20},{18,22},{21,17},... | collective-permute-start | bytes 983048 | tf_op jit(solution)/shard_map/ppermute | solution.py:308
  32.5 1.3 %collective-permute-start.12 = (bf16[256,640]{1,0:T(8,128)(2,1)S(1)}, bf16[256,640]{1,0:T(8,128)(2,1)S(1)}, u32[]{:S(2)}, u32[]{:S(2)}) collective-permute-start(bf16[256,640]{1,0:T(8,128)(2,1)S(1)} %add.27), channel_id=1, source_target_pairs={{0,6},{2,4},{8,14},{10,12},{13,11},{15,9},{16,22},{18,20},{21,19},... | collective-permute-start | bytes 983048 | tf_op jit(solution)/shard_map/ppermute | solution.py:308
  33.8 4.5 %collective-permute-start.11 = (bf16[256,640]{1,0:T(8,128)(2,1)S(1)}, bf16[256,640]{1,0:T(8,128)(2,1)S(1)}, u32[]{:S(2)}, u32[]{:S(2)}) collective-permute-start(bf16[256,640]{1,0:T(8,128)(2,1)S(1)} %add.27), channel_id=1, source_target_pairs={{0,2},{2,0},{5,7},{7,5},{8,10},{10,8},{13,15},{15,13},{16,18},{18,... | collective-permute-start | bytes 983048 | tf_op jit(solution)/shard_map/ppermute | solution.py:308
  38.3 0.0 collective-permute-done.4
  38.3 0.1 add.25
  38.4 1.3 %collective-permute-start.10 = (bf16[256,640]{1,0:T(8,128)(2,1)S(1)}, bf16[256,640]{1,0:T(8,128)(2,1)S(1)}, u32[]{:S(2)}, u32[]{:S(2)}) collective-permute-start(bf16[256,640]{1,0:T(8,128)(2,1)S(1)} %add.25), channel_id=1, source_target_pairs={{0,4},{2,6},{8,12},{10,14},{13,9},{15,11},{16,20},{18,22},{21,17},... | collective-permute-start | bytes 983048 | tf_op jit(solution)/shard_map/ppermute | solution.py:308
  39.7 1.3 %collective-permute-start.9 = (bf16[256,640]{1,0:T(8,128)(2,1)S(1)}, bf16[256,640]{1,0:T(8,128)(2,1)S(1)}, u32[]{:S(2)}, u32[]{:S(2)}) collective-permute-start(bf16[256,640]{1,0:T(8,128)(2,1)S(1)} %add.25), channel_id=1, source_target_pairs={{0,6},{2,4},{8,14},{10,12},{13,11},{15,9},{16,22},{18,20},{21,19},... | collective-permute-start | bytes 983048 | tf_op jit(solution)/shard_map/ppermute | solution.py:308
  41.0 0.0 collective-permute-done.13
  41.1 4.2 %collective-permute-start.8 = (bf16[256,640]{1,0:T(8,128)(2,1)S(1)}, bf16[256,640]{1,0:T(8,128)(2,1)S(1)}, u32[]{:S(2)}, u32[]{:S(2)}) collective-permute-start(bf16[256,640]{1,0:T(8,128)(2,1)S(1)} %add.25), channel_id=1, source_target_pairs={{0,2},{2,0},{5,7},{7,5},{8,10},{10,8},{13,15},{15,13},{16,18},{18,... | collective-permute-start | bytes 983048 | tf_op jit(solution)/shard_map/ppermute | solution.py:308
  45.3 0.0 collective-permute-done.12
  45.3 1.5 %collective-permute-done.11 = bf16[256,640]{1,0:T(8,128)(2,1)S(1)} collective-permute-done((bf16[256,640]{1,0:T(8,128)(2,1)S(1)}, bf16[256,640]{1,0:T(8,128)(2,1)S(1)}, u32[]{:S(2)}, u32[]{:S(2)}) %collective-permute-start.11) | collective-permute-done | bytes 327712 | tf_op jit(solution)/shard_map/ppermute | solution.py:308
  46.8 0.1 add.28.refs_0_
  46.9 0.1 add.29.refs_1_
  47.0 1.2 %project.2.keyval = bf16[512,1280]{1,0:T(8,128)(2,1)S(1)} custom-call(bf16[640,1280]{1,0:T(8,128)(2,1)S(1)} %copy-done, bf16[256,640]{1,0:T(8,128)(2,1)S(1)} %add.28.refs_0_, bf16[256,640]{1,0:T(8,128)(2,1)S(1)} %add.29.refs_1_), custom_call_target="tpu_custom_call" | custom-call | flops 1 | bytes 1 | tf_op jit(solution)/shard_map/project/pallas_call | solution.py:202
  48.2 0.1 collective-permute-start.15
  48.2 3.4 %attend.3 = (f32[512,640]{1,0:T(8,128)S(1)}, f32[512,640]{1,0:T(8,128)S(1)}, f32[512,640]{1,0:T(8,128)S(1)}) custom-call(bf16[512,640]{1,0:T(8,128)(2,1)S(1)} %get-tuple-element.43.queries_ref, bf16[512,1280]{1,0:T(8,128)(2,1)S(1)} %project.2.keyval), custom_call_target="tpu_custom_call" | custom-call | flops 1 | bytes 1 | tf_op jit(solution)/shard_map/attend/pallas_call | solution.py:283
  51.6 0.0 collective-permute-done.10
  51.6 2.2 %collective-permute-done.8 = bf16[256,640]{1,0:T(8,128)(2,1)S(1)} collective-permute-done((bf16[256,640]{1,0:T(8,128)(2,1)S(1)}, bf16[256,640]{1,0:T(8,128)(2,1)S(1)}, u32[]{:S(2)}, u32[]{:S(2)}) %collective-permute-start.8) | collective-permute-done | bytes 327712 | tf_op jit(solution)/shard_map/ppermute | solution.py:308
  53.8 0.1 add.30.refs_0_
  53.9 0.1 add.31.refs_1_
  54.0 1.2 %project.3.keyval = bf16[512,1280]{1,0:T(8,128)(2,1)S(1)} custom-call(bf16[640,1280]{1,0:T(8,128)(2,1)S(1)} %copy-done, bf16[256,640]{1,0:T(8,128)(2,1)S(1)} %add.30.refs_0_, bf16[256,640]{1,0:T(8,128)(2,1)S(1)} %add.31.refs_1_), custom_call_target="tpu_custom_call" | custom-call | flops 1 | bytes 1 | tf_op jit(solution)/shard_map/project/pallas_call | solution.py:202
  55.2 0.1 collective-permute-start.14
  55.3 3.4 %attend.4 = (f32[512,640]{1,0:T(8,128)S(1)}, f32[512,640]{1,0:T(8,128)S(1)}, f32[512,640]{1,0:T(8,128)S(1)}) custom-call(bf16[512,640]{1,0:T(8,128)(2,1)S(1)} %get-tuple-element.43.queries_ref, bf16[512,1280]{1,0:T(8,128)(2,1)S(1)} %collective-permute-done.15.keyval), custom_call_target="tpu_custom_call" | custom-call | flops 1 | bytes 1 | tf_op jit(solution)/shard_map/attend/pallas_call | solution.py:283
  58.6 0.0 copy-start.2
  58.7 3.6 %attend.5 = (f32[512,640]{1,0:T(8,128)S(1)}, f32[512,640]{1,0:T(8,128)S(1)}, f32[512,640]{1,0:T(8,128)S(1)}) custom-call(bf16[512,640]{1,0:T(8,128)(2,1)S(1)} %get-tuple-element.43.queries_ref, bf16[512,1280]{1,0:T(8,128)(2,1)S(1)} %project.3.keyval), custom_call_target="tpu_custom_call" | custom-call | flops 1 | bytes 1 | tf_op jit(solution)/shard_map/attend/pallas_call | solution.py:283
  62.3 5.4 %join.1 = bf16[512,640]{1,0:T(8,128)(2,1)} custom-call(bf16[512,640]{1,0:T(8,128)(2,1)S(1)} %get-tuple-element.43.queries_ref, bf16[512,1280]{1,0:T(8,128)(2,1)S(1)} %collective-permute-done.14.keyval, f32[512,640]{1,0:T(8,128)S(1)} %get-tuple-element.51.refs_0_, f32[512,640]{1,0:T(8,128)S(1)} %get-tuple-element.52.refs_1_, ...), custom_call_target="tpu_custom_call" | custom-call | flops 1 | bytes 1 | tf_op jit(solution)/shard_map/join/pallas_call | solution.py:283
  (16 shorter events, 0.1 us)
Async XLA Ops:
  0.0 18.4 %slice-start = ((s8[7372800]{0:T(1024)(128)(4,1)}), s8[4194304]{0:T(1024)(128)(4,1)S(1)}, s32[]{:S(2)}) async-start(s8[7372800]{0:T(1024)(128)(4,1)} %bitcast.4), calls=%async_computation | async-start | bytes 8388608
  5.1 11.9 %collective-permute-start.5 = (bf16[256,640]{1,0:T(8,128)(2,1)S(1)}, bf16[256,640]{1,0:T(8,128)(2,1)S(1)}, u32[]{:S(2)}, u32[]{:S(2)}) collective-permute-start(bf16[256,640]{1,0:T(8,128)(2,1)S(1)} %get-tuple-element.42.refs_1_), channel_id=1, source_target_pairs={{1,5},{3,7}} | collective-permute-start | bytes 983048 | tf_op jit(solution)/shard_map/ppermute | solution.py:308
  5.8 4.3 %collective-permute-start = (bf16[32,640]{1,0:T(8,128)(2,1)S(1)}, bf16[32,640]{1,0:T(8,128)(2,1)S(1)}, u32[]{:S(2)}, u32[]{:S(2)}) collective-permute-start(bf16[32,640]{1,0:T(8,128)(2,1)S(1)} %get-tuple-element.38), channel_id=1, source_target_pairs={{0,1},{1,2},{2,3},{4,5},{5,6},{6,7},{8,9},{9,10},{10,11},{12,13},{... | collective-permute-start | bytes 122888 | tf_op jit(solution)/shard_map/ppermute | solution.py:302
  8.8 4.6 %collective-permute-start.1 = (bf16[32,640]{1,0:T(8,128)(2,1)S(1)}, bf16[32,640]{1,0:T(8,128)(2,1)S(1)}, u32[]{:S(2)}, u32[]{:S(2)}) collective-permute-start(bf16[32,640]{1,0:T(8,128)(2,1)S(1)} %get-tuple-element.39), channel_id=1, source_target_pairs={{1,0},{2,1},{3,2},{5,4},{6,5},{7,6},{9,8},{10,9},{11,10},{13,12},{... | collective-permute-start | bytes 122888 | tf_op jit(solution)/shard_map/ppermute | solution.py:302
  13.4 5.0 %slice-start.1 = ((s8[7372800]{0:T(1024)(128)(4,1)}), s8[3178496]{0:T(1024)(128)(4,1)S(1)}, s32[]{:S(2)}) async-start(s8[7372800]{0:T(1024)(128)(4,1)} %bitcast.4), calls=%async_computation.1 | async-start | bytes 6356992
  13.4 5.0 %copy-start.3 = (bf16[640]{0:T(1024)(128)(2,1)S(1)}, bf16[640]{0:T(1024)(128)(2,1)}, u32[]{:S(2)}) copy-start(bf16[640]{0:T(1024)(128)(2,1)} %bias_ref.1) | copy-start | bytes 3844
  16.2 2.2 %copy-start.1 = (bf16[640,640]{1,0:T(8,128)(2,1)S(1)}, bf16[640,640]{1,0:T(8,128)(2,1)}, u32[]{:S(2)}) copy-start(bf16[640,640]{1,0:T(8,128)(2,1)} %w_query.1) | copy-start | bytes 2457604
  16.2 3.1 %collective-permute-start.2 = (bf16[256,640]{1,0:T(8,128)(2,1)S(1)}, bf16[256,640]{1,0:T(8,128)(2,1)S(1)}, u32[]{:S(2)}, u32[]{:S(2)}) collective-permute-start(bf16[256,640]{1,0:T(8,128)(2,1)S(1)} %outer.1.refs_0_), channel_id=1, source_target_pairs={{1,5},{3,7}} | collective-permute-start | bytes 983048 | tf_op jit(solution)/shard_map/ppermute | solution.py:308
  17.1 5.9 %collective-permute-start.6 = (bf16[256,640]{1,0:T(8,128)(2,1)S(1)}, bf16[256,640]{1,0:T(8,128)(2,1)S(1)}, u32[]{:S(2)}, u32[]{:S(2)}) collective-permute-start(bf16[256,640]{1,0:T(8,128)(2,1)S(1)} %broadcast_select_fusion), channel_id=1, source_target_pairs={{0,16},{5,21},{2,18},{7,23}} | collective-permute-start | bytes 983048 | tf_op jit(solution)/shard_map/ppermute | solution.py:308
  19.3 8.1 %collective-permute-start.3 = (bf16[256,640]{1,0:T(8,128)(2,1)S(1)}, bf16[256,640]{1,0:T(8,128)(2,1)S(1)}, u32[]{:S(2)}, u32[]{:S(2)}) collective-permute-start(bf16[256,640]{1,0:T(8,128)(2,1)S(1)} %broadcast_select_fusion.1), channel_id=1, source_target_pairs={{0,16},{5,21},{2,18},{7,23}} | collective-permute-start | bytes 983048 | tf_op jit(solution)/shard_map/ppermute | solution.py:308
  23.0 7.9 %collective-permute-start.7 = (bf16[256,640]{1,0:T(8,128)(2,1)S(1)}, bf16[256,640]{1,0:T(8,128)(2,1)S(1)}, u32[]{:S(2)}, u32[]{:S(2)}) collective-permute-start(bf16[256,640]{1,0:T(8,128)(2,1)S(1)} %add.26), channel_id=1, source_target_pairs={{0,8},{5,13},{2,10},{7,15},{16,24},{21,29},{18,26},{23,31}} | collective-permute-start | bytes 983048 | tf_op jit(solution)/shard_map/ppermute | solution.py:308
  27.5 10.8 %collective-permute-start.4 = (bf16[256,640]{1,0:T(8,128)(2,1)S(1)}, bf16[256,640]{1,0:T(8,128)(2,1)S(1)}, u32[]{:S(2)}, u32[]{:S(2)}) collective-permute-start(bf16[256,640]{1,0:T(8,128)(2,1)S(1)} %add.24), channel_id=1, source_target_pairs={{0,8},{5,13},{2,10},{7,15},{16,24},{21,29},{18,26},{23,31}} | collective-permute-start | bytes 983048 | tf_op jit(solution)/shard_map/ppermute | solution.py:308
  31.0 15.9 %copy-start = (bf16[640,1280]{1,0:T(8,128)(2,1)S(1)}, bf16[640,1280]{1,0:T(8,128)(2,1)}, u32[]{:S(2)}) copy-start(bf16[640,1280]{1,0:T(8,128)(2,1)} %w_keyval.3) | copy-start | bytes 4915204
  31.0 10.0 %collective-permute-start.13 = (bf16[256,640]{1,0:T(8,128)(2,1)S(1)}, bf16[256,640]{1,0:T(8,128)(2,1)S(1)}, u32[]{:S(2)}, u32[]{:S(2)}) collective-permute-start(bf16[256,640]{1,0:T(8,128)(2,1)S(1)} %add.27), channel_id=1, source_target_pairs={{0,4},{2,6},{8,12},{10,14},{13,9},{15,11},{16,20},{18,22},{21,17},... | collective-permute-start | bytes 983048 | tf_op jit(solution)/shard_map/ppermute | solution.py:308
  32.5 12.8 %collective-permute-start.12 = (bf16[256,640]{1,0:T(8,128)(2,1)S(1)}, bf16[256,640]{1,0:T(8,128)(2,1)S(1)}, u32[]{:S(2)}, u32[]{:S(2)}) collective-permute-start(bf16[256,640]{1,0:T(8,128)(2,1)S(1)} %add.27), channel_id=1, source_target_pairs={{0,6},{2,4},{8,14},{10,12},{13,11},{15,9},{16,22},{18,20},{21,19},... | collective-permute-start | bytes 983048 | tf_op jit(solution)/shard_map/ppermute | solution.py:308
  33.8 13.0 %collective-permute-start.11 = (bf16[256,640]{1,0:T(8,128)(2,1)S(1)}, bf16[256,640]{1,0:T(8,128)(2,1)S(1)}, u32[]{:S(2)}, u32[]{:S(2)}) collective-permute-start(bf16[256,640]{1,0:T(8,128)(2,1)S(1)} %add.27), channel_id=1, source_target_pairs={{0,2},{2,0},{5,7},{7,5},{8,10},{10,8},{13,15},{15,13},{16,18},{18,... | collective-permute-start | bytes 983048 | tf_op jit(solution)/shard_map/ppermute | solution.py:308
  38.4 13.2 %collective-permute-start.10 = (bf16[256,640]{1,0:T(8,128)(2,1)S(1)}, bf16[256,640]{1,0:T(8,128)(2,1)S(1)}, u32[]{:S(2)}, u32[]{:S(2)}) collective-permute-start(bf16[256,640]{1,0:T(8,128)(2,1)S(1)} %add.25), channel_id=1, source_target_pairs={{0,4},{2,6},{8,12},{10,14},{13,9},{15,11},{16,20},{18,22},{21,17},... | collective-permute-start | bytes 983048 | tf_op jit(solution)/shard_map/ppermute | solution.py:308
  39.7 11.9 %collective-permute-start.9 = (bf16[256,640]{1,0:T(8,128)(2,1)S(1)}, bf16[256,640]{1,0:T(8,128)(2,1)S(1)}, u32[]{:S(2)}, u32[]{:S(2)}) collective-permute-start(bf16[256,640]{1,0:T(8,128)(2,1)S(1)} %add.25), channel_id=1, source_target_pairs={{0,6},{2,4},{8,14},{10,12},{13,11},{15,9},{16,22},{18,20},{21,19},... | collective-permute-start | bytes 983048 | tf_op jit(solution)/shard_map/ppermute | solution.py:308
  41.1 12.7 %collective-permute-start.8 = (bf16[256,640]{1,0:T(8,128)(2,1)S(1)}, bf16[256,640]{1,0:T(8,128)(2,1)S(1)}, u32[]{:S(2)}, u32[]{:S(2)}) collective-permute-start(bf16[256,640]{1,0:T(8,128)(2,1)S(1)} %add.25), channel_id=1, source_target_pairs={{0,2},{2,0},{5,7},{7,5},{8,10},{10,8},{13,15},{15,13},{16,18},{18,... | collective-permute-start | bytes 983048 | tf_op jit(solution)/shard_map/ppermute | solution.py:308
  48.2 7.1 %collective-permute-start.15 = (bf16[512,1280]{1,0:T(8,128)(2,1)S(1)}, bf16[512,1280]{1,0:T(8,128)(2,1)S(1)}, u32[]{:S(2)}, u32[]{:S(2)}) collective-permute-start(bf16[512,1280]{1,0:T(8,128)(2,1)S(1)} %project.2.keyval), channel_id=1, source_target_pairs={{0,1},{1,0},{2,3},{3,2},{4,5},{5,4},{6,7},{7,6},{8,9},{9,8},{10,11... | collective-permute-start | bytes 3932168 | tf_op jit(solution)/shard_map/ppermute | solution.py:308
  55.2 7.1 %collective-permute-start.14 = (bf16[512,1280]{1,0:T(8,128)(2,1)S(1)}, bf16[512,1280]{1,0:T(8,128)(2,1)S(1)}, u32[]{:S(2)}, u32[]{:S(2)}) collective-permute-start(bf16[512,1280]{1,0:T(8,128)(2,1)S(1)} %project.3.keyval), channel_id=1, source_target_pairs={{0,1},{1,0},{2,3},{3,2},{4,5},{5,4},{6,7},{7,6},{8,9},{9,8},{10,11... | collective-permute-start | bytes 3932168 | tf_op jit(solution)/shard_map/ppermute | solution.py:308
  58.6 3.7 %copy-start.2 = (bf16[640,640]{1,0:T(8,128)(2,1)S(1)}, bf16[640,640]{1,0:T(8,128)(2,1)}, u32[]{:S(2)}) copy-start(bf16[640,640]{1,0:T(8,128)(2,1)} %refs_10_.1) | copy-start | bytes 2457604

commit v7 on v6

--- a/solution.py
+++ b/solution.py
@@ -369,11 +369,11 @@
     parts0 = (parts0[2], parts0[1], parts0[0])
     held1 = ordered(held1, held0)
     parts1 = exchange(held1)
-    parts1 = (parts1[2], parts1[1], parts1[0])
+    parts1 = (parts1[1], parts1[2], parts1[0])
     here0 = keyval_of(own_side(held0, [ordered(parts0, held1)[i] for i in (2, 1, 0)]))
     there0 = swap_cores(here0)
     look0 = look(here0)
-    here1 = keyval_of(own_side(held1, [ordered(parts1, look0)[i] for i in (2, 1, 0)]))
+    here1 = keyval_of(own_side(held1, [ordered(parts1, look0)[i] for i in (2, 0, 1)]))
     there1 = swap_cores(here1)
     look1 = look(ordered(there0, look0, here1))
     look2 = look(ordered(here1, look1))

time: 68.1 us -> 67.3 us (0.988)
  waiting for transfers between devices: 12.2 us -> 8.99 us
  starting transfers between devices: 27.5 us -> 29.2 us
    ppermute x14, waiting for transfers between devices: 8.95 us -> 5.7 us  [permute(): return lax.ppermute(value, ('frame', 'band'), flat)]
    ppermute x14, starting transfers between devices: 23.2 us -> 25 us  [permute(): return lax.ppermute(value, ('frame', 'band'), flat)]
  transfers between devices with their start and end apart: 16 -> 16, of which waited for: 6 -> 5; matrix products, arithmetic and copies ran while one was open for 1% -> 1% of each run, Pallas kernels for 24% -> 25%
where the time goes in v7:
time: 67.3 us; the launch traced here: 66.3 us
  starting transfers between devices  29.2 us (43%)
  Pallas kernels  26.9 us (40%)
  waiting for transfers between devices  8.99 us (13%)
  other arithmetic  0.76 us (1%)
    ppermute x14, starting transfers between devices, permute(): return lax.ppermute(value, ('frame', 'band'), flat)  25 us
    pallas_call x4, Pallas kernels, attend(): pl.pallas_call(functools.partial(attend_kernel, len(parts), last), out_sh...  15.8 us
    ppermute x14, waiting for transfers between devices, permute(): return lax.ppermute(value, ('frame', 'band'), flat)  5.7 us
    pallas_call x1, Pallas kernels, convolve_inner(): pl.pallas_call(functools.partial(inner_kernel, width, inner), out_shape=(...  5.12 us
    ppermute x1, waiting for transfers between devices, from_edges(): lax.ppermute(top, 'band', backward)  3.28 us
    ppermute x1, starting transfers between devices, from_edges(): lax.ppermute(bottom, 'band', forward)  2.98 us
    pallas_call x1, Pallas kernels, convolve_outer(): pl.pallas_call(functools.partial(outer_kernel, width, outer), out_shape=j...  2.74 us
    pallas_call x2, Pallas kernels, project(): pl.pallas_call(functools.partial(project_kernel, len(pieces)), out_shape=...  2.37 us
  transfers between devices with their start and end apart: 16, of which 5 were waited for; matrix products, arithmetic and copies ran while one was open for 1% of the time, Pallas kernels for 25%

profile of v7, /device:TPU:0, one launch (start us, length us, event | category | flops | bytes accessed | tf_op | source)
XLA Modules:
  0.0 66.3 jit_solution(2201229306611545168)
XLA Ops:
  0.0 5.1 %inner.1 = (bf16[256,640]{1,0:T(8,128)(2,1)S(1)}, bf16[512,640]{1,0:T(8,128)(2,1)S(1)}, bf16[32,640]{1,0:T(8,128)(2,1)S(1)}, bf16[32,640]{1,0:T(8,128)(2,1)S(1)}...) custom-call(bf16[512,640]{1,0:T(8,128)(2,1)} %bitcast.7, bf16[3,1920,640]{2,1,0:T(8,128)(2,1)} %bitcast.3, ...), custom_call_target="tpu_custom_call" | custom-call | flops 1 | bytes 1 | tf_op jit(solution)/shard_map/inner/pallas_call | solution.py:105
  5.1 0.7 %collective-permute-start.5 = (bf16[256,640]{1,0:T(8,128)(2,1)S(1)}, bf16[256,640]{1,0:T(8,128)(2,1)S(1)}, u32[]{:S(2)}, u32[]{:S(2)}) collective-permute-start(bf16[256,640]{1,0:T(8,128)(2,1)S(1)} %get-tuple-element.42.refs_1_), channel_id=1, source_target_pairs={{1,5},{3,7}} | collective-permute-start | bytes 983048 | tf_op jit(solution)/shard_map/ppermute | solution.py:308
  5.8 3.0 %collective-permute-start = (bf16[32,640]{1,0:T(8,128)(2,1)S(1)}, bf16[32,640]{1,0:T(8,128)(2,1)S(1)}, u32[]{:S(2)}, u32[]{:S(2)}) collective-permute-start(bf16[32,640]{1,0:T(8,128)(2,1)S(1)} %get-tuple-element.38), channel_id=1, source_target_pairs={{0,1},{1,2},{2,3},{4,5},{5,6},{6,7},{8,9},{9,10},{10,11},{12,13},{... | collective-permute-start | bytes 122888 | tf_op jit(solution)/shard_map/ppermute | solution.py:302
  8.8 1.3 %collective-permute-start.1 = (bf16[32,640]{1,0:T(8,128)(2,1)S(1)}, bf16[32,640]{1,0:T(8,128)(2,1)S(1)}, u32[]{:S(2)}, u32[]{:S(2)}) collective-permute-start(bf16[32,640]{1,0:T(8,128)(2,1)S(1)} %get-tuple-element.39), channel_id=1, source_target_pairs={{1,0},{2,1},{3,2},{5,4},{6,5},{7,6},{9,8},{10,9},{11,10},{13,12},{... | collective-permute-start | bytes 122888 | tf_op jit(solution)/shard_map/ppermute | solution.py:302
  10.1 3.3 %collective-permute-done.1.high_ref = bf16[32,640]{1,0:T(8,128)(2,1)S(1)} collective-permute-done((bf16[32,640]{1,0:T(8,128)(2,1)S(1)}, bf16[32,640]{1,0:T(8,128)(2,1)S(1)}, u32[]{:S(2)}, u32[]{:S(2)}) %collective-permute-start.1) | collective-permute-done | bytes 40992 | tf_op jit(solution)/shard_map/ppermute | solution.py:302
  13.4 2.7 %outer.1.refs_0_ = bf16[256,640]{1,0:T(8,128)(2,1)S(1)} custom-call(bf16[512,640]{1,0:T(8,128)(2,1)S(1)} %get-tuple-element.37.x_ref, bf16[32,640]{1,0:T(8,128)(2,1)S(1)} %collective-permute-done.low_ref, bf16[32,640]{1,0:T(8,128)(2,1)S(1)} %collective-permute-done.1.high_ref, bf16[3,1920,640]{2,1,0:T(8,128)(2,1)S(1)} %get-tuple-element.40.weight, ...), custom_call_target="tpu_custom_call" | custom-call | flops 1 | bytes 1 | tf_op jit(solution)/shard_map/outer/pallas_call | solution.py:134
  16.2 0.0 copy-start.1
  16.2 0.8 %collective-permute-start.2 = (bf16[256,640]{1,0:T(8,128)(2,1)S(1)}, bf16[256,640]{1,0:T(8,128)(2,1)S(1)}, u32[]{:S(2)}, u32[]{:S(2)}) collective-permute-start(bf16[256,640]{1,0:T(8,128)(2,1)S(1)} %outer.1.refs_0_), channel_id=1, source_target_pairs={{1,5},{3,7}} | collective-permute-start | bytes 983048 | tf_op jit(solution)/shard_map/ppermute | solution.py:308
  17.0 0.0 collective-permute-done.5
  17.0 0.1 broadcast_select_fusion
  17.1 1.3 %collective-permute-start.6 = (bf16[256,640]{1,0:T(8,128)(2,1)S(1)}, bf16[256,640]{1,0:T(8,128)(2,1)S(1)}, u32[]{:S(2)}, u32[]{:S(2)}) collective-permute-start(bf16[256,640]{1,0:T(8,128)(2,1)S(1)} %broadcast_select_fusion), channel_id=1, source_target_pairs={{0,16},{5,21},{2,18},{7,23}} | collective-permute-start | bytes 983048 | tf_op jit(solution)/shard_map/ppermute | solution.py:308
  18.4 0.8 %ask.1 = (bf16[512,640]{1,0:T(8,128)(2,1)S(1)}, bf16[512,640]{1,0:T(8,128)(2,1)S(1)}) custom-call(bf16[640,640]{1,0:T(8,128)(2,1)S(1)} %copy-done.1, bf16[512,640]{1,0:T(8,128)(2,1)S(1)} %get-tuple-element.37.x_ref, bf16[32,640]{1,0:T(8,128)(2,1)S(1)} %collective-permute-done.low_ref, bf16[32,640]{1,0:T(8,128)(2,1)S(1)} %collective-permute-done.1.high_ref, ...), custom_call_target="tpu_custom_call" | custom-call | flops 1 | bytes 1 | tf_op jit(solution)/shard_map/ask/pallas_call | solution.py:178
  19.3 0.0 collective-permute-done.2
  19.3 3.6 %collective-permute-start.3 = (bf16[256,640]{1,0:T(8,128)(2,1)S(1)}, bf16[256,640]{1,0:T(8,128)(2,1)S(1)}, u32[]{:S(2)}, u32[]{:S(2)}) collective-permute-start(bf16[256,640]{1,0:T(8,128)(2,1)S(1)} %broadcast_select_fusion.1), channel_id=1, source_target_pairs={{0,16},{5,21},{2,18},{7,23}} | collective-permute-start | bytes 983048 | tf_op jit(solution)/shard_map/ppermute | solution.py:308
  22.9 0.1 collective-permute-done.6
  22.9 0.1 add.26
  23.0 1.3 %collective-permute-start.7 = (bf16[256,640]{1,0:T(8,128)(2,1)S(1)}, bf16[256,640]{1,0:T(8,128)(2,1)S(1)}, u32[]{:S(2)}, u32[]{:S(2)}) collective-permute-start(bf16[256,640]{1,0:T(8,128)(2,1)S(1)} %add.26), channel_id=1, source_target_pairs={{0,8},{5,13},{2,10},{7,15},{16,24},{21,29},{18,26},{23,31}} | collective-permute-start | bytes 983048 | tf_op jit(solution)/shard_map/ppermute | solution.py:308
  24.3 3.1 %collective-permute-done.3 = bf16[256,640]{1,0:T(8,128)(2,1)S(1)} collective-permute-done((bf16[256,640]{1,0:T(8,128)(2,1)S(1)}, bf16[256,640]{1,0:T(8,128)(2,1)S(1)}, u32[]{:S(2)}, u32[]{:S(2)}) %collective-permute-start.3) | collective-permute-done | bytes 327712 | tf_op jit(solution)/shard_map/ppermute | solution.py:308
  27.4 0.1 add.24
  27.5 1.3 %collective-permute-start.4 = (bf16[256,640]{1,0:T(8,128)(2,1)S(1)}, bf16[256,640]{1,0:T(8,128)(2,1)S(1)}, u32[]{:S(2)}, u32[]{:S(2)}) collective-permute-start(bf16[256,640]{1,0:T(8,128)(2,1)S(1)} %add.24), channel_id=1, source_target_pairs={{0,8},{5,13},{2,10},{7,15},{16,24},{21,29},{18,26},{23,31}} | collective-permute-start | bytes 983048 | tf_op jit(solution)/shard_map/ppermute | solution.py:308
  28.8 2.1 %collective-permute-done.7 = bf16[256,640]{1,0:T(8,128)(2,1)S(1)} collective-permute-done((bf16[256,640]{1,0:T(8,128)(2,1)S(1)}, bf16[256,640]{1,0:T(8,128)(2,1)S(1)}, u32[]{:S(2)}, u32[]{:S(2)}) %collective-permute-start.7) | collective-permute-done | bytes 327712 | tf_op jit(solution)/shard_map/ppermute | solution.py:308
  30.9 0.1 add.27
  31.0 0.0 copy-start
  31.0 1.4 %collective-permute-start.13 = (bf16[256,640]{1,0:T(8,128)(2,1)S(1)}, bf16[256,640]{1,0:T(8,128)(2,1)S(1)}, u32[]{:S(2)}, u32[]{:S(2)}) collective-permute-start(bf16[256,640]{1,0:T(8,128)(2,1)S(1)} %add.27), channel_id=1, source_target_pairs={{0,4},{2,6},{8,12},{10,14},{13,9},{15,11},{16,20},{18,22},{21,17},... | collective-permute-start | bytes 983048 | tf_op jit(solution)/shard_map/ppermute | solution.py:308
  32.5 1.3 %collective-permute-start.12 = (bf16[256,640]{1,0:T(8,128)(2,1)S(1)}, bf16[256,640]{1,0:T(8,128)(2,1)S(1)}, u32[]{:S(2)}, u32[]{:S(2)}) collective-permute-start(bf16[256,640]{1,0:T(8,128)(2,1)S(1)} %add.27), channel_id=1, source_target_pairs={{0,6},{2,4},{8,14},{10,12},{13,11},{15,9},{16,22},{18,20},{21,19},... | collective-permute-start | bytes 983048 | tf_op jit(solution)/shard_map/ppermute | solution.py:308
  33.8 4.5 %collective-permute-start.11 = (bf16[256,640]{1,0:T(8,128)(2,1)S(1)}, bf16[256,640]{1,0:T(8,128)(2,1)S(1)}, u32[]{:S(2)}, u32[]{:S(2)}) collective-permute-start(bf16[256,640]{1,0:T(8,128)(2,1)S(1)} %add.27), channel_id=1, source_target_pairs={{0,2},{2,0},{5,7},{7,5},{8,10},{10,8},{13,15},{15,13},{16,18},{18,... | collective-permute-start | bytes 983048 | tf_op jit(solution)/shard_map/ppermute | solution.py:308
  38.3 0.0 collective-permute-done.4
  38.3 0.1 add.25
  38.4 1.3 %collective-permute-start.10 = (bf16[256,640]{1,0:T(8,128)(2,1)S(1)}, bf16[256,640]{1,0:T(8,128)(2,1)S(1)}, u32[]{:S(2)}, u32[]{:S(2)}) collective-permute-start(bf16[256,640]{1,0:T(8,128)(2,1)S(1)} %add.25), channel_id=1, source_target_pairs={{0,4},{2,6},{8,12},{10,14},{13,9},{15,11},{16,20},{18,22},{21,17},... | collective-permute-start | bytes 983048 | tf_op jit(solution)/shard_map/ppermute | solution.py:308
  39.7 1.9 %collective-permute-start.9 = (bf16[256,640]{1,0:T(8,128)(2,1)S(1)}, bf16[256,640]{1,0:T(8,128)(2,1)S(1)}, u32[]{:S(2)}, u32[]{:S(2)}) collective-permute-start(bf16[256,640]{1,0:T(8,128)(2,1)S(1)} %add.25), channel_id=1, source_target_pairs={{0,2},{2,0},{5,7},{7,5},{8,10},{10,8},{13,15},{15,13},{16,18},{18,... | collective-permute-start | bytes 983048 | tf_op jit(solution)/shard_map/ppermute | solution.py:308
  41.7 5.3 %collective-permute-start.8 = (bf16[256,640]{1,0:T(8,128)(2,1)S(1)}, bf16[256,640]{1,0:T(8,128)(2,1)S(1)}, u32[]{:S(2)}, u32[]{:S(2)}) collective-permute-start(bf16[256,640]{1,0:T(8,128)(2,1)S(1)} %add.25), channel_id=1, source_target_pairs={{0,6},{2,4},{8,14},{10,12},{13,11},{15,9},{16,22},{18,20},{21,19},... | collective-permute-start | bytes 983048 | tf_op jit(solution)/shard_map/ppermute | solution.py:308
  47.0 0.1 add.28.refs_0_
  47.1 0.1 add.29.refs_1_
  47.2 1.2 %project.2.keyval = bf16[512,1280]{1,0:T(8,128)(2,1)S(1)} custom-call(bf16[640,1280]{1,0:T(8,128)(2,1)S(1)} %copy-done, bf16[256,640]{1,0:T(8,128)(2,1)S(1)} %add.28.refs_0_, bf16[256,640]{1,0:T(8,128)(2,1)S(1)} %add.29.refs_1_), custom_call_target="tpu_custom_call" | custom-call | flops 1 | bytes 1 | tf_op jit(solution)/shard_map/project/pallas_call | solution.py:202
  48.4 0.1 collective-permute-start.15
  48.4 3.4 %attend.3 = (f32[512,640]{1,0:T(8,128)S(1)}, f32[512,640]{1,0:T(8,128)S(1)}, f32[512,640]{1,0:T(8,128)S(1)}) custom-call(bf16[512,640]{1,0:T(8,128)(2,1)S(1)} %get-tuple-element.43.queries_ref, bf16[512,1280]{1,0:T(8,128)(2,1)S(1)} %project.2.keyval), custom_call_target="tpu_custom_call" | custom-call | flops 1 | bytes 1 | tf_op jit(solution)/shard_map/attend/pallas_call | solution.py:283
  51.8 0.0 collective-permute-done.10
  51.8 0.0 collective-permute-done.9
  51.8 0.4 collective-permute-done.8
  52.3 0.1 add.30.refs_0_
  52.3 0.1 add.31.refs_1_
  52.4 1.2 %project.3.keyval = bf16[512,1280]{1,0:T(8,128)(2,1)S(1)} custom-call(bf16[640,1280]{1,0:T(8,128)(2,1)S(1)} %copy-done, bf16[256,640]{1,0:T(8,128)(2,1)S(1)} %add.30.refs_0_, bf16[256,640]{1,0:T(8,128)(2,1)S(1)} %add.31.refs_1_), custom_call_target="tpu_custom_call" | custom-call | flops 1 | bytes 1 | tf_op jit(solution)/shard_map/project/pallas_call | solution.py:202
  53.6 0.2 collective-permute-start.14
  53.8 3.4 %attend.4 = (f32[512,640]{1,0:T(8,128)S(1)}, f32[512,640]{1,0:T(8,128)S(1)}, f32[512,640]{1,0:T(8,128)S(1)}) custom-call(bf16[512,640]{1,0:T(8,128)(2,1)S(1)} %get-tuple-element.43.queries_ref, bf16[512,1280]{1,0:T(8,128)(2,1)S(1)} %collective-permute-done.15.keyval), custom_call_target="tpu_custom_call" | custom-call | flops 1 | bytes 1 | tf_op jit(solution)/shard_map/attend/pallas_call | solution.py:283
  57.2 0.0 copy-start.2
  57.2 3.6 %attend.5 = (f32[512,640]{1,0:T(8,128)S(1)}, f32[512,640]{1,0:T(8,128)S(1)}, f32[512,640]{1,0:T(8,128)S(1)}) custom-call(bf16[512,640]{1,0:T(8,128)(2,1)S(1)} %get-tuple-element.43.queries_ref, bf16[512,1280]{1,0:T(8,128)(2,1)S(1)} %project.3.keyval), custom_call_target="tpu_custom_call" | custom-call | flops 1 | bytes 1 | tf_op jit(solution)/shard_map/attend/pallas_call | solution.py:283
  60.8 0.0 collective-permute-done.14.keyval
  60.8 5.4 %join.1 = bf16[512,640]{1,0:T(8,128)(2,1)} custom-call(bf16[512,640]{1,0:T(8,128)(2,1)S(1)} %get-tuple-element.43.queries_ref, bf16[512,1280]{1,0:T(8,128)(2,1)S(1)} %collective-permute-done.14.keyval, f32[512,640]{1,0:T(8,128)S(1)} %get-tuple-element.51.refs_0_, f32[512,640]{1,0:T(8,128)S(1)} %get-tuple-element.52.refs_1_, ...), custom_call_target="tpu_custom_call" | custom-call | flops 1 | bytes 1 | tf_op jit(solution)/shard_map/join/pallas_call | solution.py:283
  (16 shorter events, 0.1 us)
Async XLA Ops:
  0.0 18.4 %slice-start = ((s8[7372800]{0:T(1024)(128)(4,1)}), s8[4194304]{0:T(1024)(128)(4,1)S(1)}, s32[]{:S(2)}) async-start(s8[7372800]{0:T(1024)(128)(4,1)} %bitcast.4), calls=%async_computation | async-start | bytes 8388608
  5.1 11.9 %collective-permute-start.5 = (bf16[256,640]{1,0:T(8,128)(2,1)S(1)}, bf16[256,640]{1,0:T(8,128)(2,1)S(1)}, u32[]{:S(2)}, u32[]{:S(2)}) collective-permute-start(bf16[256,640]{1,0:T(8,128)(2,1)S(1)} %get-tuple-element.42.refs_1_), channel_id=1, source_target_pairs={{1,5},{3,7}} | collective-permute-start | bytes 983048 | tf_op jit(solution)/shard_map/ppermute | solution.py:308
  5.8 4.3 %collective-permute-start = (bf16[32,640]{1,0:T(8,128)(2,1)S(1)}, bf16[32,640]{1,0:T(8,128)(2,1)S(1)}, u32[]{:S(2)}, u32[]{:S(2)}) collective-permute-start(bf16[32,640]{1,0:T(8,128)(2,1)S(1)} %get-tuple-element.38), channel_id=1, source_target_pairs={{0,1},{1,2},{2,3},{4,5},{5,6},{6,7},{8,9},{9,10},{10,11},{12,13},{... | collective-permute-start | bytes 122888 | tf_op jit(solution)/shard_map/ppermute | solution.py:302
  8.8 4.6 %collective-permute-start.1 = (bf16[32,640]{1,0:T(8,128)(2,1)S(1)}, bf16[32,640]{1,0:T(8,128)(2,1)S(1)}, u32[]{:S(2)}, u32[]{:S(2)}) collective-permute-start(bf16[32,640]{1,0:T(8,128)(2,1)S(1)} %get-tuple-element.39), channel_id=1, source_target_pairs={{1,0},{2,1},{3,2},{5,4},{6,5},{7,6},{9,8},{10,9},{11,10},{13,12},{... | collective-permute-start | bytes 122888 | tf_op jit(solution)/shard_map/ppermute | solution.py:302
  13.4 5.0 %slice-start.1 = ((s8[7372800]{0:T(1024)(128)(4,1)}), s8[3178496]{0:T(1024)(128)(4,1)S(1)}, s32[]{:S(2)}) async-start(s8[7372800]{0:T(1024)(128)(4,1)} %bitcast.4), calls=%async_computation.1 | async-start | bytes 6356992
  13.4 5.0 %copy-start.3 = (bf16[640]{0:T(1024)(128)(2,1)S(1)}, bf16[640]{0:T(1024)(128)(2,1)}, u32[]{:S(2)}) copy-start(bf16[640]{0:T(1024)(128)(2,1)} %bias_ref.1) | copy-start | bytes 3844
  16.2 2.2 %copy-start.1 = (bf16[640,640]{1,0:T(8,128)(2,1)S(1)}, bf16[640,640]{1,0:T(8,128)(2,1)}, u32[]{:S(2)}) copy-start(bf16[640,640]{1,0:T(8,128)(2,1)} %w_query.1) | copy-start | bytes 2457604
  16.2 3.1 %collective-permute-start.2 = (bf16[256,640]{1,0:T(8,128)(2,1)S(1)}, bf16[256,640]{1,0:T(8,128)(2,1)S(1)}, u32[]{:S(2)}, u32[]{:S(2)}) collective-permute-start(bf16[256,640]{1,0:T(8,128)(2,1)S(1)} %outer.1.refs_0_), channel_id=1, source_target_pairs={{1,5},{3,7}} | collective-permute-start | bytes 983048 | tf_op jit(solution)/shard_map/ppermute | solution.py:308
  17.1 5.9 %collective-permute-start.6 = (bf16[256,640]{1,0:T(8,128)(2,1)S(1)}, bf16[256,640]{1,0:T(8,128)(2,1)S(1)}, u32[]{:S(2)}, u32[]{:S(2)}) collective-permute-start(bf16[256,640]{1,0:T(8,128)(2,1)S(1)} %broadcast_select_fusion), channel_id=1, source_target_pairs={{0,16},{5,21},{2,18},{7,23}} | collective-permute-start | bytes 983048 | tf_op jit(solution)/shard_map/ppermute | solution.py:308
  19.3 8.1 %collective-permute-start.3 = (bf16[256,640]{1,0:T(8,128)(2,1)S(1)}, bf16[256,640]{1,0:T(8,128)(2,1)S(1)}, u32[]{:S(2)}, u32[]{:S(2)}) collective-permute-start(bf16[256,640]{1,0:T(8,128)(2,1)S(1)} %broadcast_select_fusion.1), channel_id=1, source_target_pairs={{0,16},{5,21},{2,18},{7,23}} | collective-permute-start | bytes 983048 | tf_op jit(solution)/shard_map/ppermute | solution.py:308
  23.0 7.9 %collective-permute-start.7 = (bf16[256,640]{1,0:T(8,128)(2,1)S(1)}, bf16[256,640]{1,0:T(8,128)(2,1)S(1)}, u32[]{:S(2)}, u32[]{:S(2)}) collective-permute-start(bf16[256,640]{1,0:T(8,128)(2,1)S(1)} %add.26), channel_id=1, source_target_pairs={{0,8},{5,13},{2,10},{7,15},{16,24},{21,29},{18,26},{23,31}} | collective-permute-start | bytes 983048 | tf_op jit(solution)/shard_map/ppermute | solution.py:308
  27.5 10.8 %collective-permute-start.4 = (bf16[256,640]{1,0:T(8,128)(2,1)S(1)}, bf16[256,640]{1,0:T(8,128)(2,1)S(1)}, u32[]{:S(2)}, u32[]{:S(2)}) collective-permute-start(bf16[256,640]{1,0:T(8,128)(2,1)S(1)} %add.24), channel_id=1, source_target_pairs={{0,8},{5,13},{2,10},{7,15},{16,24},{21,29},{18,26},{23,31}} | collective-permute-start | bytes 983048 | tf_op jit(solution)/shard_map/ppermute | solution.py:308
  31.0 16.1 %copy-start = (bf16[640,1280]{1,0:T(8,128)(2,1)S(1)}, bf16[640,1280]{1,0:T(8,128)(2,1)}, u32[]{:S(2)}) copy-start(bf16[640,1280]{1,0:T(8,128)(2,1)} %w_keyval.3) | copy-start | bytes 4915204
  31.0 10.6 %collective-permute-start.13 = (bf16[256,640]{1,0:T(8,128)(2,1)S(1)}, bf16[256,640]{1,0:T(8,128)(2,1)S(1)}, u32[]{:S(2)}, u32[]{:S(2)}) collective-permute-start(bf16[256,640]{1,0:T(8,128)(2,1)S(1)} %add.27), channel_id=1, source_target_pairs={{0,4},{2,6},{8,12},{10,14},{13,9},{15,11},{16,20},{18,22},{21,17},... | collective-permute-start | bytes 983048 | tf_op jit(solution)/shard_map/ppermute | solution.py:308
  32.5 14.5 %collective-permute-start.12 = (bf16[256,640]{1,0:T(8,128)(2,1)S(1)}, bf16[256,640]{1,0:T(8,128)(2,1)S(1)}, u32[]{:S(2)}, u32[]{:S(2)}) collective-permute-start(bf16[256,640]{1,0:T(8,128)(2,1)S(1)} %add.27), channel_id=1, source_target_pairs={{0,6},{2,4},{8,14},{10,12},{13,11},{15,9},{16,22},{18,20},{21,19},... | collective-permute-start | bytes 983048 | tf_op jit(solution)/shard_map/ppermute | solution.py:308
  33.8 13.1 %collective-permute-start.11 = (bf16[256,640]{1,0:T(8,128)(2,1)S(1)}, bf16[256,640]{1,0:T(8,128)(2,1)S(1)}, u32[]{:S(2)}, u32[]{:S(2)}) collective-permute-start(bf16[256,640]{1,0:T(8,128)(2,1)S(1)} %add.27), channel_id=1, source_target_pairs={{0,2},{2,0},{5,7},{7,5},{8,10},{10,8},{13,15},{15,13},{16,18},{18,... | collective-permute-start | bytes 983048 | tf_op jit(solution)/shard_map/ppermute | solution.py:308
  38.4 13.4 %collective-permute-start.10 = (bf16[256,640]{1,0:T(8,128)(2,1)S(1)}, bf16[256,640]{1,0:T(8,128)(2,1)S(1)}, u32[]{:S(2)}, u32[]{:S(2)}) collective-permute-start(bf16[256,640]{1,0:T(8,128)(2,1)S(1)} %add.25), channel_id=1, source_target_pairs={{0,4},{2,6},{8,12},{10,14},{13,9},{15,11},{16,20},{18,22},{21,17},... | collective-permute-start | bytes 983048 | tf_op jit(solution)/shard_map/ppermute | solution.py:308
  39.7 12.1 %collective-permute-start.9 = (bf16[256,640]{1,0:T(8,128)(2,1)S(1)}, bf16[256,640]{1,0:T(8,128)(2,1)S(1)}, u32[]{:S(2)}, u32[]{:S(2)}) collective-permute-start(bf16[256,640]{1,0:T(8,128)(2,1)S(1)} %add.25), channel_id=1, source_target_pairs={{0,2},{2,0},{5,7},{7,5},{8,10},{10,8},{13,15},{15,13},{16,18},{18,... | collective-permute-start | bytes 983048 | tf_op jit(solution)/shard_map/ppermute | solution.py:308
  41.7 10.6 %collective-permute-start.8 = (bf16[256,640]{1,0:T(8,128)(2,1)S(1)}, bf16[256,640]{1,0:T(8,128)(2,1)S(1)}, u32[]{:S(2)}, u32[]{:S(2)}) collective-permute-start(bf16[256,640]{1,0:T(8,128)(2,1)S(1)} %add.25), channel_id=1, source_target_pairs={{0,6},{2,4},{8,14},{10,12},{13,11},{15,9},{16,22},{18,20},{21,19},... | collective-permute-start | bytes 983048 | tf_op jit(solution)/shard_map/ppermute | solution.py:308
  48.4 5.4 %collective-permute-start.15 = (bf16[512,1280]{1,0:T(8,128)(2,1)S(1)}, bf16[512,1280]{1,0:T(8,128)(2,1)S(1)}, u32[]{:S(2)}, u32[]{:S(2)}) collective-permute-start(bf16[512,1280]{1,0:T(8,128)(2,1)S(1)} %project.2.keyval), channel_id=1, source_target_pairs={{0,1},{1,0},{2,3},{3,2},{4,5},{5,4},{6,7},{7,6},{8,9},{9,8},{10,11... | collective-permute-start | bytes 3932168 | tf_op jit(solution)/shard_map/ppermute | solution.py:308
  53.6 7.2 %collective-permute-start.14 = (bf16[512,1280]{1,0:T(8,128)(2,1)S(1)}, bf16[512,1280]{1,0:T(8,128)(2,1)S(1)}, u32[]{:S(2)}, u32[]{:S(2)}) collective-permute-start(bf16[512,1280]{1,0:T(8,128)(2,1)S(1)} %project.3.keyval), channel_id=1, source_target_pairs={{0,1},{1,0},{2,3},{3,2},{4,5},{5,4},{6,7},{7,6},{8,9},{9,8},{10,11... | collective-permute-start | bytes 3932168 | tf_op jit(solution)/shard_map/ppermute | solution.py:308
  57.2 3.7 %copy-start.2 = (bf16[640,640]{1,0:T(8,128)(2,1)S(1)}, bf16[640,640]{1,0:T(8,128)(2,1)}, u32[]{:S(2)}) copy-start(bf16[640,640]{1,0:T(8,128)(2,1)} %refs_10_.1) | copy-start | bytes 2457604

commit v8 on v7

--- a/solution.py
+++ b/solution.py
@@ -187,27 +187,28 @@
     )(w_query, x, low, high, weight, bias, *pieces)
 
 
-def project_kernel(piece_count, w_keyval, *refs):
-    pieces, keyval_ref = refs[:piece_count], refs[piece_count]
+def project_kernel(w_keyval, *refs):
+    halves, keyval_ref = refs[:-1], refs[-1]
     start = 0
-    for piece in pieces:
-        stop = start + piece.shape[0]
-        keyval = jnp.dot(piece[...], w_keyval[...], preferred_element_type=jnp.float32)
+    for one, other in zip(halves[::2], halves[1::2]):
+        stop = start + one.shape[0]
+        piece = one[...] + other[...]
+        keyval = jnp.dot(piece, w_keyval[...], preferred_element_type=jnp.float32)
         keyval_ref[start:stop, :] = keyval.astype(jnp.bfloat16)
         start = stop
 
 
 def project(pieces, w_keyval):
-    tokens = sum(piece.shape[0] for piece in pieces)
+    tokens = sum(one.shape[0] for one, _ in pieces)
     return pl.pallas_call(
-        functools.partial(project_kernel, len(pieces)),
+        project_kernel,
         out_shape=jax.ShapeDtypeStruct((tokens, w_keyval.shape[1]), jnp.bfloat16),
-        in_specs=[IN_VMEM] * (len(pieces) + 1),
+        in_specs=[IN_VMEM] * (2 * len(pieces) + 1),
         out_specs=IN_VMEM,
         compiler_params=pltpu.CompilerParams(vmem_limit_bytes=CONV_VMEM_BYTES),
         cost_estimate=QUICK,
         name="project",
-    )(w_keyval, *pieces)
+    )(w_keyval, *(half for piece in pieces for half in piece))
 
 
 def attend_kernel(part_count, last, queries_ref, keyval, *refs):
@@ -357,13 +358,14 @@
 
 def own_side(held, parts):
     beside, diagonal, far = parts
-    return [held + beside, far + diagonal]
+    return [(held, beside), (far, diagonal)]
 
 
 def sees_all(chunks, starts, early, keyval_of, look):
     frames, bands = lax.axis_size("frame"), lax.axis_size("band")
     if frames < 2 or frames & (frames - 1) or bands != 4:
-        return [], keyval_of([lax.all_gather(chunk, ("frame", "band"))[b] for chunk in chunks for b in range(bands)])
+        pieces = [lax.all_gather(chunk, ("frame", "band"))[b] for chunk in chunks for b in range(bands)]
+        return [], keyval_of([(piece, jnp.zeros_like(piece)) for piece in pieces])
     held0, held1 = cast(starts, (*early, starts[1]))
     parts0 = exchange(held0)
     parts0 = (parts0[2], parts0[1], parts0[0])

time: 67.3 us -> 67.1 us (level)
  no operation moved by 1% of the time
where the time goes in v8:
time: 67.1 us; the launch traced here: 66 us
  starting transfers between devices  29.1 us (43%)
  Pallas kernels  26.9 us (40%)
  waiting for transfers between devices  9.19 us (14%)
    ppermute x14, starting transfers between devices, permute(): return lax.ppermute(value, ('frame', 'band'), flat)  24.9 us
    pallas_call x4, Pallas kernels, attend(): pl.pallas_call(functools.partial(attend_kernel, len(parts), last), out_sh...  15.8 us
    ppermute x14, waiting for transfers between devices, permute(): return lax.ppermute(value, ('frame', 'band'), flat)  5.9 us
    pallas_call x1, Pallas kernels, convolve_inner(): pl.pallas_call(functools.partial(inner_kernel, width, inner), out_shape=(...  5.12 us
    ppermute x1, waiting for transfers between devices, from_edges(): lax.ppermute(top, 'band', backward)  3.28 us
    ppermute x1, starting transfers between devices, from_edges(): lax.ppermute(bottom, 'band', forward)  2.98 us
    pallas_call x1, Pallas kernels, convolve_outer(): pl.pallas_call(functools.partial(outer_kernel, width, outer), out_shape=j...  2.74 us
    pallas_call x2, Pallas kernels, project(): pl.pallas_call(project_kernel, out_shape=jax.ShapeDtypeStruct((tokens, w_...  2.37 us
  transfers between devices with their start and end apart: 16, of which 5 were waited for; matrix products, arithmetic and copies ran while one was open for 1% of the time, Pallas kernels for 25%

profile of v8, /device:TPU:0, one launch (start us, length us, event | category | flops | bytes accessed | tf_op | source)
XLA Modules:
  0.0 66.0 jit_solution(15728549398535422228)
XLA Ops:
  0.0 5.1 %inner.1 = (bf16[256,640]{1,0:T(8,128)(2,1)S(1)}, bf16[512,640]{1,0:T(8,128)(2,1)S(1)}, bf16[32,640]{1,0:T(8,128)(2,1)S(1)}, bf16[32,640]{1,0:T(8,128)(2,1)S(1)}...) custom-call(bf16[512,640]{1,0:T(8,128)(2,1)} %bitcast.7, bf16[3,1920,640]{2,1,0:T(8,128)(2,1)} %bitcast.3, ...), custom_call_target="tpu_custom_call" | custom-call | flops 1 | bytes 1 | tf_op jit(solution)/shard_map/inner/pallas_call | solution.py:105
  5.1 0.7 %collective-permute-start.5 = (bf16[256,640]{1,0:T(8,128)(2,1)S(1)}, bf16[256,640]{1,0:T(8,128)(2,1)S(1)}, u32[]{:S(2)}, u32[]{:S(2)}) collective-permute-start(bf16[256,640]{1,0:T(8,128)(2,1)S(1)} %get-tuple-element.42.refs_1_), channel_id=1, source_target_pairs={{1,5},{3,7}} | collective-permute-start | bytes 983048 | tf_op jit(solution)/shard_map/ppermute | solution.py:309
  5.8 3.0 %collective-permute-start = (bf16[32,640]{1,0:T(8,128)(2,1)S(1)}, bf16[32,640]{1,0:T(8,128)(2,1)S(1)}, u32[]{:S(2)}, u32[]{:S(2)}) collective-permute-start(bf16[32,640]{1,0:T(8,128)(2,1)S(1)} %get-tuple-element.38), channel_id=1, source_target_pairs={{0,1},{1,2},{2,3},{4,5},{5,6},{6,7},{8,9},{9,10},{10,11},{12,13},{... | collective-permute-start | bytes 122888 | tf_op jit(solution)/shard_map/ppermute | solution.py:303
  8.8 1.3 %collective-permute-start.1 = (bf16[32,640]{1,0:T(8,128)(2,1)S(1)}, bf16[32,640]{1,0:T(8,128)(2,1)S(1)}, u32[]{:S(2)}, u32[]{:S(2)}) collective-permute-start(bf16[32,640]{1,0:T(8,128)(2,1)S(1)} %get-tuple-element.39), channel_id=1, source_target_pairs={{1,0},{2,1},{3,2},{5,4},{6,5},{7,6},{9,8},{10,9},{11,10},{13,12},{... | collective-permute-start | bytes 122888 | tf_op jit(solution)/shard_map/ppermute | solution.py:303
  10.1 0.0 collective-permute-done.low_ref
  10.1 3.3 %collective-permute-done.1.high_ref = bf16[32,640]{1,0:T(8,128)(2,1)S(1)} collective-permute-done((bf16[32,640]{1,0:T(8,128)(2,1)S(1)}, bf16[32,640]{1,0:T(8,128)(2,1)S(1)}, u32[]{:S(2)}, u32[]{:S(2)}) %collective-permute-start.1) | collective-permute-done | bytes 40992 | tf_op jit(solution)/shard_map/ppermute | solution.py:303
  13.4 2.7 %outer.1.refs_0_ = bf16[256,640]{1,0:T(8,128)(2,1)S(1)} custom-call(bf16[512,640]{1,0:T(8,128)(2,1)S(1)} %get-tuple-element.37.x_ref, bf16[32,640]{1,0:T(8,128)(2,1)S(1)} %collective-permute-done.low_ref, bf16[32,640]{1,0:T(8,128)(2,1)S(1)} %collective-permute-done.1.high_ref, bf16[3,1920,640]{2,1,0:T(8,128)(2,1)S(1)} %get-tuple-element.40.weight, ...), custom_call_target="tpu_custom_call" | custom-call | flops 1 | bytes 1 | tf_op jit(solution)/shard_map/outer/pallas_call | solution.py:134
  16.2 0.0 copy-start.1
  16.2 0.8 %collective-permute-start.2 = (bf16[256,640]{1,0:T(8,128)(2,1)S(1)}, bf16[256,640]{1,0:T(8,128)(2,1)S(1)}, u32[]{:S(2)}, u32[]{:S(2)}) collective-permute-start(bf16[256,640]{1,0:T(8,128)(2,1)S(1)} %outer.1.refs_0_), channel_id=1, source_target_pairs={{1,5},{3,7}} | collective-permute-start | bytes 983048 | tf_op jit(solution)/shard_map/ppermute | solution.py:309
  17.0 0.0 collective-permute-done.5
  17.0 0.1 broadcast_select_fusion
  17.1 1.3 %collective-permute-start.6 = (bf16[256,640]{1,0:T(8,128)(2,1)S(1)}, bf16[256,640]{1,0:T(8,128)(2,1)S(1)}, u32[]{:S(2)}, u32[]{:S(2)}) collective-permute-start(bf16[256,640]{1,0:T(8,128)(2,1)S(1)} %broadcast_select_fusion), channel_id=1, source_target_pairs={{0,16},{5,21},{2,18},{7,23}} | collective-permute-start | bytes 983048 | tf_op jit(solution)/shard_map/ppermute | solution.py:309
  18.4 0.8 %ask.1 = (bf16[512,640]{1,0:T(8,128)(2,1)S(1)}, bf16[512,640]{1,0:T(8,128)(2,1)S(1)}) custom-call(bf16[640,640]{1,0:T(8,128)(2,1)S(1)} %copy-done.1, bf16[512,640]{1,0:T(8,128)(2,1)S(1)} %get-tuple-element.37.x_ref, bf16[32,640]{1,0:T(8,128)(2,1)S(1)} %collective-permute-done.low_ref, bf16[32,640]{1,0:T(8,128)(2,1)S(1)} %collective-permute-done.1.high_ref, ...), custom_call_target="tpu_custom_call" | custom-call | flops 1 | bytes 1 | tf_op jit(solution)/shard_map/ask/pallas_call | solution.py:178
  19.3 0.0 collective-permute-done.2
  19.3 3.6 %collective-permute-start.3 = (bf16[256,640]{1,0:T(8,128)(2,1)S(1)}, bf16[256,640]{1,0:T(8,128)(2,1)S(1)}, u32[]{:S(2)}, u32[]{:S(2)}) collective-permute-start(bf16[256,640]{1,0:T(8,128)(2,1)S(1)} %broadcast_select_fusion.1), channel_id=1, source_target_pairs={{0,16},{5,21},{2,18},{7,23}} | collective-permute-start | bytes 983048 | tf_op jit(solution)/shard_map/ppermute | solution.py:309
  22.9 0.1 collective-permute-done.6
  22.9 0.1 add.14
  23.0 0.0 copy-start
  23.0 1.4 %collective-permute-start.7 = (bf16[256,640]{1,0:T(8,128)(2,1)S(1)}, bf16[256,640]{1,0:T(8,128)(2,1)S(1)}, u32[]{:S(2)}, u32[]{:S(2)}) collective-permute-start(bf16[256,640]{1,0:T(8,128)(2,1)S(1)} %add.14), channel_id=1, source_target_pairs={{0,8},{5,13},{2,10},{7,15},{16,24},{21,29},{18,26},{23,31}} | collective-permute-start | bytes 983048 | tf_op jit(solution)/shard_map/ppermute | solution.py:309
  24.5 3.0 %collective-permute-done.3 = bf16[256,640]{1,0:T(8,128)(2,1)S(1)} collective-permute-done((bf16[256,640]{1,0:T(8,128)(2,1)S(1)}, bf16[256,640]{1,0:T(8,128)(2,1)S(1)}, u32[]{:S(2)}, u32[]{:S(2)}) %collective-permute-start.3) | collective-permute-done | bytes 327712 | tf_op jit(solution)/shard_map/ppermute | solution.py:309
  27.4 0.1 add.12
  27.5 1.3 %collective-permute-start.4 = (bf16[256,640]{1,0:T(8,128)(2,1)S(1)}, bf16[256,640]{1,0:T(8,128)(2,1)S(1)}, u32[]{:S(2)}, u32[]{:S(2)}) collective-permute-start(bf16[256,640]{1,0:T(8,128)(2,1)S(1)} %add.12), channel_id=1, source_target_pairs={{0,8},{5,13},{2,10},{7,15},{16,24},{21,29},{18,26},{23,31}} | collective-permute-start | bytes 983048 | tf_op jit(solution)/shard_map/ppermute | solution.py:309
  28.8 2.1 %collective-permute-done.7 = bf16[256,640]{1,0:T(8,128)(2,1)S(1)} collective-permute-done((bf16[256,640]{1,0:T(8,128)(2,1)S(1)}, bf16[256,640]{1,0:T(8,128)(2,1)S(1)}, u32[]{:S(2)}, u32[]{:S(2)}) %collective-permute-start.7) | collective-permute-done | bytes 327712 | tf_op jit(solution)/shard_map/ppermute | solution.py:309
  30.9 0.1 add.15.refs_0_
  31.0 1.3 %collective-permute-start.13 = (bf16[256,640]{1,0:T(8,128)(2,1)S(1)}, bf16[256,640]{1,0:T(8,128)(2,1)S(1)}, u32[]{:S(2)}, u32[]{:S(2)}) collective-permute-start(bf16[256,640]{1,0:T(8,128)(2,1)S(1)} %add.15.refs_0_), channel_id=1, source_target_pairs={{0,4},{2,6},{8,12},{10,14},{13,9},{15,11},{16,20},{18,22},{21,17},... | collective-permute-start | bytes 983048 | tf_op jit(solution)/shard_map/ppermute | solution.py:309
  32.4 1.3 %collective-permute-start.12 = (bf16[256,640]{1,0:T(8,128)(2,1)S(1)}, bf16[256,640]{1,0:T(8,128)(2,1)S(1)}, u32[]{:S(2)}, u32[]{:S(2)}) collective-permute-start(bf16[256,640]{1,0:T(8,128)(2,1)S(1)} %add.15.refs_0_), channel_id=1, source_target_pairs={{0,6},{2,4},{8,14},{10,12},{13,11},{15,9},{16,22},{18,20},{21,19},... | collective-permute-start | bytes 983048 | tf_op jit(solution)/shard_map/ppermute | solution.py:309
  33.7 4.5 %collective-permute-start.11 = (bf16[256,640]{1,0:T(8,128)(2,1)S(1)}, bf16[256,640]{1,0:T(8,128)(2,1)S(1)}, u32[]{:S(2)}, u32[]{:S(2)}) collective-permute-start(bf16[256,640]{1,0:T(8,128)(2,1)S(1)} %add.15.refs_0_), channel_id=1, source_target_pairs={{0,2},{2,0},{5,7},{7,5},{8,10},{10,8},{13,15},{15,13},{16,18},{18,... | collective-permute-start | bytes 983048 | tf_op jit(solution)/shard_map/ppermute | solution.py:309
  38.2 0.0 collective-permute-done.4
  38.2 0.1 add.13.refs_0_
  38.3 1.3 %collective-permute-start.10 = (bf16[256,640]{1,0:T(8,128)(2,1)S(1)}, bf16[256,640]{1,0:T(8,128)(2,1)S(1)}, u32[]{:S(2)}, u32[]{:S(2)}) collective-permute-start(bf16[256,640]{1,0:T(8,128)(2,1)S(1)} %add.13.refs_0_), channel_id=1, source_target_pairs={{0,4},{2,6},{8,12},{10,14},{13,9},{15,11},{16,20},{18,22},{21,17},... | collective-permute-start | bytes 983048 | tf_op jit(solution)/shard_map/ppermute | solution.py:309
  39.6 1.9 %collective-permute-start.9 = (bf16[256,640]{1,0:T(8,128)(2,1)S(1)}, bf16[256,640]{1,0:T(8,128)(2,1)S(1)}, u32[]{:S(2)}, u32[]{:S(2)}) collective-permute-start(bf16[256,640]{1,0:T(8,128)(2,1)S(1)} %add.13.refs_0_), channel_id=1, source_target_pairs={{0,2},{2,0},{5,7},{7,5},{8,10},{10,8},{13,15},{15,13},{16,18},{18,... | collective-permute-start | bytes 983048 | tf_op jit(solution)/shard_map/ppermute | solution.py:309
  41.5 0.0 collective-permute-done.13.refs_1_
  41.5 5.3 %collective-permute-start.8 = (bf16[256,640]{1,0:T(8,128)(2,1)S(1)}, bf16[256,640]{1,0:T(8,128)(2,1)S(1)}, u32[]{:S(2)}, u32[]{:S(2)}) collective-permute-start(bf16[256,640]{1,0:T(8,128)(2,1)S(1)} %add.13.refs_0_), channel_id=1, source_target_pairs={{0,6},{2,4},{8,14},{10,12},{13,11},{15,9},{16,22},{18,20},{21,19},... | collective-permute-start | bytes 983048 | tf_op jit(solution)/shard_map/ppermute | solution.py:309
  46.8 0.0 collective-permute-done.12.refs_3_
  46.8 0.0 collective-permute-done.11.refs_2_
  46.8 1.2 %project.2.keyval = bf16[512,1280]{1,0:T(8,128)(2,1)S(1)} custom-call(bf16[640,1280]{1,0:T(8,128)(2,1)S(1)} %copy-done, bf16[256,640]{1,0:T(8,128)(2,1)S(1)} %add.15.refs_0_, bf16[256,640]{1,0:T(8,128)(2,1)S(1)} %collective-permute-done.13.refs_1_, bf16[256,640]{1,0:T(8,128)(2,1)S(1)} %collective-permute-done.11.refs_2_, ...), custom_call_target="tpu_custom_call" | custom-call | flops 1 | bytes 1 | tf_op jit(solution)/shard_map/project/pallas_call | solution.py:203
  48.0 0.1 collective-permute-start.15
  48.1 3.4 %attend.3 = (f32[512,640]{1,0:T(8,128)S(1)}, f32[512,640]{1,0:T(8,128)S(1)}, f32[512,640]{1,0:T(8,128)S(1)}) custom-call(bf16[512,640]{1,0:T(8,128)(2,1)S(1)} %get-tuple-element.43.queries_ref, bf16[512,1280]{1,0:T(8,128)(2,1)S(1)} %project.2.keyval), custom_call_target="tpu_custom_call" | custom-call | flops 1 | bytes 1 | tf_op jit(solution)/shard_map/attend/pallas_call | solution.py:284
  51.5 0.0 collective-permute-done.9.refs_2_
  51.5 0.8 %collective-permute-done.8.refs_3_ = bf16[256,640]{1,0:T(8,128)(2,1)S(1)} collective-permute-done((bf16[256,640]{1,0:T(8,128)(2,1)S(1)}, bf16[256,640]{1,0:T(8,128)(2,1)S(1)}, u32[]{:S(2)}, u32[]{:S(2)}) %collective-permute-start.8) | collective-permute-done | bytes 327712 | tf_op jit(solution)/shard_map/ppermute | solution.py:309
  52.3 1.2 %project.3.keyval = bf16[512,1280]{1,0:T(8,128)(2,1)S(1)} custom-call(bf16[640,1280]{1,0:T(8,128)(2,1)S(1)} %copy-done, bf16[256,640]{1,0:T(8,128)(2,1)S(1)} %add.13.refs_0_, bf16[256,640]{1,0:T(8,128)(2,1)S(1)} %collective-permute-done.10.refs_1_, bf16[256,640]{1,0:T(8,128)(2,1)S(1)} %collective-permute-done.9.refs_2_, ...), custom_call_target="tpu_custom_call" | custom-call | flops 1 | bytes 1 | tf_op jit(solution)/shard_map/project/pallas_call | solution.py:203
  53.5 0.1 collective-permute-start.14
  53.5 0.0 collective-permute-done.15.keyval
  53.5 3.4 %attend.4 = (f32[512,640]{1,0:T(8,128)S(1)}, f32[512,640]{1,0:T(8,128)S(1)}, f32[512,640]{1,0:T(8,128)S(1)}) custom-call(bf16[512,640]{1,0:T(8,128)(2,1)S(1)} %get-tuple-element.43.queries_ref, bf16[512,1280]{1,0:T(8,128)(2,1)S(1)} %collective-permute-done.15.keyval), custom_call_target="tpu_custom_call" | custom-call | flops 1 | bytes 1 | tf_op jit(solution)/shard_map/attend/pallas_call | solution.py:284
  56.9 0.0 copy-start.2
  56.9 3.6 %attend.5 = (f32[512,640]{1,0:T(8,128)S(1)}, f32[512,640]{1,0:T(8,128)S(1)}, f32[512,640]{1,0:T(8,128)S(1)}) custom-call(bf16[512,640]{1,0:T(8,128)(2,1)S(1)} %get-tuple-element.43.queries_ref, bf16[512,1280]{1,0:T(8,128)(2,1)S(1)} %project.3.keyval), custom_call_target="tpu_custom_call" | custom-call | flops 1 | bytes 1 | tf_op jit(solution)/shard_map/attend/pallas_call | solution.py:284
  60.6 0.0 collective-permute-done.14.keyval
  60.6 5.4 %join.1 = bf16[512,640]{1,0:T(8,128)(2,1)} custom-call(bf16[512,640]{1,0:T(8,128)(2,1)S(1)} %get-tuple-element.43.queries_ref, bf16[512,1280]{1,0:T(8,128)(2,1)S(1)} %collective-permute-done.14.keyval, f32[512,640]{1,0:T(8,128)S(1)} %get-tuple-element.51.refs_0_, f32[512,640]{1,0:T(8,128)S(1)} %get-tuple-element.52.refs_1_, ...), custom_call_target="tpu_custom_call" | custom-call | flops 1 | bytes 1 | tf_op jit(solution)/shard_map/join/pallas_call | solution.py:284
  (12 shorter events, 0.1 us)
Async XLA Ops:
  0.0 18.4 %slice-start = ((s8[7372800]{0:T(1024)(128)(4,1)}), s8[4194304]{0:T(1024)(128)(4,1)S(1)}, s32[]{:S(2)}) async-start(s8[7372800]{0:T(1024)(128)(4,1)} %bitcast.4), calls=%async_computation | async-start | bytes 8388608
  5.1 11.9 %collective-permute-start.5 = (bf16[256,640]{1,0:T(8,128)(2,1)S(1)}, bf16[256,640]{1,0:T(8,128)(2,1)S(1)}, u32[]{:S(2)}, u32[]{:S(2)}) collective-permute-start(bf16[256,640]{1,0:T(8,128)(2,1)S(1)} %get-tuple-element.42.refs_1_), channel_id=1, source_target_pairs={{1,5},{3,7}} | collective-permute-start | bytes 983048 | tf_op jit(solution)/shard_map/ppermute | solution.py:309
  5.8 4.3 %collective-permute-start = (bf16[32,640]{1,0:T(8,128)(2,1)S(1)}, bf16[32,640]{1,0:T(8,128)(2,1)S(1)}, u32[]{:S(2)}, u32[]{:S(2)}) collective-permute-start(bf16[32,640]{1,0:T(8,128)(2,1)S(1)} %get-tuple-element.38), channel_id=1, source_target_pairs={{0,1},{1,2},{2,3},{4,5},{5,6},{6,7},{8,9},{9,10},{10,11},{12,13},{... | collective-permute-start | bytes 122888 | tf_op jit(solution)/shard_map/ppermute | solution.py:303
  8.8 4.6 %collective-permute-start.1 = (bf16[32,640]{1,0:T(8,128)(2,1)S(1)}, bf16[32,640]{1,0:T(8,128)(2,1)S(1)}, u32[]{:S(2)}, u32[]{:S(2)}) collective-permute-start(bf16[32,640]{1,0:T(8,128)(2,1)S(1)} %get-tuple-element.39), channel_id=1, source_target_pairs={{1,0},{2,1},{3,2},{5,4},{6,5},{7,6},{9,8},{10,9},{11,10},{13,12},{... | collective-permute-start | bytes 122888 | tf_op jit(solution)/shard_map/ppermute | solution.py:303
  13.4 5.0 %slice-start.1 = ((s8[7372800]{0:T(1024)(128)(4,1)}), s8[3178496]{0:T(1024)(128)(4,1)S(1)}, s32[]{:S(2)}) async-start(s8[7372800]{0:T(1024)(128)(4,1)} %bitcast.4), calls=%async_computation.1 | async-start | bytes 6356992
  13.4 5.0 %copy-start.3 = (bf16[640]{0:T(1024)(128)(2,1)S(1)}, bf16[640]{0:T(1024)(128)(2,1)}, u32[]{:S(2)}) copy-start(bf16[640]{0:T(1024)(128)(2,1)} %bias_ref.1) | copy-start | bytes 3844
  16.2 2.2 %copy-start.1 = (bf16[640,640]{1,0:T(8,128)(2,1)S(1)}, bf16[640,640]{1,0:T(8,128)(2,1)}, u32[]{:S(2)}) copy-start(bf16[640,640]{1,0:T(8,128)(2,1)} %w_query.1) | copy-start | bytes 2457604
  16.2 3.1 %collective-permute-start.2 = (bf16[256,640]{1,0:T(8,128)(2,1)S(1)}, bf16[256,640]{1,0:T(8,128)(2,1)S(1)}, u32[]{:S(2)}, u32[]{:S(2)}) collective-permute-start(bf16[256,640]{1,0:T(8,128)(2,1)S(1)} %outer.1.refs_0_), channel_id=1, source_target_pairs={{1,5},{3,7}} | collective-permute-start | bytes 983048 | tf_op jit(solution)/shard_map/ppermute | solution.py:309
  17.1 5.9 %collective-permute-start.6 = (bf16[256,640]{1,0:T(8,128)(2,1)S(1)}, bf16[256,640]{1,0:T(8,128)(2,1)S(1)}, u32[]{:S(2)}, u32[]{:S(2)}) collective-permute-start(bf16[256,640]{1,0:T(8,128)(2,1)S(1)} %broadcast_select_fusion), channel_id=1, source_target_pairs={{0,16},{5,21},{2,18},{7,23}} | collective-permute-start | bytes 983048 | tf_op jit(solution)/shard_map/ppermute | solution.py:309
  19.3 8.1 %collective-permute-start.3 = (bf16[256,640]{1,0:T(8,128)(2,1)S(1)}, bf16[256,640]{1,0:T(8,128)(2,1)S(1)}, u32[]{:S(2)}, u32[]{:S(2)}) collective-permute-start(bf16[256,640]{1,0:T(8,128)(2,1)S(1)} %broadcast_select_fusion.1), channel_id=1, source_target_pairs={{0,16},{5,21},{2,18},{7,23}} | collective-permute-start | bytes 983048 | tf_op jit(solution)/shard_map/ppermute | solution.py:309
  23.0 23.8 %copy-start = (bf16[640,1280]{1,0:T(8,128)(2,1)S(1)}, bf16[640,1280]{1,0:T(8,128)(2,1)}, u32[]{:S(2)}) copy-start(bf16[640,1280]{1,0:T(8,128)(2,1)} %w_keyval.3) | copy-start | bytes 4915204
  23.0 7.9 %collective-permute-start.7 = (bf16[256,640]{1,0:T(8,128)(2,1)S(1)}, bf16[256,640]{1,0:T(8,128)(2,1)S(1)}, u32[]{:S(2)}, u32[]{:S(2)}) collective-permute-start(bf16[256,640]{1,0:T(8,128)(2,1)S(1)} %add.14), channel_id=1, source_target_pairs={{0,8},{5,13},{2,10},{7,15},{16,24},{21,29},{18,26},{23,31}} | collective-permute-start | bytes 983048 | tf_op jit(solution)/shard_map/ppermute | solution.py:309
  27.5 10.6 %collective-permute-start.4 = (bf16[256,640]{1,0:T(8,128)(2,1)S(1)}, bf16[256,640]{1,0:T(8,128)(2,1)S(1)}, u32[]{:S(2)}, u32[]{:S(2)}) collective-permute-start(bf16[256,640]{1,0:T(8,128)(2,1)S(1)} %add.12), channel_id=1, source_target_pairs={{0,8},{5,13},{2,10},{7,15},{16,24},{21,29},{18,26},{23,31}} | collective-permute-start | bytes 983048 | tf_op jit(solution)/shard_map/ppermute | solution.py:309
  31.0 10.5 %collective-permute-start.13 = (bf16[256,640]{1,0:T(8,128)(2,1)S(1)}, bf16[256,640]{1,0:T(8,128)(2,1)S(1)}, u32[]{:S(2)}, u32[]{:S(2)}) collective-permute-start(bf16[256,640]{1,0:T(8,128)(2,1)S(1)} %add.15.refs_0_), channel_id=1, source_target_pairs={{0,4},{2,6},{8,12},{10,14},{13,9},{15,11},{16,20},{18,22},{21,17},... | collective-permute-start | bytes 983048 | tf_op jit(solution)/shard_map/ppermute | solution.py:309
  32.4 14.5 %collective-permute-start.12 = (bf16[256,640]{1,0:T(8,128)(2,1)S(1)}, bf16[256,640]{1,0:T(8,128)(2,1)S(1)}, u32[]{:S(2)}, u32[]{:S(2)}) collective-permute-start(bf16[256,640]{1,0:T(8,128)(2,1)S(1)} %add.15.refs_0_), channel_id=1, source_target_pairs={{0,6},{2,4},{8,14},{10,12},{13,11},{15,9},{16,22},{18,20},{21,19},... | collective-permute-start | bytes 983048 | tf_op jit(solution)/shard_map/ppermute | solution.py:309
  33.7 13.2 %collective-permute-start.11 = (bf16[256,640]{1,0:T(8,128)(2,1)S(1)}, bf16[256,640]{1,0:T(8,128)(2,1)S(1)}, u32[]{:S(2)}, u32[]{:S(2)}) collective-permute-start(bf16[256,640]{1,0:T(8,128)(2,1)S(1)} %add.15.refs_0_), channel_id=1, source_target_pairs={{0,2},{2,0},{5,7},{7,5},{8,10},{10,8},{13,15},{15,13},{16,18},{18,... | collective-permute-start | bytes 983048 | tf_op jit(solution)/shard_map/ppermute | solution.py:309
  38.3 13.2 %collective-permute-start.10 = (bf16[256,640]{1,0:T(8,128)(2,1)S(1)}, bf16[256,640]{1,0:T(8,128)(2,1)S(1)}, u32[]{:S(2)}, u32[]{:S(2)}) collective-permute-start(bf16[256,640]{1,0:T(8,128)(2,1)S(1)} %add.13.refs_0_), channel_id=1, source_target_pairs={{0,4},{2,6},{8,12},{10,14},{13,9},{15,11},{16,20},{18,22},{21,17},... | collective-permute-start | bytes 983048 | tf_op jit(solution)/shard_map/ppermute | solution.py:309
  39.6 11.9 %collective-permute-start.9 = (bf16[256,640]{1,0:T(8,128)(2,1)S(1)}, bf16[256,640]{1,0:T(8,128)(2,1)S(1)}, u32[]{:S(2)}, u32[]{:S(2)}) collective-permute-start(bf16[256,640]{1,0:T(8,128)(2,1)S(1)} %add.13.refs_0_), channel_id=1, source_target_pairs={{0,2},{2,0},{5,7},{7,5},{8,10},{10,8},{13,15},{15,13},{16,18},{18,... | collective-permute-start | bytes 983048 | tf_op jit(solution)/shard_map/ppermute | solution.py:309
  41.5 10.7 %collective-permute-start.8 = (bf16[256,640]{1,0:T(8,128)(2,1)S(1)}, bf16[256,640]{1,0:T(8,128)(2,1)S(1)}, u32[]{:S(2)}, u32[]{:S(2)}) collective-permute-start(bf16[256,640]{1,0:T(8,128)(2,1)S(1)} %add.13.refs_0_), channel_id=1, source_target_pairs={{0,6},{2,4},{8,14},{10,12},{13,11},{15,9},{16,22},{18,20},{21,19},... | collective-permute-start | bytes 983048 | tf_op jit(solution)/shard_map/ppermute | solution.py:309
  48.0 5.5 %collective-permute-start.15 = (bf16[512,1280]{1,0:T(8,128)(2,1)S(1)}, bf16[512,1280]{1,0:T(8,128)(2,1)S(1)}, u32[]{:S(2)}, u32[]{:S(2)}) collective-permute-start(bf16[512,1280]{1,0:T(8,128)(2,1)S(1)} %project.2.keyval), channel_id=1, source_target_pairs={{0,1},{1,0},{2,3},{3,2},{4,5},{5,4},{6,7},{7,6},{8,9},{9,8},{10,11... | collective-permute-start | bytes 3932168 | tf_op jit(solution)/shard_map/ppermute | solution.py:309
  53.5 7.1 %collective-permute-start.14 = (bf16[512,1280]{1,0:T(8,128)(2,1)S(1)}, bf16[512,1280]{1,0:T(8,128)(2,1)S(1)}, u32[]{:S(2)}, u32[]{:S(2)}) collective-permute-start(bf16[512,1280]{1,0:T(8,128)(2,1)S(1)} %project.3.keyval), channel_id=1, source_target_pairs={{0,1},{1,0},{2,3},{3,2},{4,5},{5,4},{6,7},{7,6},{8,9},{9,8},{10,11... | collective-permute-start | bytes 3932168 | tf_op jit(solution)/shard_map/ppermute | solution.py:309
  56.9 3.7 %copy-start.2 = (bf16[640,640]{1,0:T(8,128)(2,1)S(1)}, bf16[640,640]{1,0:T(8,128)(2,1)}, u32[]{:S(2)}) copy-start(bf16[640,640]{1,0:T(8,128)(2,1)} %refs_10_.1) | copy-start | bytes 2457604

commit v9 on v7

--- a/solution.py
+++ b/solution.py
@@ -369,11 +369,11 @@
     parts0 = (parts0[2], parts0[1], parts0[0])
     held1 = ordered(held1, held0)
     parts1 = exchange(held1)
-    parts1 = (parts1[1], parts1[2], parts1[0])
+    parts1 = (parts1[2], parts1[0], parts1[1])
     here0 = keyval_of(own_side(held0, [ordered(parts0, held1)[i] for i in (2, 1, 0)]))
     there0 = swap_cores(here0)
     look0 = look(here0)
-    here1 = keyval_of(own_side(held1, [ordered(parts1, look0)[i] for i in (2, 0, 1)]))
+    here1 = keyval_of(own_side(held1, [ordered(parts1, look0)[i] for i in (1, 2, 0)]))
     there1 = swap_cores(here1)
     look1 = look(ordered(there0, look0, here1))
     look2 = look(ordered(here1, look1))

time: 67.3 us -> 68.1 us (1.012)
  waiting for transfers between devices: 8.99 us -> 12.2 us
  starting transfers between devices: 29.2 us -> 27.5 us
    ppermute x14, waiting for transfers between devices: 5.7 us -> 8.95 us  [permute(): return lax.ppermute(value, ('frame', 'band'), flat)]
    ppermute x14, starting transfers between devices: 25 us -> 23.2 us  [permute(): return lax.ppermute(value, ('frame', 'band'), flat)]
  transfers between devices with their start and end apart: 16 -> 16, of which waited for: 5 -> 6; matrix products, arithmetic and copies ran while one was open for 1% -> 1% of each run, Pallas kernels for 25% -> 24%
where the time goes in v9:
time: 68.1 us; the launch traced here: 67.7 us
  starting transfers between devices  27.5 us (40%)
  Pallas kernels  26.9 us (40%)
  waiting for transfers between devices  12.2 us (18%)
  other arithmetic  0.76 us (1%)
    ppermute x14, starting transfers between devices, permute(): return lax.ppermute(value, ('frame', 'band'), flat)  23.2 us
    pallas_call x4, Pallas kernels, attend(): pl.pallas_call(functools.partial(attend_kernel, len(parts), last), out_sh...  15.8 us
    ppermute x14, waiting for transfers between devices, permute(): return lax.ppermute(value, ('frame', 'band'), flat)  8.95 us
    pallas_call x1, Pallas kernels, convolve_inner(): pl.pallas_call(functools.partial(inner_kernel, width, inner), out_shape=(...  5.12 us
    ppermute x1, waiting for transfers between devices, from_edges(): lax.ppermute(top, 'band', backward)  3.28 us
    ppermute x1, starting transfers between devices, from_edges(): lax.ppermute(bottom, 'band', forward)  2.98 us
    pallas_call x1, Pallas kernels, convolve_outer(): pl.pallas_call(functools.partial(outer_kernel, width, outer), out_shape=j...  2.74 us
    pallas_call x2, Pallas kernels, project(): pl.pallas_call(functools.partial(project_kernel, len(pieces)), out_shape=...  2.37 us
  transfers between devices with their start and end apart: 16, of which 6 were waited for; matrix products, arithmetic and copies ran while one was open for 1% of the time, Pallas kernels for 24%

profile of v9, /device:TPU:0, one launch (start us, length us, event | category | flops | bytes accessed | tf_op | source)
XLA Modules:
  0.0 67.7 jit_solution(6461974359900563)
XLA Ops:
  0.0 5.1 %inner.1 = (bf16[256,640]{1,0:T(8,128)(2,1)S(1)}, bf16[512,640]{1,0:T(8,128)(2,1)S(1)}, bf16[32,640]{1,0:T(8,128)(2,1)S(1)}, bf16[32,640]{1,0:T(8,128)(2,1)S(1)}...) custom-call(bf16[512,640]{1,0:T(8,128)(2,1)} %bitcast.7, bf16[3,1920,640]{2,1,0:T(8,128)(2,1)} %bitcast.3, ...), custom_call_target="tpu_custom_call" | custom-call | flops 1 | bytes 1 | tf_op jit(solution)/shard_map/inner/pallas_call | solution.py:105
  5.1 0.7 %collective-permute-start.5 = (bf16[256,640]{1,0:T(8,128)(2,1)S(1)}, bf16[256,640]{1,0:T(8,128)(2,1)S(1)}, u32[]{:S(2)}, u32[]{:S(2)}) collective-permute-start(bf16[256,640]{1,0:T(8,128)(2,1)S(1)} %get-tuple-element.42.refs_1_), channel_id=1, source_target_pairs={{1,5},{3,7}} | collective-permute-start | bytes 983048 | tf_op jit(solution)/shard_map/ppermute | solution.py:308
  5.8 3.0 %collective-permute-start = (bf16[32,640]{1,0:T(8,128)(2,1)S(1)}, bf16[32,640]{1,0:T(8,128)(2,1)S(1)}, u32[]{:S(2)}, u32[]{:S(2)}) collective-permute-start(bf16[32,640]{1,0:T(8,128)(2,1)S(1)} %get-tuple-element.38), channel_id=1, source_target_pairs={{0,1},{1,2},{2,3},{4,5},{5,6},{6,7},{8,9},{9,10},{10,11},{12,13},{... | collective-permute-start | bytes 122888 | tf_op jit(solution)/shard_map/ppermute | solution.py:302
  8.8 1.3 %collective-permute-start.1 = (bf16[32,640]{1,0:T(8,128)(2,1)S(1)}, bf16[32,640]{1,0:T(8,128)(2,1)S(1)}, u32[]{:S(2)}, u32[]{:S(2)}) collective-permute-start(bf16[32,640]{1,0:T(8,128)(2,1)S(1)} %get-tuple-element.39), channel_id=1, source_target_pairs={{1,0},{2,1},{3,2},{5,4},{6,5},{7,6},{9,8},{10,9},{11,10},{13,12},{... | collective-permute-start | bytes 122888 | tf_op jit(solution)/shard_map/ppermute | solution.py:302
  10.1 0.0 collective-permute-done.low_ref
  10.1 3.3 %collective-permute-done.1.high_ref = bf16[32,640]{1,0:T(8,128)(2,1)S(1)} collective-permute-done((bf16[32,640]{1,0:T(8,128)(2,1)S(1)}, bf16[32,640]{1,0:T(8,128)(2,1)S(1)}, u32[]{:S(2)}, u32[]{:S(2)}) %collective-permute-start.1) | collective-permute-done | bytes 40992 | tf_op jit(solution)/shard_map/ppermute | solution.py:302
  13.4 2.7 %outer.1.refs_0_ = bf16[256,640]{1,0:T(8,128)(2,1)S(1)} custom-call(bf16[512,640]{1,0:T(8,128)(2,1)S(1)} %get-tuple-element.37.x_ref, bf16[32,640]{1,0:T(8,128)(2,1)S(1)} %collective-permute-done.low_ref, bf16[32,640]{1,0:T(8,128)(2,1)S(1)} %collective-permute-done.1.high_ref, bf16[3,1920,640]{2,1,0:T(8,128)(2,1)S(1)} %get-tuple-element.40.weight, ...), custom_call_target="tpu_custom_call" | custom-call | flops 1 | bytes 1 | tf_op jit(solution)/shard_map/outer/pallas_call | solution.py:134
  16.2 0.0 copy-start.1
  16.2 0.8 %collective-permute-start.2 = (bf16[256,640]{1,0:T(8,128)(2,1)S(1)}, bf16[256,640]{1,0:T(8,128)(2,1)S(1)}, u32[]{:S(2)}, u32[]{:S(2)}) collective-permute-start(bf16[256,640]{1,0:T(8,128)(2,1)S(1)} %outer.1.refs_0_), channel_id=1, source_target_pairs={{1,5},{3,7}} | collective-permute-start | bytes 983048 | tf_op jit(solution)/shard_map/ppermute | solution.py:308
  17.0 0.1 broadcast_select_fusion
  17.1 1.3 %collective-permute-start.6 = (bf16[256,640]{1,0:T(8,128)(2,1)S(1)}, bf16[256,640]{1,0:T(8,128)(2,1)S(1)}, u32[]{:S(2)}, u32[]{:S(2)}) collective-permute-start(bf16[256,640]{1,0:T(8,128)(2,1)S(1)} %broadcast_select_fusion), channel_id=1, source_target_pairs={{0,16},{5,21},{2,18},{7,23}} | collective-permute-start | bytes 983048 | tf_op jit(solution)/shard_map/ppermute | solution.py:308
  18.4 0.8 %ask.1 = (bf16[512,640]{1,0:T(8,128)(2,1)S(1)}, bf16[512,640]{1,0:T(8,128)(2,1)S(1)}) custom-call(bf16[640,640]{1,0:T(8,128)(2,1)S(1)} %copy-done.1, bf16[512,640]{1,0:T(8,128)(2,1)S(1)} %get-tuple-element.37.x_ref, bf16[32,640]{1,0:T(8,128)(2,1)S(1)} %collective-permute-done.low_ref, bf16[32,640]{1,0:T(8,128)(2,1)S(1)} %collective-permute-done.1.high_ref, ...), custom_call_target="tpu_custom_call" | custom-call | flops 1 | bytes 1 | tf_op jit(solution)/shard_map/ask/pallas_call | solution.py:178
  19.3 3.6 %collective-permute-start.3 = (bf16[256,640]{1,0:T(8,128)(2,1)S(1)}, bf16[256,640]{1,0:T(8,128)(2,1)S(1)}, u32[]{:S(2)}, u32[]{:S(2)}) collective-permute-start(bf16[256,640]{1,0:T(8,128)(2,1)S(1)} %broadcast_select_fusion.1), channel_id=1, source_target_pairs={{0,16},{5,21},{2,18},{7,23}} | collective-permute-start | bytes 983048 | tf_op jit(solution)/shard_map/ppermute | solution.py:308
  22.9 0.1 collective-permute-done.6
  22.9 0.1 add.26
  23.0 1.3 %collective-permute-start.7 = (bf16[256,640]{1,0:T(8,128)(2,1)S(1)}, bf16[256,640]{1,0:T(8,128)(2,1)S(1)}, u32[]{:S(2)}, u32[]{:S(2)}) collective-permute-start(bf16[256,640]{1,0:T(8,128)(2,1)S(1)} %add.26), channel_id=1, source_target_pairs={{0,8},{5,13},{2,10},{7,15},{16,24},{21,29},{18,26},{23,31}} | collective-permute-start | bytes 983048 | tf_op jit(solution)/shard_map/ppermute | solution.py:308
  24.3 3.1 %collective-permute-done.3 = bf16[256,640]{1,0:T(8,128)(2,1)S(1)} collective-permute-done((bf16[256,640]{1,0:T(8,128)(2,1)S(1)}, bf16[256,640]{1,0:T(8,128)(2,1)S(1)}, u32[]{:S(2)}, u32[]{:S(2)}) %collective-permute-start.3) | collective-permute-done | bytes 327712 | tf_op jit(solution)/shard_map/ppermute | solution.py:308
  27.4 0.1 add.24
  27.5 1.3 %collective-permute-start.4 = (bf16[256,640]{1,0:T(8,128)(2,1)S(1)}, bf16[256,640]{1,0:T(8,128)(2,1)S(1)}, u32[]{:S(2)}, u32[]{:S(2)}) collective-permute-start(bf16[256,640]{1,0:T(8,128)(2,1)S(1)} %add.24), channel_id=1, source_target_pairs={{0,8},{5,13},{2,10},{7,15},{16,24},{21,29},{18,26},{23,31}} | collective-permute-start | bytes 983048 | tf_op jit(solution)/shard_map/ppermute | solution.py:308
  28.8 2.1 %collective-permute-done.7 = bf16[256,640]{1,0:T(8,128)(2,1)S(1)} collective-permute-done((bf16[256,640]{1,0:T(8,128)(2,1)S(1)}, bf16[256,640]{1,0:T(8,128)(2,1)S(1)}, u32[]{:S(2)}, u32[]{:S(2)}) %collective-permute-start.7) | collective-permute-done | bytes 327712 | tf_op jit(solution)/shard_map/ppermute | solution.py:308
  30.9 0.1 add.27
  31.0 0.0 copy-start
  31.0 1.4 %collective-permute-start.13 = (bf16[256,640]{1,0:T(8,128)(2,1)S(1)}, bf16[256,640]{1,0:T(8,128)(2,1)S(1)}, u32[]{:S(2)}, u32[]{:S(2)}) collective-permute-start(bf16[256,640]{1,0:T(8,128)(2,1)S(1)} %add.27), channel_id=1, source_target_pairs={{0,4},{2,6},{8,12},{10,14},{13,9},{15,11},{16,20},{18,22},{21,17},... | collective-permute-start | bytes 983048 | tf_op jit(solution)/shard_map/ppermute | solution.py:308
  32.5 1.3 %collective-permute-start.12 = (bf16[256,640]{1,0:T(8,128)(2,1)S(1)}, bf16[256,640]{1,0:T(8,128)(2,1)S(1)}, u32[]{:S(2)}, u32[]{:S(2)}) collective-permute-start(bf16[256,640]{1,0:T(8,128)(2,1)S(1)} %add.27), channel_id=1, source_target_pairs={{0,6},{2,4},{8,14},{10,12},{13,11},{15,9},{16,22},{18,20},{21,19},... | collective-permute-start | bytes 983048 | tf_op jit(solution)/shard_map/ppermute | solution.py:308
  33.8 4.5 %collective-permute-start.11 = (bf16[256,640]{1,0:T(8,128)(2,1)S(1)}, bf16[256,640]{1,0:T(8,128)(2,1)S(1)}, u32[]{:S(2)}, u32[]{:S(2)}) collective-permute-start(bf16[256,640]{1,0:T(8,128)(2,1)S(1)} %add.27), channel_id=1, source_target_pairs={{0,2},{2,0},{5,7},{7,5},{8,10},{10,8},{13,15},{15,13},{16,18},{18,... | collective-permute-start | bytes 983048 | tf_op jit(solution)/shard_map/ppermute | solution.py:308
  38.3 0.0 collective-permute-done.4
  38.3 0.1 add.25
  38.4 1.3 %collective-permute-start.10 = (bf16[256,640]{1,0:T(8,128)(2,1)S(1)}, bf16[256,640]{1,0:T(8,128)(2,1)S(1)}, u32[]{:S(2)}, u32[]{:S(2)}) collective-permute-start(bf16[256,640]{1,0:T(8,128)(2,1)S(1)} %add.25), channel_id=1, source_target_pairs={{0,6},{2,4},{8,14},{10,12},{13,11},{15,9},{16,22},{18,20},{21,19},... | collective-permute-start | bytes 983048 | tf_op jit(solution)/shard_map/ppermute | solution.py:308
  39.7 1.3 %collective-permute-start.9 = (bf16[256,640]{1,0:T(8,128)(2,1)S(1)}, bf16[256,640]{1,0:T(8,128)(2,1)S(1)}, u32[]{:S(2)}, u32[]{:S(2)}) collective-permute-start(bf16[256,640]{1,0:T(8,128)(2,1)S(1)} %add.25), channel_id=1, source_target_pairs={{0,4},{2,6},{8,12},{10,14},{13,9},{15,11},{16,20},{18,22},{21,17},... | collective-permute-start | bytes 983048 | tf_op jit(solution)/shard_map/ppermute | solution.py:308
  41.0 0.0 collective-permute-done.13
  41.1 4.2 %collective-permute-start.8 = (bf16[256,640]{1,0:T(8,128)(2,1)S(1)}, bf16[256,640]{1,0:T(8,128)(2,1)S(1)}, u32[]{:S(2)}, u32[]{:S(2)}) collective-permute-start(bf16[256,640]{1,0:T(8,128)(2,1)S(1)} %add.25), channel_id=1, source_target_pairs={{0,2},{2,0},{5,7},{7,5},{8,10},{10,8},{13,15},{15,13},{16,18},{18,... | collective-permute-start | bytes 983048 | tf_op jit(solution)/shard_map/ppermute | solution.py:308
  45.3 0.0 collective-permute-done.12
  45.3 1.5 %collective-permute-done.11 = bf16[256,640]{1,0:T(8,128)(2,1)S(1)} collective-permute-done((bf16[256,640]{1,0:T(8,128)(2,1)S(1)}, bf16[256,640]{1,0:T(8,128)(2,1)S(1)}, u32[]{:S(2)}, u32[]{:S(2)}) %collective-permute-start.11) | collective-permute-done | bytes 327712 | tf_op jit(solution)/shard_map/ppermute | solution.py:308
  46.8 0.1 add.28.refs_0_
  46.9 0.1 add.29.refs_1_
  47.0 1.2 %project.2.keyval = bf16[512,1280]{1,0:T(8,128)(2,1)S(1)} custom-call(bf16[640,1280]{1,0:T(8,128)(2,1)S(1)} %copy-done, bf16[256,640]{1,0:T(8,128)(2,1)S(1)} %add.28.refs_0_, bf16[256,640]{1,0:T(8,128)(2,1)S(1)} %add.29.refs_1_), custom_call_target="tpu_custom_call" | custom-call | flops 1 | bytes 1 | tf_op jit(solution)/shard_map/project/pallas_call | solution.py:202
  48.2 0.1 collective-permute-start.15
  48.2 3.4 %attend.3 = (f32[512,640]{1,0:T(8,128)S(1)}, f32[512,640]{1,0:T(8,128)S(1)}, f32[512,640]{1,0:T(8,128)S(1)}) custom-call(bf16[512,640]{1,0:T(8,128)(2,1)S(1)} %get-tuple-element.43.queries_ref, bf16[512,1280]{1,0:T(8,128)(2,1)S(1)} %project.2.keyval), custom_call_target="tpu_custom_call" | custom-call | flops 1 | bytes 1 | tf_op jit(solution)/shard_map/attend/pallas_call | solution.py:283
  51.6 0.0 collective-permute-done.10
  51.6 2.2 %collective-permute-done.8 = bf16[256,640]{1,0:T(8,128)(2,1)S(1)} collective-permute-done((bf16[256,640]{1,0:T(8,128)(2,1)S(1)}, bf16[256,640]{1,0:T(8,128)(2,1)S(1)}, u32[]{:S(2)}, u32[]{:S(2)}) %collective-permute-start.8) | collective-permute-done | bytes 327712 | tf_op jit(solution)/shard_map/ppermute | solution.py:308
  53.8 0.1 add.30.refs_0_
  53.9 0.1 add.31.refs_1_
  54.0 1.2 %project.3.keyval = bf16[512,1280]{1,0:T(8,128)(2,1)S(1)} custom-call(bf16[640,1280]{1,0:T(8,128)(2,1)S(1)} %copy-done, bf16[256,640]{1,0:T(8,128)(2,1)S(1)} %add.30.refs_0_, bf16[256,640]{1,0:T(8,128)(2,1)S(1)} %add.31.refs_1_), custom_call_target="tpu_custom_call" | custom-call | flops 1 | bytes 1 | tf_op jit(solution)/shard_map/project/pallas_call | solution.py:202
  55.2 0.1 collective-permute-start.14
  55.3 3.4 %attend.4 = (f32[512,640]{1,0:T(8,128)S(1)}, f32[512,640]{1,0:T(8,128)S(1)}, f32[512,640]{1,0:T(8,128)S(1)}) custom-call(bf16[512,640]{1,0:T(8,128)(2,1)S(1)} %get-tuple-element.43.queries_ref, bf16[512,1280]{1,0:T(8,128)(2,1)S(1)} %collective-permute-done.15.keyval), custom_call_target="tpu_custom_call" | custom-call | flops 1 | bytes 1 | tf_op jit(solution)/shard_map/attend/pallas_call | solution.py:283
  58.6 0.0 copy-start.2
  58.7 3.6 %attend.5 = (f32[512,640]{1,0:T(8,128)S(1)}, f32[512,640]{1,0:T(8,128)S(1)}, f32[512,640]{1,0:T(8,128)S(1)}) custom-call(bf16[512,640]{1,0:T(8,128)(2,1)S(1)} %get-tuple-element.43.queries_ref, bf16[512,1280]{1,0:T(8,128)(2,1)S(1)} %project.3.keyval), custom_call_target="tpu_custom_call" | custom-call | flops 1 | bytes 1 | tf_op jit(solution)/shard_map/attend/pallas_call | solution.py:283
  62.3 5.4 %join.1 = bf16[512,640]{1,0:T(8,128)(2,1)} custom-call(bf16[512,640]{1,0:T(8,128)(2,1)S(1)} %get-tuple-element.43.queries_ref, bf16[512,1280]{1,0:T(8,128)(2,1)S(1)} %collective-permute-done.14.keyval, f32[512,640]{1,0:T(8,128)S(1)} %get-tuple-element.51.refs_0_, f32[512,640]{1,0:T(8,128)S(1)} %get-tuple-element.52.refs_1_, ...), custom_call_target="tpu_custom_call" | custom-call | flops 1 | bytes 1 | tf_op jit(solution)/shard_map/join/pallas_call | solution.py:283
  (16 shorter events, 0.1 us)
Async XLA Ops:
  0.0 18.4 %slice-start = ((s8[7372800]{0:T(1024)(128)(4,1)}), s8[4194304]{0:T(1024)(128)(4,1)S(1)}, s32[]{:S(2)}) async-start(s8[7372800]{0:T(1024)(128)(4,1)} %bitcast.4), calls=%async_computation | async-start | bytes 8388608
  5.1 11.9 %collective-permute-start.5 = (bf16[256,640]{1,0:T(8,128)(2,1)S(1)}, bf16[256,640]{1,0:T(8,128)(2,1)S(1)}, u32[]{:S(2)}, u32[]{:S(2)}) collective-permute-start(bf16[256,640]{1,0:T(8,128)(2,1)S(1)} %get-tuple-element.42.refs_1_), channel_id=1, source_target_pairs={{1,5},{3,7}} | collective-permute-start | bytes 983048 | tf_op jit(solution)/shard_map/ppermute | solution.py:308
  5.8 4.3 %collective-permute-start = (bf16[32,640]{1,0:T(8,128)(2,1)S(1)}, bf16[32,640]{1,0:T(8,128)(2,1)S(1)}, u32[]{:S(2)}, u32[]{:S(2)}) collective-permute-start(bf16[32,640]{1,0:T(8,128)(2,1)S(1)} %get-tuple-element.38), channel_id=1, source_target_pairs={{0,1},{1,2},{2,3},{4,5},{5,6},{6,7},{8,9},{9,10},{10,11},{12,13},{... | collective-permute-start | bytes 122888 | tf_op jit(solution)/shard_map/ppermute | solution.py:302
  8.8 4.6 %collective-permute-start.1 = (bf16[32,640]{1,0:T(8,128)(2,1)S(1)}, bf16[32,640]{1,0:T(8,128)(2,1)S(1)}, u32[]{:S(2)}, u32[]{:S(2)}) collective-permute-start(bf16[32,640]{1,0:T(8,128)(2,1)S(1)} %get-tuple-element.39), channel_id=1, source_target_pairs={{1,0},{2,1},{3,2},{5,4},{6,5},{7,6},{9,8},{10,9},{11,10},{13,12},{... | collective-permute-start | bytes 122888 | tf_op jit(solution)/shard_map/ppermute | solution.py:302
  13.4 5.0 %slice-start.1 = ((s8[7372800]{0:T(1024)(128)(4,1)}), s8[3178496]{0:T(1024)(128)(4,1)S(1)}, s32[]{:S(2)}) async-start(s8[7372800]{0:T(1024)(128)(4,1)} %bitcast.4), calls=%async_computation.1 | async-start | bytes 6356992
  13.4 5.0 %copy-start.3 = (bf16[640]{0:T(1024)(128)(2,1)S(1)}, bf16[640]{0:T(1024)(128)(2,1)}, u32[]{:S(2)}) copy-start(bf16[640]{0:T(1024)(128)(2,1)} %bias_ref.1) | copy-start | bytes 3844
  16.2 2.2 %copy-start.1 = (bf16[640,640]{1,0:T(8,128)(2,1)S(1)}, bf16[640,640]{1,0:T(8,128)(2,1)}, u32[]{:S(2)}) copy-start(bf16[640,640]{1,0:T(8,128)(2,1)} %w_query.1) | copy-start | bytes 2457604
  16.2 3.1 %collective-permute-start.2 = (bf16[256,640]{1,0:T(8,128)(2,1)S(1)}, bf16[256,640]{1,0:T(8,128)(2,1)S(1)}, u32[]{:S(2)}, u32[]{:S(2)}) collective-permute-start(bf16[256,640]{1,0:T(8,128)(2,1)S(1)} %outer.1.refs_0_), channel_id=1, source_target_pairs={{1,5},{3,7}} | collective-permute-start | bytes 983048 | tf_op jit(solution)/shard_map/ppermute | solution.py:308
  17.1 5.9 %collective-permute-start.6 = (bf16[256,640]{1,0:T(8,128)(2,1)S(1)}, bf16[256,640]{1,0:T(8,128)(2,1)S(1)}, u32[]{:S(2)}, u32[]{:S(2)}) collective-permute-start(bf16[256,640]{1,0:T(8,128)(2,1)S(1)} %broadcast_select_fusion), channel_id=1, source_target_pairs={{0,16},{5,21},{2,18},{7,23}} | collective-permute-start | bytes 983048 | tf_op jit(solution)/shard_map/ppermute | solution.py:308
  19.3 8.1 %collective-permute-start.3 = (bf16[256,640]{1,0:T(8,128)(2,1)S(1)}, bf16[256,640]{1,0:T(8,128)(2,1)S(1)}, u32[]{:S(2)}, u32[]{:S(2)}) collective-permute-start(bf16[256,640]{1,0:T(8,128)(2,1)S(1)} %broadcast_select_fusion.1), channel_id=1, source_target_pairs={{0,16},{5,21},{2,18},{7,23}} | collective-permute-start | bytes 983048 | tf_op jit(solution)/shard_map/ppermute | solution.py:308
  23.0 7.9 %collective-permute-start.7 = (bf16[256,640]{1,0:T(8,128)(2,1)S(1)}, bf16[256,640]{1,0:T(8,128)(2,1)S(1)}, u32[]{:S(2)}, u32[]{:S(2)}) collective-permute-start(bf16[256,640]{1,0:T(8,128)(2,1)S(1)} %add.26), channel_id=1, source_target_pairs={{0,8},{5,13},{2,10},{7,15},{16,24},{21,29},{18,26},{23,31}} | collective-permute-start | bytes 983048 | tf_op jit(solution)/shard_map/ppermute | solution.py:308
  27.5 10.8 %collective-permute-start.4 = (bf16[256,640]{1,0:T(8,128)(2,1)S(1)}, bf16[256,640]{1,0:T(8,128)(2,1)S(1)}, u32[]{:S(2)}, u32[]{:S(2)}) collective-permute-start(bf16[256,640]{1,0:T(8,128)(2,1)S(1)} %add.24), channel_id=1, source_target_pairs={{0,8},{5,13},{2,10},{7,15},{16,24},{21,29},{18,26},{23,31}} | collective-permute-start | bytes 983048 | tf_op jit(solution)/shard_map/ppermute | solution.py:308
  31.0 15.9 %copy-start = (bf16[640,1280]{1,0:T(8,128)(2,1)S(1)}, bf16[640,1280]{1,0:T(8,128)(2,1)}, u32[]{:S(2)}) copy-start(bf16[640,1280]{1,0:T(8,128)(2,1)} %w_keyval.3) | copy-start | bytes 4915204
  31.0 10.0 %collective-permute-start.13 = (bf16[256,640]{1,0:T(8,128)(2,1)S(1)}, bf16[256,640]{1,0:T(8,128)(2,1)S(1)}, u32[]{:S(2)}, u32[]{:S(2)}) collective-permute-start(bf16[256,640]{1,0:T(8,128)(2,1)S(1)} %add.27), channel_id=1, source_target_pairs={{0,4},{2,6},{8,12},{10,14},{13,9},{15,11},{16,20},{18,22},{21,17},... | collective-permute-start | bytes 983048 | tf_op jit(solution)/shard_map/ppermute | solution.py:308
  32.5 12.8 %collective-permute-start.12 = (bf16[256,640]{1,0:T(8,128)(2,1)S(1)}, bf16[256,640]{1,0:T(8,128)(2,1)S(1)}, u32[]{:S(2)}, u32[]{:S(2)}) collective-permute-start(bf16[256,640]{1,0:T(8,128)(2,1)S(1)} %add.27), channel_id=1, source_target_pairs={{0,6},{2,4},{8,14},{10,12},{13,11},{15,9},{16,22},{18,20},{21,19},... | collective-permute-start | bytes 983048 | tf_op jit(solution)/shard_map/ppermute | solution.py:308
  33.8 13.0 %collective-permute-start.11 = (bf16[256,640]{1,0:T(8,128)(2,1)S(1)}, bf16[256,640]{1,0:T(8,128)(2,1)S(1)}, u32[]{:S(2)}, u32[]{:S(2)}) collective-permute-start(bf16[256,640]{1,0:T(8,128)(2,1)S(1)} %add.27), channel_id=1, source_target_pairs={{0,2},{2,0},{5,7},{7,5},{8,10},{10,8},{13,15},{15,13},{16,18},{18,... | collective-permute-start | bytes 983048 | tf_op jit(solution)/shard_map/ppermute | solution.py:308
  38.4 13.2 %collective-permute-start.10 = (bf16[256,640]{1,0:T(8,128)(2,1)S(1)}, bf16[256,640]{1,0:T(8,128)(2,1)S(1)}, u32[]{:S(2)}, u32[]{:S(2)}) collective-permute-start(bf16[256,640]{1,0:T(8,128)(2,1)S(1)} %add.25), channel_id=1, source_target_pairs={{0,6},{2,4},{8,14},{10,12},{13,11},{15,9},{16,22},{18,20},{21,19},... | collective-permute-start | bytes 983048 | tf_op jit(solution)/shard_map/ppermute | solution.py:308
  39.7 11.9 %collective-permute-start.9 = (bf16[256,640]{1,0:T(8,128)(2,1)S(1)}, bf16[256,640]{1,0:T(8,128)(2,1)S(1)}, u32[]{:S(2)}, u32[]{:S(2)}) collective-permute-start(bf16[256,640]{1,0:T(8,128)(2,1)S(1)} %add.25), channel_id=1, source_target_pairs={{0,4},{2,6},{8,12},{10,14},{13,9},{15,11},{16,20},{18,22},{21,17},... | collective-permute-start | bytes 983048 | tf_op jit(solution)/shard_map/ppermute | solution.py:308
  41.1 12.7 %collective-permute-start.8 = (bf16[256,640]{1,0:T(8,128)(2,1)S(1)}, bf16[256,640]{1,0:T(8,128)(2,1)S(1)}, u32[]{:S(2)}, u32[]{:S(2)}) collective-permute-start(bf16[256,640]{1,0:T(8,128)(2,1)S(1)} %add.25), channel_id=1, source_target_pairs={{0,2},{2,0},{5,7},{7,5},{8,10},{10,8},{13,15},{15,13},{16,18},{18,... | collective-permute-start | bytes 983048 | tf_op jit(solution)/shard_map/ppermute | solution.py:308
  48.2 7.1 %collective-permute-start.15 = (bf16[512,1280]{1,0:T(8,128)(2,1)S(1)}, bf16[512,1280]{1,0:T(8,128)(2,1)S(1)}, u32[]{:S(2)}, u32[]{:S(2)}) collective-permute-start(bf16[512,1280]{1,0:T(8,128)(2,1)S(1)} %project.2.keyval), channel_id=1, source_target_pairs={{0,1},{1,0},{2,3},{3,2},{4,5},{5,4},{6,7},{7,6},{8,9},{9,8},{10,11... | collective-permute-start | bytes 3932168 | tf_op jit(solution)/shard_map/ppermute | solution.py:308
  55.2 7.1 %collective-permute-start.14 = (bf16[512,1280]{1,0:T(8,128)(2,1)S(1)}, bf16[512,1280]{1,0:T(8,128)(2,1)S(1)}, u32[]{:S(2)}, u32[]{:S(2)}) collective-permute-start(bf16[512,1280]{1,0:T(8,128)(2,1)S(1)} %project.3.keyval), channel_id=1, source_target_pairs={{0,1},{1,0},{2,3},{3,2},{4,5},{5,4},{6,7},{7,6},{8,9},{9,8},{10,11... | collective-permute-start | bytes 3932168 | tf_op jit(solution)/shard_map/ppermute | solution.py:308
  58.6 3.7 %copy-start.2 = (bf16[640,640]{1,0:T(8,128)(2,1)S(1)}, bf16[640,640]{1,0:T(8,128)(2,1)}, u32[]{:S(2)}) copy-start(bf16[640,640]{1,0:T(8,128)(2,1)} %refs_10_.1) | copy-start | bytes 2457604
